TPU v7x, 128 devices: a whole 4x4x4 slice. The times are simulated.
128 devices in a mesh: beam: 8 (over y_lo, z), det: 16 (over y_hi, x, core).
Axes of the slice: x: 4, y: 4 (y_hi: 2, y_lo: 2; y = y_hi * 2 + y_lo), z: 4, core: 2. Of those that a mesh axis runs over, the one named last changes fastest.
Arguments:
- concentration: float32 [10, 4, 1024, 2048], P(None, None, 'beam', 'det'), may hold values from 0.1 to 1
- incident_sigma: float32 [2, 10], replicated, may hold values from 0.1 to 0.8
- line_sigma: float32 [12, 10], replicated, may hold values from 0.05 to 0.4
- line_yield: float32 [12, 10], replicated, may hold values from 0.05 to 0.4
- step_rate: float32 [10], replicated, may hold values from 1 to 4
- view_axis: int32 [2], replicated, may hold values from 0 to 1, each once
- measured_first: float32 [12, 4, 2048], P(None, None, 'det'), may hold values from 0 to 0.8
- live_first: int32 [4, 2048], P(None, 'det'), may hold values 0 or 1
- measured_second: float32 [12, 4, 1024], P(None, None, 'beam'), may hold values from 0 to 0.8
- live_second: int32 [4, 1024], P(None, 'beam'), may hold values 0 or 1
Outputs:
- updated: float32 [10, 4, 1024, 2048], P(None, None, 'beam', 'det')
Inputs may be any that keep to these rules, and one draw needn't show every extreme that they name: `view_axis`: holds 0 once and 1 once. `live_first`: 1 marks a live pixel. `live_second`: 1 marks a live pixel.
All inputs are finite; a program needn't handle non-finite values. No bound on the sum of `live_first` or of `live_second` on one device may be relied on, other than what follows from the above.
Results may differ from a plain program's by a relative error of at most 0.00011.
Values sent between devices are 32-bit elements; how exact they have to be, the bound alone decides.
A program may use at most 128 MiB of HBM per device.

v0:
```python
import jax
import jax.numpy as jnp
from jax import lax
from jax.sharding import PartitionSpec as P

STEPS = 2


HIGH = lax.Precision.HIGHEST


def entering(part, axis, combine, identity, reverse):
    count = lax.axis_size(axis)
    place = lax.axis_index(axis)
    ahead = count - 1 - place if reverse else place
    gathered = lax.all_gather(part, axis)
    state = jnp.zeros_like(part) + jnp.asarray(identity, part.dtype)

    def one(turn, state):
        source = count - 1 - turn if reverse else turn
        return combine(state, lax.dynamic_index_in_dim(gathered, source, 0, False))

    return lax.fori_loop(0, ahead, one, state)


def along_rows(values, later):
    count = values.shape[-2]
    rows = lax.broadcasted_iota(jnp.int32, (count, count), 0)
    cols = lax.broadcasted_iota(jnp.int32, (count, count), 1)
    table = jnp.where(cols > rows if later else cols < rows, 1.0, 0.0).astype(jnp.float32)
    return jnp.einsum("ik,...kj->...ij", table, values, precision=HIGH)


def along_cols(values, later):
    count = values.shape[-1]
    rows = lax.broadcasted_iota(jnp.int32, (count, count), 0)
    cols = lax.broadcasted_iota(jnp.int32, (count, count), 1)
    table = jnp.where(rows > cols if later else rows < cols, 1.0, 0.0).astype(jnp.float32)
    return jnp.einsum("...ik,kj->...ij", values, table, precision=HIGH)


def add_pair(earlier, later):
    return earlier + later


def beam_chain(totals, backward):
    return entering(totals, "beam", add_pair, jnp.zeros_like(totals), backward)


def det_chain(totals, backward):
    return entering(totals, "det", add_pair, jnp.zeros_like(totals), backward)


def shards(
    concentration,
    incident_sigma,
    line_sigma,
    line_yield,
    step_rate,
    view_axis,
    measured_first,
    live_first,
    measured_second,
    live_second,
):
    lines = line_sigma.shape[0]
    elements = line_sigma.shape[1]
    det_count = lax.axis_size("det")
    step_x = 1.0 / (concentration.shape[2] * lax.axis_size("beam"))
    step_y = 1.0 / (concentration.shape[3] * det_count)
    sigma_first = jnp.where(view_axis[0] == 0, incident_sigma[0], incident_sigma[1])
    sigma_second = jnp.where(view_axis[0] == 0, incident_sigma[1], incident_sigma[0])
    table = jnp.concatenate([sigma_first[None], line_sigma, sigma_second[None]], 0)
    ones_row = jnp.ones((1, lines), jnp.float32)
    zero_row = jnp.zeros((1, lines), jnp.float32)
    zero_block = jnp.zeros((elements, lines), jnp.float32)
    pick_first = jnp.concatenate([ones_row, zero_block], 0)
    pick_second = jnp.concatenate([zero_row, line_sigma.T], 0)
    cross_first = jnp.concatenate([line_sigma.T, zero_row], 0)
    cross_second = jnp.concatenate([zero_block, ones_row], 0)
    live_one = live_first.astype(jnp.float32)
    live_two = live_second.astype(jnp.float32)
    conc = concentration
    for turn in range(STEPS):
        rates = jnp.einsum("re,ezij->rzij", table, conc, precision=HIGH)
        emitted = jnp.einsum("le,ezij->lzij", line_yield, conc, precision=HIGH)
        got_x = beam_chain(jnp.sum(rates[: lines + 1], axis=2), False)
        got_y = det_chain(jnp.sum(rates[1:], axis=3), False)
        cum_x = along_rows(rates[: lines + 1], False)
        cum_y = along_cols(rates[1:], False)
        tin_first = jnp.exp(-step_x * (cum_x[0] + got_x[0][:, None, :]))
        tout_second = jnp.exp(-step_x * (cum_x[1:] + got_x[1:][:, :, None, :]))
        tout_first = jnp.exp(-step_y * (cum_y[:lines] + got_y[:lines][:, :, :, None]))
        tin_second = jnp.exp(-step_y * (cum_y[lines] + got_y[lines][:, :, None]))
        part_first = step_x * jnp.sum(emitted * tin_first[None] * tout_first, axis=2)
        part_second = step_y * jnp.sum(emitted * tin_second[None] * tout_second, axis=3)
        pred_first = lax.psum(part_first, "beam")
        res_first = live_one[None] * (pred_first - measured_first)
        pred_second = lax.psum(part_second, "det")
        res_second = live_two[None] * (pred_second - measured_second)
        w_first = res_first[:, :, None, :] * tin_first[None] * tout_first
        w_second = res_second[:, :, :, None] * tin_second[None] * tout_second
        p_first = w_first * emitted
        p_second = w_second * emitted
        grad = jnp.einsum("le,lzij->ezij", line_yield, w_first + w_second, precision=HIGH)
        back_x = jnp.einsum("ml,lzij->mzij", pick_first, p_first, precision=HIGH) + jnp.einsum(
            "ml,lzij->mzij", pick_second, p_second, precision=HIGH
        )
        back_y = jnp.einsum("ml,lzij->mzij", cross_first, p_first, precision=HIGH) + jnp.einsum(
            "ml,lzij->mzij", cross_second, p_second, precision=HIGH
        )
        after_x = beam_chain(jnp.sum(back_x, axis=2), True)
        after_y = det_chain(jnp.sum(back_y, axis=3), True)
        rev_x = along_rows(back_x, True) + after_x[:, :, None, :]
        rev_y = along_cols(back_y, True) + after_y[:, :, :, None]
        grad = grad - step_x * (sigma_first[:, None, None, None] * rev_x[0][None] + rev_x[1:])
        grad = grad - step_y * (
            rev_y[:elements] + sigma_second[:, None, None, None] * rev_y[elements][None]
        )
        conc = conc - step_rate[:, None, None, None] * grad
    return conc


def solution(mesh):
    in_specs = (
        P(None, None, "beam", "det"),
        P(),
        P(),
        P(),
        P(),
        P(),
        P(None, None, "det"),
        P(None, "det"),
        P(None, None, "beam"),
        P(None, "beam"),
    )
    out_specs = P(None, None, "beam", "det")
    return jax.shard_map(shards, mesh=mesh, in_specs=in_specs, out_specs=out_specs, check_vma=False)
```

profile of v0, /device:TPU:0, one launch (start us, length us, event | category | flops | bytes accessed | tf_op | source)
XLA Modules:
  0.0 712.7 jit_solution(18397688998669549124)
XLA Ops:
  22.7 29.7 %all-gather = f32[104,4,128]{2,1,0:T(4,128)S(1)} all-gather(f32[13,4,128]{2,1,0:T(4,128)S(1)} %copy.50), channel_id=2, replica_groups=mesh['beam'=8,'det'=16] {'beam'}, dimensions={0}, use_global_device_ids=true | all-gather | bytes 239616 | tf_op jit(solution)/shard_map/all_gather | solution.py:16
  59.4 26.6 %all-gather.1 = f32[208,4,128]{2,1,0:T(4,128)} all-gather(f32[13,4,128]{2,1,0:T(4,128)S(1)} %copy.53), channel_id=3, replica_groups=mesh['beam'=8,'det'=16] {'det'}, dimensions={0}, use_global_device_ids=true | all-gather | bytes 452608 | tf_op jit(solution)/shard_map/all_gather | solution.py:16
  91.2 16.2 %multiply_reduce_fusion = (f32[12,4,128]{0,2,1:T(8,128)}, f32[12,4,128]{2,0,1:T(8,128)S(1)}, f32[12,4,128,128]{3,0,2,1:T(8,128)}) fusion(f32[13,4,128,128]{3,0,2,1:T(8,128)S(1)} %bitcast.182, f32[12,4,128]{2,0,1:T(8,128)S(1)} %copy.56, f32[4,128,128]{2,1,0:T(8,128)S(1)} %copy-done.15, f32[12,4,128]{0,2,1:T(8,128)S(1)} %copy-done.22, ...), kind=kOutput, calls=%fused_computation.59 | convolution fusion | flops 102223872 | bytes 12681696 | tf_op jit(solution)/shard_map/le,ezij->lzij/dot_general | solution.py:86
  108.0 35.1 %psum.28 = f32[12,4,128]{2,0,1:T(8,128)S(1)} all-reduce(f32[12,4,128]{2,0,1:T(8,128)} %broadcast_multiply_fusion.3), channel_id=1, replica_groups=mesh['beam'=8,'det'=16] {'beam'}, use_global_device_ids=true, to_apply=%region_7.8 | all-reduce | flops 6144 | bytes 49152 | tf_op jit(solution)/shard_map/psum | solution.py:97
  143.9 9.0 %fusion.71 = f32[11,4,128,128]{3,0,2,1:T(8,128)} fusion(f32[12,4,128,128]{3,0,2,1:T(8,128)} %get-tuple-element.407, f32[12,4,128,128]{3,2,1,0:T(8,128)S(1)} %slice.134, f32[12,4,128]{2,0,1:T(8,128)S(1)} %fusion.105, f32[12,4,128]{0,2,1:T(8,128)} %copy.54, f32[4,128,128]{2,1,0:T(8,128)} %bitcast.190, f32[10,12]{1,0:T(8,128)S(1)} %bitcast.205), kind=kOutput, calls=%fused_computation.100 | convolution fusion | flops 107741184 | bytes 9486816 | tf_op jit(solution)/shard_map/ml,lzij->mzij/dot_general | solution.py:109
  153.7 73.9 %psum.29 = f32[12,4,128]{0,2,1:T(8,128)} all-reduce(f32[12,4,128]{0,2,1:T(8,128)} %broadcast_multiply_fusion.1), channel_id=1, replica_groups=mesh['beam'=8,'det'=16] {'det'}, use_global_device_ids=true, to_apply=%region_9.10 | all-reduce | flops 6144 | bytes 49152 | tf_op jit(solution)/shard_map/psum | solution.py:99
  229.6 9.2 %fusion.171 = (f32[11,4,128]{0,2,1:T(8,128)}, f32[11,4,128,128]{3,0,2,1:T(8,128)S(1)}) fusion(f32[11,4,128,128]{3,0,2,1:T(8,128)} %fusion.71, f32[11,12,1,1]{1,0,3,2:T(8,128)S(1)} %copy-done.37, f32[12,4,128,128]{3,0,2,1:T(8,128)} %get-tuple-element.407, f32[13,4,128,128]{3,0,2,1:T(8,128)} %bitcast.180, f32[12,4,128]{0,2,1:T(8,128)S(1)} %subtract_multiply_fusion.1, ...), kind=kOutput, calls=%fused_computation.223 | convolution fusion | flops 109177344 | bytes 12655120 | tf_op jit(solution)/shard_map/ml,lzij->mzij/dot_general | solution.py:109
  244.5 21.4 %all-gather.3 = f32[176,4,128]{2,1,0:T(4,128)} all-gather(f32[11,4,128]{2,1,0:T(4,128)S(1)} %copy.65), channel_id=5, replica_groups=mesh['beam'=8,'det'=16] {'det'}, dimensions={0}, use_global_device_ids=true | all-gather | bytes 382976 | tf_op jit(solution)/shard_map/all_gather | solution.py:16
  265.9 11.6 %while.91 = (s32[]{:T(128)}, f32[11,4,128]{2,1,0:T(4,128)S(1)}, s32[]{:T(128)}, f32[16,11,4,128]{3,2,1,0:T(4,128)}, s32[]{:T(128)}, /*index=5*/s32[]{:T(128)}, s32[]{:T(128)}, s32[]{:T(128)}) while((s32[]{:T(128)}, f32[11,4,128]{2,1,0:T(4,128)S(1)}, s32[]{:T(128)}, f32[16,11,4,128]{3,2,1,0:T(4,128)}, s32[]{:T(128)}, /*index=5*/s32[]{:T(128)}, ...), condition=%wide.region_15.16_spmd, body=%wide.region_14.15_spmd.sunk | while | flops 5638 | bytes 67727 | solution.py:23
  295.1 6.9 fusion.47
  307.2 30.3 %all-gather.2 = f32[88,4,128]{2,1,0:T(4,128)} all-gather(f32[11,4,128]{2,1,0:T(4,128)S(1)} %copy.61), channel_id=4, replica_groups=mesh['beam'=8,'det'=16] {'beam'}, dimensions={0}, use_global_device_ids=true | all-gather | bytes 202752 | tf_op jit(solution)/shard_map/all_gather | solution.py:16
  348.5 15.7 %copy_subtract_fusion = f32[10,4,128,128]{3,0,2,1:T(8,128)S(1)} fusion(f32[10,4,128,128]{3,2,1,0:T(8,128)S(1)} %copy-done.9, f32[11,4,128,128]{3,0,2,1:T(8,128)} %copy_add_fusion.3, f32[11,4,128,128]{3,0,2,1:T(8,128)S(1)} %add_bitcast_fusion.1, f32[4,128,128]{2,1,0:T(8,128)S(1)} %bitcast.203, f32[10]{0:T(128)S(1)} %bitcast.211, ...), kind=kOutput, calls=%fused_computation.12 | convolution fusion | flops 108003328 | bytes 18186840 | tf_op jit(solution)/shard_map/le,lzij->ezij/dot_general | solution.py:105
  382.2 28.3 %all-gather.4 = f32[104,4,128]{2,1,0:T(4,128)S(1)} all-gather(f32[13,4,128]{2,1,0:T(4,128)S(1)} %copy.71), channel_id=6, replica_groups=mesh['beam'=8,'det'=16] {'beam'}, dimensions={0}, use_global_device_ids=true | all-gather | bytes 239616 | tf_op jit(solution)/shard_map/all_gather | solution.py:16
  417.5 21.9 %all-gather.5 = f32[208,4,128]{2,1,0:T(4,128)} all-gather(f32[13,4,128]{2,1,0:T(4,128)S(1)} %copy.74), channel_id=7, replica_groups=mesh['beam'=8,'det'=16] {'det'}, dimensions={0}, use_global_device_ids=true | all-gather | bytes 452608 | tf_op jit(solution)/shard_map/all_gather | solution.py:16
  444.6 14.2 %fusion.26 = (f32[12,4,128]{0,2,1:T(8,128)}, f32[12,4,128]{2,0,1:T(8,128)S(1)}, f32[4,128,128,12]{2,3,1,0:T(8,128)}) fusion(f32[13,4,128,128]{3,0,2,1:T(8,128)S(1)} %bitcast.177, f32[12,4,128]{2,0,1:T(8,128)S(1)} %copy.77, f32[4,128,128]{2,1,0:T(8,128)S(1)} %copy-done.14, f32[12,4,128]{0,2,1:T(8,128)S(1)} %copy-done.16, ...), kind=kOutput, calls=%fused_computation.47 | convolution fusion | flops 102223872 | bytes 12681696 | tf_op jit(solution)/shard_map/le,ezij->lzij/dot_general | solution.py:86
  459.4 31.6 %psum.30 = f32[12,4,128]{2,0,1:T(8,128)S(1)} all-reduce(f32[12,4,128]{2,0,1:T(8,128)} %broadcast_multiply_fusion.2), channel_id=1, replica_groups=mesh['beam'=8,'det'=16] {'beam'}, use_global_device_ids=true, to_apply=%region_23.24 | all-reduce | flops 6144 | bytes 49152 | tf_op jit(solution)/shard_map/psum | solution.py:97
  491.7 9.0 %fusion.75 = f32[11,4,128,128]{3,0,2,1:T(8,128)} fusion(f32[4,128,128,12]{2,3,1,0:T(8,128)} %get-tuple-element.412, f32[12,4,128,128]{3,2,1,0:T(8,128)S(1)} %slice.144, f32[12,4,128]{2,0,1:T(8,128)S(1)} %fusion.106, f32[12,4,128]{0,2,1:T(8,128)} %copy.75, f32[4,128,128]{2,1,0:T(8,128)} %bitcast.186, f32[10,12]{1,0:T(8,128)S(1)} %bitcast.207), kind=kOutput, calls=%fused_computation.102 | convolution fusion | flops 107741184 | bytes 9486816 | tf_op jit(solution)/shard_map/ml,lzij->mzij/dot_general | solution.py:109
  501.4 76.4 %psum.31 = f32[12,4,128]{0,2,1:T(8,128)} all-reduce(f32[12,4,128]{0,2,1:T(8,128)} %broadcast_multiply_fusion), channel_id=1, replica_groups=mesh['beam'=8,'det'=16] {'det'}, use_global_device_ids=true, to_apply=%region_25.26 | all-reduce | flops 6144 | bytes 49152 | tf_op jit(solution)/shard_map/psum | solution.py:99
  579.0 9.2 %fusion.173 = (f32[11,4,128]{0,2,1:T(8,128)}, f32[11,4,128,128]{3,0,2,1:T(8,128)S(1)}) fusion(f32[11,4,128,128]{3,0,2,1:T(8,128)} %fusion.75, f32[11,12,1,1]{1,0,3,2:T(8,128)S(1)} %copy-done.38, f32[4,128,128,12]{2,3,1,0:T(8,128)} %get-tuple-element.412, f32[13,4,128,128]{3,0,2,1:T(8,128)} %bitcast.175, f32[12,4,128]{0,2,1:T(8,128)S(1)} %subtract_multiply_fusion, ...), kind=kOutput, calls=%fused_computation.225 | convolution fusion | flops 109177344 | bytes 12655120 | tf_op jit(solution)/shard_map/ml,lzij->mzij/dot_general | solution.py:109
  593.9 21.4 %all-gather.7 = f32[176,4,128]{2,1,0:T(4,128)} all-gather(f32[11,4,128]{2,1,0:T(4,128)S(1)} %copy.85), channel_id=9, replica_groups=mesh['beam'=8,'det'=16] {'det'}, dimensions={0}, use_global_device_ids=true | all-gather | bytes 382976 | tf_op jit(solution)/shard_map/all_gather | solution.py:16
  615.3 11.6 %while.95 = (s32[]{:T(128)}, f32[11,4,128]{2,1,0:T(4,128)S(1)}, s32[]{:T(128)}, f32[16,11,4,128]{3,2,1,0:T(4,128)}, s32[]{:T(128)}, /*index=5*/s32[]{:T(128)}, s32[]{:T(128)}, s32[]{:T(128)}) while((s32[]{:T(128)}, f32[11,4,128]{2,1,0:T(4,128)S(1)}, s32[]{:T(128)}, f32[16,11,4,128]{3,2,1,0:T(4,128)}, s32[]{:T(128)}, /*index=5*/s32[]{:T(128)}, ...), condition=%wide.region_31.32_spmd, body=%wide.region_30.31_spmd.sunk | while | flops 5638 | bytes 67727 | solution.py:23
  644.6 6.9 fusion.43
  656.7 30.3 %all-gather.6 = f32[88,4,128]{2,1,0:T(4,128)} all-gather(f32[11,4,128]{2,1,0:T(4,128)S(1)} %copy.81), channel_id=8, replica_groups=mesh['beam'=8,'det'=16] {'beam'}, dimensions={0}, use_global_device_ids=true | all-gather | bytes 202752 | tf_op jit(solution)/shard_map/all_gather | solution.py:16
  698.0 11.9 %fusion.7 = f32[10,4,128,128]{3,0,2,1:T(8,128)S(1)} fusion(f32[10,4,128,128]{3,0,2,1:T(8,128)S(1)} %copy-done.11, f32[11,4,128,128]{3,0,2,1:T(8,128)} %copy_add_fusion.2, f32[11,4,128,128]{3,0,2,1:T(8,128)S(1)} %add_bitcast_fusion, f32[4,128,128]{2,1,0:T(8,128)S(1)} %bitcast.201, f32[4,128,128]{2,1,0:T(8,128)S(1)} %bitcast.202, f32[10]{0:T(128)S(1)} %bitcast.212, ...), kind=kOutput, calls=%fused_computation.17 | convolution fusion | flops 108003328 | bytes 18186840 | tf_op jit(solution)/shard_map/le,lzij->ezij/dot_general | solution.py:105
  (240 shorter events, 185.8 us)
Async XLA Ops:
  0.0 91.2 %copy-start = (f32[12,10]{1,0:T(8,128)S(1)}, f32[12,10]{1,0:T(8,128)}, u32[]{:S(2)}) copy-start(f32[12,10]{1,0:T(8,128)} %param.29) | copy-start | bytes 1444
  58.2 28.7 %copy-start.12 = (f32[13,4,128,128]{3,2,1,0:T(8,128)}, f32[13,4,128,128]{3,2,1,0:T(8,128)S(1)}, u32[]{:S(2)}) copy-start(f32[13,4,128,128]{3,2,1,0:T(8,128)S(1)} %fusion.36) | copy-start | bytes 10223620
  91.1 16.3 %copy-start.25 = (f32[1,4,128,128]{3,0,2,1:T(1,128)}, f32[1,4,128,128]{3,0,2,1:T(1,128)S(1)}, u32[]{:S(2)}) copy-start(f32[1,4,128,128]{3,0,2,1:T(1,128)S(1)} %fusion.86) | copy-start | bytes 786436
  91.2 51.9 %copy-start.52 = (s32[4,128]{1,0:T(4,128)S(1)}, s32[4,128]{1,0:T(4,128)}, u32[]{:S(2)}) copy-start(s32[4,128]{1,0:T(4,128)} %param.33) | copy-start | bytes 6148
  91.2 52.6 %copy-start.36 = (f32[12,10]{1,0:T(8,128)S(1)}, f32[12,10]{1,0:T(8,128)}, u32[]{:S(2)}) copy-start(f32[12,10]{1,0:T(8,128)} %param.28) | copy-start | bytes 1444
  143.1 9.9 %copy-start.44 = (f32[4,128]{1,0:T(4,128)}, f32[4,128]{1,0:T(4,128)S(1)}, u32[]{:S(2)}) copy-start(f32[4,128]{1,0:T(4,128)S(1)} %convert_element_type.6) | copy-start | bytes 6148
  143.9 9.0 %copy-start.34 = (f32[12,4,128]{0,2,1:T(8,128)S(1)}, f32[12,4,128]{0,2,1:T(8,128)}, u32[]{:S(2)}) copy-start(f32[12,4,128]{0,2,1:T(8,128)} %get-tuple-element.333) | copy-start | bytes 73732
  143.9 83.6 %copy-start.41 = (f32[12,4,128]{2,1,0:T(4,128)S(1)}, f32[12,4,128]{2,1,0:T(4,128)}, u32[]{:S(2)}) copy-start(f32[12,4,128]{2,1,0:T(4,128)} %param.34) | copy-start | bytes 73732
  143.9 84.5 %copy-start.53 = (s32[4,128]{1,0:T(4,128)S(1)}, s32[4,128]{1,0:T(4,128)}, u32[]{:S(2)}) copy-start(s32[4,128]{1,0:T(4,128)} %param.35) | copy-start | bytes 6148
  143.9 85.6 %copy-start.37 = (f32[11,12,1,1]{1,0,3,2:T(8,128)S(1)}, f32[11,12,1,1]{1,0,3,2:T(8,128)}, u32[]{:S(2)}) copy-start(f32[11,12,1,1]{1,0,3,2:T(8,128)} %constant.165) | copy-start | bytes 1588
  228.4 10.4 %copy-start.42 = (f32[4,128]{1,0:T(4,128)}, f32[4,128]{1,0:T(4,128)S(1)}, u32[]{:S(2)}) copy-start(f32[4,128]{1,0:T(4,128)S(1)} %convert_element_type.7) | copy-start | bytes 6148
  229.6 9.2 %copy-start.31 = (f32[12,4,128]{0,2,1:T(8,128)}, f32[12,4,128]{0,2,1:T(8,128)S(1)}, u32[]{:S(2)}) copy-start(f32[12,4,128]{0,2,1:T(8,128)S(1)} %subtract_multiply_fusion.1) | copy-start | bytes 73732
  265.9 18.0 %copy-start.39 = (f32[11,12,1,1]{1,0,3,2:T(8,128)S(1)}, f32[11,12,1,1]{1,0,3,2:T(8,128)}, u32[]{:S(2)}) copy-start(f32[11,12,1,1]{1,0,3,2:T(8,128)} %constant.164) | copy-start | bytes 1588
  283.9 6.5 copy-start.7
  416.3 24.0 %copy-start.13 = (f32[13,4,128,128]{3,2,1,0:T(8,128)}, f32[13,4,128,128]{3,2,1,0:T(8,128)S(1)}, u32[]{:S(2)}) copy-start(f32[13,4,128,128]{3,2,1,0:T(8,128)S(1)} %fusion.32) | copy-start | bytes 10223620
  444.6 14.2 %copy-start.19 = (f32[1,4,128,128]{3,0,2,1:T(1,128)}, f32[1,4,128,128]{3,0,2,1:T(1,128)S(1)}, u32[]{:S(2)}) copy-start(f32[1,4,128,128]{3,0,2,1:T(1,128)S(1)} %fusion.81) | copy-start | bytes 786436
  444.6 46.4 %copy-start.45 = (f32[4,128]{1,0:T(4,128)S(1)}, f32[4,128]{1,0:T(4,128)}, u32[]{:S(2)}) copy-start(f32[4,128]{1,0:T(4,128)} %copy-done.44) | copy-start | bytes 6148
  491.7 9.0 %copy-start.35 = (f32[12,4,128]{0,2,1:T(8,128)S(1)}, f32[12,4,128]{0,2,1:T(8,128)}, u32[]{:S(2)}) copy-start(f32[12,4,128]{0,2,1:T(8,128)} %get-tuple-element.329) | copy-start | bytes 73732
  491.7 86.1 %copy-start.43 = (f32[4,128]{1,0:T(4,128)S(1)}, f32[4,128]{1,0:T(4,128)}, u32[]{:S(2)}) copy-start(f32[4,128]{1,0:T(4,128)} %copy-done.42) | copy-start | bytes 6148
  491.7 87.3 %copy-start.38 = (f32[11,12,1,1]{1,0,3,2:T(8,128)S(1)}, f32[11,12,1,1]{1,0,3,2:T(8,128)}, u32[]{:S(2)}) copy-start(f32[11,12,1,1]{1,0,3,2:T(8,128)} %constant.165) | copy-start | bytes 1588
  579.0 9.2 %copy-start.28 = (f32[12,4,128]{0,2,1:T(8,128)}, f32[12,4,128]{0,2,1:T(8,128)S(1)}, u32[]{:S(2)}) copy-start(f32[12,4,128]{0,2,1:T(8,128)S(1)} %subtract_multiply_fusion) | copy-start | bytes 73732
  615.3 17.9 %copy-start.40 = (f32[11,12,1,1]{1,0,3,2:T(8,128)S(1)}, f32[11,12,1,1]{1,0,3,2:T(8,128)}, u32[]{:S(2)}) copy-start(f32[11,12,1,1]{1,0,3,2:T(8,128)} %constant.164) | copy-start | bytes 1588
  633.3 6.5 copy-start.4
  633.3 6.5 copy-start.29
  (32 other events, 151.9 us)
where the time goes:
time: 725 us; the launch traced here: 713 us
  blocking collectives  427 us (59%)
  matrix products  175 us (24%)
  other arithmetic  67.3 us (9%)
  local copies, waits for them, and re-layouts  41.1 us (6%)
    all_gather x8, blocking collectives, entering(): gathered = lax.all_gather(part, axis)  210 us
    psum x2, blocking collectives, shards(): pred_second = lax.psum(part_second, 'det')  150 us
    psum x2, blocking collectives, shards(): pred_first = lax.psum(part_first, 'beam')  66.6 us
    add x44, other arithmetic, add_pair(): return earlier + later  33.2 us
    dot_general x2, matrix products, shards(): emitted = jnp.einsum('le,ezij->lzij', line_yield, conc, precision=HIGH)  30.3 us
    dot_general x2, matrix products, shards(): jnp.einsum('le,lzij->ezij', line_yield, w_first + w_second, precision=HIGH)  27.7 us
    dot_general x4, matrix products, along_rows(): return jnp.einsum('ik,...kj->...ij', table, values, precision=HIGH)  27.1 us
    dot_general x4, matrix products, along_cols(): return jnp.einsum('...ik,kj->...ij', values, table, precision=HIGH)  20.6 us

commit v1 on v0

v1 whole, which is shorter than its diff:
```python
import math

import jax
import jax.numpy as jnp
from jax import lax
from jax.experimental import pallas as pl
from jax.experimental.pallas import tpu as pltpu
from jax.sharding import PartitionSpec as P

STEPS = 2
HIGH = lax.Precision.HIGHEST
MESH = pl.DeviceIdType.MESH
F32 = jnp.float32
BF16 = jnp.bfloat16
ELEMENTS = 10
LINES = 12
ZS = 4
N = 128
FIELDS = 26
LOG2E = math.log2(math.e)


def split(value):
    high = value.astype(BF16)
    return high, (value - high.astype(F32)).astype(BF16)


def iota(shape, dim):
    return lax.broadcasted_iota(jnp.int32, shape, dim)


def dot(a, b):
    return jnp.dot(a, b, preferred_element_type=F32)


def exact(a, b):
    return jnp.dot(a, b, preferred_element_type=F32, precision=HIGH)


def exact_nt(a, b):
    return lax.dot_general(
        a, b, (((1,), (1,)), ((), ())), preferred_element_type=F32, precision=HIGH
    )


def one_hot(condition):
    return jnp.where(condition, 1.0, 0.0).astype(F32)


def cum_cols(value, table):
    high, low = split(value)
    return dot(jnp.concatenate([high, low], 1), table)


def cum_rows(value, table):
    high, low = split(value)
    return dot(table, jnp.concatenate([high, low], 0))


class Ring:
    def __init__(self, axis, send, recv, back, done, sems):
        self.axis = axis
        self.count = recv.shape[2]
        self.me = lax.axis_index(axis)
        self.send, self.recv, self.back, self.done, self.sems = send, recv, back, done, sems
        self.tiles = self.count // ZS

    def greet(self, barrier):
        def one(d, carry):
            peer = lax.rem(self.me + d, self.count)
            pl.semaphore_signal(
                barrier, inc=1, device_id={self.axis: peer}, device_id_type=MESH
            )
            return carry

        lax.fori_loop(1, self.count, one, 0)

    def copy(self, src, dst, step, phase, leg, peer):
        return pltpu.make_async_remote_copy(
            src_ref=src,
            dst_ref=dst,
            send_sem=self.sems.at[step, phase, leg, 0],
            recv_sem=self.sems.at[step, phase, leg, 1],
            device_id={self.axis: peer},
            device_id_type=MESH,
        )

    def start(self, step, phase):
        mine = (step, phase, pl.ds(self.me, 1))
        self.recv[mine] = self.send[mine]

        def one(d, carry):
            peer = lax.rem(self.me + d, self.count)
            self.copy(
                self.send.at[step, phase, peer], self.recv.at[step, phase, self.me], step, phase, 0, peer
            ).start()
            return carry

        lax.fori_loop(1, self.count, one, 0)

    def wait(self, src, dst, step, phase, leg):
        several = (step, phase, pl.ds(0, self.count - 1))
        peer = lax.rem(self.me + 1, self.count)
        whole = self.copy(src.at[several], dst.at[several], step, phase, leg, peer)
        whole.wait_send()
        whole.wait_recv()

    def middle(self, step, phase, mode):
        self.wait(self.send, self.recv, step, phase, 0)
        total = jnp.zeros((8, N), F32)
        order = range(self.count)
        for t in reversed(order) if mode == "later" else order:
            if mode != "sum":
                self.back[step, phase, t] = total
            total = total + self.recv[step, phase, t]
        if mode == "sum":
            self.back[step, phase, 0] = total
            self.done[step, phase, pl.ds(self.me, 1)] = total[None]
        else:
            mine = (step, phase, pl.ds(self.me, 1))
            self.done[mine] = self.back[mine]

        def one(d, carry):
            peer = lax.rem(self.me + d, self.count)
            source = 0 if mode == "sum" else peer
            self.copy(
                self.back.at[step, phase, source], self.done.at[step, phase, self.me], step, phase, 1, peer
            ).start()
            return carry

        lax.fori_loop(1, self.count, one, 0)

    def finish(self, step, phase):
        self.wait(self.back, self.done, step, phase, 1)

    def put(self, step, phase, z, row, per, value):
        self.send[step, phase, z * self.tiles + row // per, pl.ds(row % per, 1), :] = value

    def get(self, step, phase, z, row, per):
        return self.done[step, phase, z * self.tiles + row // per, pl.ds(row % per, 1), :]

    def got(self, step, phase, z):
        rows = self.done[step, phase, pl.ds(z * self.tiles, self.tiles)]
        return rows.reshape(self.tiles * 8, N)

    def put_all(self, step, phase, z, rows):
        self.send[step, phase, pl.ds(z * self.tiles, self.tiles)] = rows.reshape(self.tiles, 8, N)


def over_z(body):
    def one(z, carry):
        body(z)
        return carry

    lax.fori_loop(0, ZS, one, 0)


def kernel(
    step_x, step_y,
    axis_ref, conc_ref, inc_ref, sig_ref, yld_ref, rate_ref, m1_ref, live1_ref, m2_ref, live2_ref,
    c_ref,
    f_ref, a1_ref, a2_ref, s2c_ref, ex_ref, ey_ref, q1_ref, q2_ref, r1_ref, r2_ref, mx_ref, my_ref,
    tx_ref, ty_ref, tab_ref, back_ref, mix_ref, unmix_ref, up_ref, down_ref, left_ref, right_ref,
    wax_ref, way_ref, wcx_ref, wcy_ref,
    bsend, brecv, bback, bdone, bsems, dsend, drecv, dback, ddone, dsems,
):
    beam = Ring("beam", bsend, brecv, bback, bdone, bsems)
    det = Ring("det", dsend, drecv, dback, ddone, dsems)
    per_x = {ELEMENTS: -(-ELEMENTS // beam.tiles), LINES: -(-LINES // beam.tiles)}
    per_y = {ELEMENTS: -(-ELEMENTS // det.tiles), LINES: -(-LINES // det.tiles)}
    barrier = pltpu.get_barrier_semaphore()
    beam.greet(barrier)
    det.greet(barrier)

    for ref in (bsend, dsend, q1_ref, q2_ref, r1_ref, r2_ref, tx_ref, ty_ref, tab_ref, back_ref):
        ref[...] = jnp.zeros(ref.shape, F32)

    lane = iota((N, N), 1)

    def totals(z, step):
        acc = jnp.zeros((N, N), F32)
        for e in range(ELEMENTS):
            c = c_ref[e, z]
            beam.put(step, 0, z, e, per_x[ELEMENTS], jnp.sum(c, 0, keepdims=True))
            acc = jnp.where(lane == e, jnp.sum(c, 1, keepdims=True), acc)
        rows = acc.T
        for e in range(ELEMENTS):
            det.put(step, 0, z, e, per_y[ELEMENTS], rows[e : e + 1])

    def begin(z):
        c_ref[:, z] = conc_ref[:, z]
        totals(z, 0)

    over_z(begin)
    pl.semaphore_wait(barrier, beam.count + det.count - 2)

    def tables():
        first = axis_ref[0] == 0
        one, two = inc_ref[0:1, :], inc_ref[1:2, :]
        s1 = jnp.where(first, one, two)
        s2 = jnp.where(first, two, one)
        scale = -LOG2E * step_y
        sig, yld, rate = sig_ref[...], yld_ref[...], rate_ref[...]
        cols = pl.ds(0, ELEMENTS)
        tab_ref[0:LINES, cols] = scale * sig
        tab_ref[LINES : LINES + 1, cols] = scale * s2
        tab_ref[LINES + 1 : LINES + 2, cols] = scale * s1
        tab_ref[LINES + 2 : FIELDS, cols] = yld
        back_ref[0:LINES, cols] = yld * rate
        back_ref[LINES : 2 * LINES, cols] = -sig * rate
        back_ref[2 * LINES : 2 * LINES + 1, cols] = -s1 * rate
        back_ref[2 * LINES + 1 : FIELDS, cols] = -s2 * rate

        tab, back = tab_ref[...], back_ref[...]
        wide = 8 * ELEMENTS
        pick = one_hot((iota((8 * FIELDS, 32), 0) >> 3) == iota((8 * FIELDS, 32), 1))
        col = iota((N, 256), 1)
        part = (col >= wide).astype(jnp.int32) + (col >= 2 * wide).astype(jnp.int32)
        spread = one_hot(((col - wide * part) >> 3) == iota((N, 256), 0))
        spread = jnp.where(col < 3 * wide, spread, 0.0)
        full = exact(pick, exact(tab, spread))
        shape = (8 * FIELDS, 256)
        full = jnp.where((iota(shape, 0) & 7) == (iota(shape, 1) & 7), full, 0.0)
        high, low = split(full)
        part = iota(shape, 1)
        mix_ref[...] = jnp.where((part >= wide) & (part < 2 * wide), low.astype(F32), high.astype(F32)).astype(BF16)

        pick = one_hot((iota((wide, N), 0) >> 3) == iota((wide, N), 1))
        shape = (wide, 8 * FIELDS)
        spread = one_hot((iota((32, 8 * FIELDS), 1) >> 3) == iota((32, 8 * FIELDS), 0))
        full = exact(exact_nt(pick, back), spread)
        full = jnp.where((iota(shape, 0) & 7) == (iota(shape, 1) & 7), full, 0.0)
        high, low = split(full)
        unmix_ref[0:wide] = high
        unmix_ref[wide : 2 * wide] = low

        def layout(ring, per):
            shape = (8 * ring.tiles, N)
            row = iota(shape, 0)
            inside = row & 7
            return one_hot((inside < per) & ((row >> 3) * per + inside == iota(shape, 1)))

        place_x = layout(beam, per_x[ELEMENTS])
        place_y = layout(det, per_y[ELEMENTS])
        used = iota((32, N), 0) < LINES + 2
        rates = jnp.where(used, tab, 0.0)
        wax_ref[...] = exact_nt(rates * (step_x / step_y), place_x)
        way_ref[...] = exact_nt(rates, place_y)
        row = iota((32, N), 0)
        lines = (row >= LINES) & (row < 2 * LINES)
        wcx_ref[...] = exact_nt(place_x, jnp.where(lines | (row == 2 * LINES), -step_x * back, 0.0))
        wcy_ref[...] = exact_nt(place_y, jnp.where(lines | (row == 2 * LINES + 1), -step_y * back, 0.0))

        r, c = iota((2 * N, N), 0) & (N - 1), iota((2 * N, N), 1)
        up_ref[...] = one_hot(r < c).astype(BF16)
        down_ref[...] = (step_y * one_hot(r > c)).astype(BF16)
        r, c = iota((N, 2 * N), 0), iota((N, 2 * N), 1) & (N - 1)
        left_ref[...] = (step_x / step_y * one_hot(c < r)).astype(BF16)
        right_ref[...] = (step_x * one_hot(c > r)).astype(BF16)
        for z in range(ZS):
            for l in range(LINES):
                mx_ref[z, l : l + 1, :] = m1_ref[l, z : z + 1, :]
                my_ref[z, l : l + 1, :] = m2_ref[l, z : z + 1, :]

    def blocks(body):
        def one(n, carry):
            body(n // 4, pl.multiple_of((n % 4) * 32, 32))
            return carry

        lax.fori_loop(0, 4 * ZS, one, 0)

    def mix(z, r0):
        parts = []
        for b in range(4):
            high, low = split(c_ref[:, z, pl.ds(r0 + 8 * b, 8), :].reshape(8 * ELEMENTS, N))
            parts.append(jnp.concatenate([high, high, low, jnp.zeros((16, N), BF16)], 0))
        out = dot(mix_ref[...], jnp.concatenate(parts, 1))
        for b in range(4):
            f_ref[z, :, pl.ds(r0 + 8 * b, 8), :] = out[:, b * N : (b + 1) * N].reshape(FIELDS, 8, N)

    def unmix(z, r0):
        highs, lows = [], []
        for b in range(4):
            rows = pl.ds(r0 + 8 * b, 8)
            w = a1_ref[z, :, rows, :].reshape(8 * LINES, N)
            v = f_ref[z, 0 : LINES + 2, rows, :].reshape(8 * (LINES + 2), N)
            high, low = split(jnp.concatenate([w, v], 0))
            highs.append(high)
            lows.append(low)
        wide = 8 * ELEMENTS
        one = dot(unmix_ref[...], jnp.concatenate(highs, 1))
        two = dot(unmix_ref[0:wide], jnp.concatenate(lows, 1))
        out = one[0:wide] + (one[wide:] + two)
        for b in range(4):
            rows = pl.ds(r0 + 8 * b, 8)
            c_ref[:, z, rows, :] = c_ref[:, z, rows, :] - out[:, b * N : (b + 1) * N].reshape(ELEMENTS, 8, N)

    def attenuate(z):
        tin1 = jnp.exp2(cum_rows(f_ref[z, LINES + 1], left_ref[...]))
        tin2 = jnp.exp2(cum_cols(f_ref[z, LINES], up_ref[...]))
        for l in range(0, LINES, 2):
            high0, low0 = split(f_ref[z, l])
            high1, low1 = split(f_ref[z, l + 1])
            across = jnp.concatenate(
                [jnp.concatenate([high0, low0], 1), jnp.concatenate([high1, low1], 1)], 0
            )
            along = jnp.concatenate(
                [jnp.concatenate([high0, high1], 1), jnp.concatenate([low0, low1], 1)], 0
            )
            over_y = jnp.exp2(dot(across, up_ref[...]))
            over_x = jnp.exp2(dot(left_ref[...], along))
            for k in range(2):
                a1_ref[z, l + k] = tin1 * over_y[k * N : (k + 1) * N]
                a2_ref[z, l + k] = tin2 * over_x[:, k * N : (k + 1) * N]

    def turned(rows):
        return jnp.concatenate([rows, jnp.zeros((N - rows.shape[0], N), F32)], 0).T

    def counts(z, step):
        ex = jnp.exp2(exact(wax_ref[...], beam.got(step, 0, z))[0:16])
        ey = jnp.exp2(exact(way_ref[...], det.got(step, 0, z))[0:16])
        ex_ref[z], ey_ref[z] = ex, ey
        cols = turned(ey)
        enter = step_x * ex[LINES + 1 : LINES + 2]
        acc = jnp.zeros((N, N), F32)
        for l in range(LINES):
            q = f_ref[z, LINES + 2 + l]
            a1 = a1_ref[z, l] * cols[:, l : l + 1]
            a1_ref[z, l] = a1
            part = enter * jnp.sum(q * a1, 0, keepdims=True)
            q1_ref[z, l : l + 1, :] = part
            beam.put(step, 1, z, l, per_x[LINES], part)
            acc = jnp.where(lane == l, jnp.sum(q * (a2_ref[z, l] * ex[l : l + 1]), 1, keepdims=True), acc)
        rows = acc.T
        part = step_y * ey[LINES : LINES + 1] * rows[0:16]
        q2_ref[z] = part
        for l in range(LINES):
            det.put(step, 1, z, l, per_y[LINES], part[l : l + 1])

    def residuals(z, step):
        live1 = live1_ref[pl.ds(z, 1), :].astype(F32)
        live2 = live2_ref[pl.ds(z, 1), :].astype(F32)
        for l in range(LINES):
            row = pl.ds(l, 1)
            r1_ref[z, row, :] = live1 * (beam.get(step, 1, z, l, per_x[LINES]) - mx_ref[z, row, :])
            r2_ref[z, row, :] = live2 * (det.get(step, 1, z, l, per_y[LINES]) - my_ref[z, row, :])
        ex, ey = ex_ref[z], ey_ref[z]
        res1, res2 = r1_ref[z], r2_ref[z]
        tx_ref[2 * LINES : 2 * LINES + 1] = jnp.sum(res1 * q1_ref[z], 0, keepdims=True) / step_x
        ty_ref[2 * LINES + 1 : 2 * LINES + 2] = jnp.sum(res2 * q2_ref[z], 0, keepdims=True) / step_y
        r1 = res1 * ex[LINES + 1 : LINES + 2]
        r1_ref[z] = r1
        cols = turned(res2 * ey[LINES : LINES + 1])
        s2c_ref[z] = cols
        acc = jnp.zeros((N, N), F32)
        for l in range(LINES):
            q = f_ref[z, LINES + 2 + l]
            acc = jnp.where(lane == LINES + l, jnp.sum(q * (a1_ref[z, l] * r1[l : l + 1]), 1, keepdims=True), acc)
            seen = jnp.sum(q * (a2_ref[z, l] * cols[:, l : l + 1]), 0, keepdims=True)
            tx_ref[LINES + l : LINES + l + 1, :] = ex[l : l + 1] * seen
        ty_ref[LINES : 2 * LINES, :] = acc.T[LINES : 2 * LINES]
        beam.put_all(step, 2, z, exact(wcx_ref[...], tx_ref[...]))
        det.put_all(step, 2, z, exact(wcy_ref[...], ty_ref[...]))

    def weights(z):
        ex, r1 = ex_ref[z], r1_ref[z]
        cols = s2c_ref[z]
        sum1 = jnp.zeros((N, N), F32)
        sum2 = jnp.zeros((N, N), F32)
        for l in range(LINES):
            q = f_ref[z, LINES + 2 + l]
            w1 = a1_ref[z, l] * r1[l : l + 1]
            w2 = a2_ref[z, l] * ex[l : l + 1] * cols[:, l : l + 1]
            a1_ref[z, l] = w1 + w2
            p1, p2 = q * w1, q * w2
            sum1, sum2 = sum1 + p1, sum2 + p2
            f_ref[z, l] = cum_cols(p1, down_ref[...]) + cum_rows(p2, right_ref[...])
        f_ref[z, LINES] = cum_rows(sum1, right_ref[...])
        f_ref[z, LINES + 1] = cum_cols(sum2, down_ref[...])

    def update(z, step):
        cols = turned(det.got(step, 2, z))
        for e in range(ELEMENTS):
            per = per_y[ELEMENTS]
            spot = (e // per) * 8 + e % per
            c_ref[e, z] = c_ref[e, z] + beam.get(step, 2, z, e, per_x[ELEMENTS]) + cols[:, spot : spot + 1]

    def turn(step, carry):
        @pl.when(step > 0)
        def again():
            over_z(lambda z: totals(z, step))

        beam.start(step, 0)
        det.start(step, 0)

        @pl.when(step == 0)
        def prepare():
            tables()

        blocks(mix)
        beam.middle(step, 0, "earlier")
        det.middle(step, 0, "earlier")
        over_z(attenuate)
        beam.finish(step, 0)
        det.finish(step, 0)
        over_z(lambda z: counts(z, step))
        beam.start(step, 1)
        det.start(step, 1)
        beam.middle(step, 1, "sum")
        det.middle(step, 1, "sum")
        beam.finish(step, 1)
        det.finish(step, 1)
        over_z(lambda z: residuals(z, step))
        beam.start(step, 2)
        det.start(step, 2)
        over_z(weights)
        beam.middle(step, 2, "later")
        det.middle(step, 2, "later")
        blocks(unmix)
        beam.finish(step, 2)
        det.finish(step, 2)
        over_z(lambda z: update(z, step))
        return carry

    lax.fori_loop(0, STEPS, turn, 0)


def solution(mesh):
    beams, dets = mesh.shape["beam"], mesh.shape["det"]

    def shards(conc, inc, sig, yld, rate, axis, m1, live1, m2, live2):
        step_x = 1.0 / (conc.shape[2] * beams)
        step_y = 1.0 / (conc.shape[3] * dets)

        def body(*refs):
            kernel(step_x, step_y, *refs)

        field = (N, N)
        rows = pltpu.VMEM((ZS, 16, N), F32)

        def exchange(count):
            tiles = pltpu.VMEM((STEPS, 3, count, 8, N), F32)
            return [tiles] * 4 + [pltpu.SemaphoreType.DMA((STEPS, 3, 2, 2))]

        vmem = pl.BlockSpec(memory_space=pltpu.VMEM)
        return pl.pallas_call(
            body,
            out_shape=jax.ShapeDtypeStruct(conc.shape, F32),
            in_specs=[pl.BlockSpec(memory_space=pltpu.SMEM)] + [vmem] * 9,
            out_specs=vmem,
            scratch_shapes=[
                pltpu.VMEM((ZS, FIELDS) + field, F32),
                pltpu.VMEM((ZS, LINES) + field, F32),
                pltpu.VMEM((ZS, LINES) + field, F32),
                pltpu.VMEM((ZS,) + field, F32),
                *[rows] * 8,
                *[pltpu.VMEM((32, N), F32)] * 4,
                pltpu.VMEM((8 * FIELDS, 2 * N), BF16),
                pltpu.VMEM((16 * ELEMENTS, 8 * FIELDS), BF16),
                *[pltpu.VMEM((2 * N, N), BF16)] * 2,
                *[pltpu.VMEM((N, 2 * N), BF16)] * 2,
                pltpu.VMEM((32, 2 * beams), F32),
                pltpu.VMEM((32, 2 * dets), F32),
                pltpu.VMEM((2 * beams, 32), F32),
                pltpu.VMEM((2 * dets, 32), F32),
                *exchange(beams),
                *exchange(dets),
            ],
            compiler_params=pltpu.CompilerParams(
                collective_id=0, has_side_effects=True, vmem_limit_bytes=52 * 1024 * 1024
            ),
        )(axis, conc, inc, sig, yld, rate[None], m1, live1, m2, live2)

    in_specs = (
        P(None, None, "beam", "det"),
        P(),
        P(),
        P(),
        P(),
        P(),
        P(None, None, "det"),
        P(None, "det"),
        P(None, None, "beam"),
        P(None, "beam"),
    )
    out_specs = P(None, None, "beam", "det")
    return jax.shard_map(shards, mesh=mesh, in_specs=in_specs, out_specs=out_specs, check_vma=False)
```

time: 725 us -> 102 us (0.14); the launches traced: 713 us -> 100 us
  blocking collectives: 427 us -> 0 us
  matrix products: 175 us -> 0 us
  Pallas kernels: 0 us -> 90.3 us
  other arithmetic: 67.3 us -> 0 us
  local copies, waits for them, and re-layouts: 41.1 us -> 9.75 us
    psum x4 -> x0, blocking collectives: 217 us -> none  [the longest x2 150 us: shards(): pred_second = lax.psum(part_second, 'det')]
    all_gather x8 -> x0, blocking collectives: 210 us -> none  [entering(): gathered = lax.all_gather(part, axis)]
    dot_general x22 -> x0, matrix products: 175 us -> none  [the longest x2 30.3 us: shards(): emitted = jnp.einsum('le,ezij->lzij', line_yield, conc, precision=HIGH)]
    pallas_call x0 -> x1, Pallas kernels: none -> 90.3 us  [shards(): pl.pallas_call(body, out_shape=jax.ShapeDtypeStruct(conc.shape, F32), in_...]
    add x48 -> x0, other arithmetic: 49.6 us -> none  [the longest x44 33.2 us: add_pair(): return earlier + later]
    dot_general x4 -> x0, local copies, waits for them, and re-layouts: 17.3 us -> none  [along_rows(): return jnp.einsum('ik,...kj->...ij', table, values, precision=HIGH)]
    slice x14 -> x0, local copies, waits for them, and re-layouts: 11.6 us -> none  [the longest x2 5.07 us: shards(): rev_y[elements][None]]
    mul x10 -> x0, other arithmetic: 8.17 us -> none  [the longest x2 2.32 us: shards(): res_second = live_two[None] * (pred_second - measured_second)]
where the time goes in v1:
time: 102 us; the launch traced here: 100 us
  Pallas kernels  90.3 us (89%)
  local copies, waits for them, and re-layouts  9.75 us (10%)
    pallas_call x1, Pallas kernels, shards(): pl.pallas_call(body, out_shape=jax.ShapeDtypeStruct(conc.shape, F32), in_...  90.3 us
    unnamed x19, local copies, waits for them, and re-layouts  9.75 us

profile of v1, /device:TPU:0, one launch (start us, length us, event | category | flops | bytes accessed | tf_op | source)
XLA Modules:
  0.0 100.0 jit_solution(13781542443640768177)
XLA Ops:
  0.0 0.0 copy-start
  0.0 0.7 copy-done
  0.7 0.0 copy-start.1
  0.7 0.7 copy-done.1
  1.5 0.0 copy-start.2
  1.5 0.7 copy-done.2
  2.2 0.0 copy-start.3
  2.2 0.7 copy-done.3
  2.9 0.0 copy-start.4
  2.9 0.7 copy-done.4
  3.6 0.0 copy-start.5
  3.6 0.7 copy-done.5
  4.2 0.0 copy-start.6
  4.2 0.7 copy-done.6
  4.9 0.0 copy-start.7
  4.9 0.7 copy-done.7
  5.6 0.0 copy-start.8
  5.6 0.7 copy-done.8
  6.2 90.3 %shard_map.100 = f32[10,4,128,128]{3,2,1,0:T(8,128)} custom-call(s32[2]{0:T(128)S(1)} %copy-done.7, f32[10,4,128,128]{3,2,1,0:T(8,128)} %refs_1_.1, f32[2,10]{1,0:T(2,128)S(1)} %copy-done.6, f32[12,10]{1,0:T(8,128)S(1)} %copy-done.2, f32[12,10]{1,0:T(8,128)S(1)} %copy-done.3, f32[1,10]{1,0:T(1,128)S(1)} %bitcast.1, f32[12,4,128]{2,1,0:T(4,128)S(1)} %copy-done, ...), custom_call_target="tpu_custom_call" | custom-call | tf_op jit(solution)/shard_map/pallas_call | solution.py:446
  96.5 3.5 %copy.12 = f32[10,4,128,128]{3,2,1,0:T(8,128)} copy(f32[10,4,128,128]{3,2,1,0:T(8,128)} %shard_map.100) | data formatting | bytes 5242880
Async XLA Ops:
  0.0 0.7 copy-start
  0.7 0.7 copy-start.1
  1.5 0.7 copy-start.2
  2.2 0.7 copy-start.3
  2.9 0.7 copy-start.4
  3.6 0.7 copy-start.5
  4.2 0.7 copy-start.6
  4.9 0.7 copy-start.7
  5.6 0.7 copy-start.8

commit v2 on v1

v2 whole, which is shorter than its diff:
```python
import math

import jax
import jax.numpy as jnp
from jax import lax
from jax.experimental import pallas as pl
from jax.experimental.pallas import tpu as pltpu
from jax.sharding import PartitionSpec as P

STEPS = 2
HIGH = lax.Precision.HIGHEST
MESH = pl.DeviceIdType.MESH
F32 = jnp.float32
BF16 = jnp.bfloat16
ELEMENTS = 10
LINES = 12
ZS = 4
N = 128
FIELDS = 26
LOG2E = math.log2(math.e)


def split(value):
    high = value.astype(BF16)
    return high, (value - high.astype(F32)).astype(BF16)


def iota(shape, dim):
    return lax.broadcasted_iota(jnp.int32, shape, dim)


def dot(a, b):
    return jnp.dot(a, b, preferred_element_type=F32)


def exact(a, b):
    return jnp.dot(a, b, preferred_element_type=F32, precision=HIGH)


def exact_nt(a, b):
    return lax.dot_general(
        a, b, (((1,), (1,)), ((), ())), preferred_element_type=F32, precision=HIGH
    )


def one_hot(condition):
    return jnp.where(condition, 1.0, 0.0).astype(F32)


def cum_cols(value, table):
    high, low = split(value)
    return dot(jnp.concatenate([high, low], 1), table)


def cum_rows(value, table):
    high, low = split(value)
    return dot(table, jnp.concatenate([high, low], 0))


class Ring:
    def __init__(self, axis, send, recv, back, done, sems):
        self.axis = axis
        self.count = recv.shape[2]
        self.me = lax.axis_index(axis)
        self.send, self.recv, self.back, self.done, self.sems = send, recv, back, done, sems
        self.tiles = self.count // ZS
        self.wide = 8 * self.tiles
        half = self.count // 2
        self.hops = sorted(range(1, self.count), key=lambda d: (abs(d - half), d))

    def peer(self, d):
        return lax.rem(self.me + d, self.count)

    def greet(self, barrier):
        for d in self.hops:
            pl.semaphore_signal(barrier, inc=1, device_id={self.axis: self.peer(d)}, device_id_type=MESH)

    def copy(self, src, dst, step, phase, leg, peer):
        return pltpu.make_async_remote_copy(
            src_ref=src,
            dst_ref=dst,
            send_sem=self.sems.at[step, phase, leg, 0],
            recv_sem=self.sems.at[step, phase, leg, 1],
            device_id={self.axis: peer},
            device_id_type=MESH,
        )

    def start(self, step, phase):
        mine = (step, phase, pl.ds(self.me, 1))
        self.recv[mine] = self.send[mine]
        for d in self.hops:
            peer = self.peer(d)
            src, dst = self.send.at[step, phase, peer], self.recv.at[step, phase, self.me]
            self.copy(src, dst, step, phase, 0, peer).start()

    def wait(self, src, dst, step, phase, leg):
        several = (step, phase, pl.ds(0, self.count - 1))
        whole = self.copy(src.at[several], dst.at[several], step, phase, leg, self.peer(1))
        whole.wait_send()
        whole.wait_recv()

    def middle(self, step, phase, mode):
        self.wait(self.send, self.recv, step, phase, 0)
        total = jnp.zeros((8, N), F32)
        order = range(self.count)
        for t in reversed(order) if mode == "later" else order:
            if mode != "sum":
                self.back[step, phase, t] = total
            total = total + self.recv[step, phase, t]
        mine = (step, phase, pl.ds(self.me, 1))
        if mode == "sum":
            self.back[step, phase, 0] = total
            self.done[mine] = total[None]
        else:
            self.done[mine] = self.back[mine]
        for d in self.hops:
            peer = self.peer(d)
            src = self.back.at[step, phase, 0 if mode == "sum" else peer]
            self.copy(src, self.done.at[step, phase, self.me], step, phase, 1, peer).start()

    def finish(self, step, phase):
        self.wait(self.back, self.done, step, phase, 1)

    def spot(self, z, row, of):
        per = -(-of // self.tiles)
        return self.wide * z + 8 * (row // per) + row % per

    def rows(self, ref, step, phase):
        return ref[step, phase].reshape(8 * self.count, N)

    def put(self, step, phase, spot, value):
        self.send[step, phase, spot // 8, spot % 8 : spot % 8 + 1, :] = value

    def put_all(self, step, phase, rows):
        self.send[step, phase] = rows.reshape(self.count, 8, N)


def kernel(
    step_x, step_y,
    axis_hbm, inc_hbm, sig_hbm, yld_hbm, rate_hbm, m1_hbm, live1_hbm, m2_hbm, live2_hbm, conc_hbm,
    out_hbm, dx_ref, dy_ref,
    axis_ref, inc_ref, sig_ref, yld_ref, rate_ref, m1_ref, live1_ref, m2_ref, live2_ref, c_ref,
    load_sems, conc_sems,
    f_ref, a1_ref, a2_ref, ex_ref, ey_ref, r1_ref, s2c_ref, mx_ref, my_ref, lx_ref, ly_ref,
    tx_ref, ty_ref, tab_ref, back_ref, mix_ref, unmix_ref, up_ref, down_ref, left_ref, right_ref,
    wax_ref, way_ref, wcx_ref, wcy_ref,
    bsend, brecv, bback, bdone, bsems, dsend, drecv, dback, ddone, dsems,
):
    conc_loads = [
        pltpu.make_async_copy(conc_hbm.at[:, z], c_ref.at[:, z], conc_sems.at[z]) for z in range(ZS)
    ]
    hbm = (axis_hbm, inc_hbm, sig_hbm, yld_hbm, rate_hbm, m1_hbm, live1_hbm, m2_hbm, live2_hbm)
    vmem = (axis_ref, inc_ref, sig_ref, yld_ref, rate_ref, m1_ref, live1_ref, m2_ref, live2_ref)
    loads = [pltpu.make_async_copy(a, b, load_sems.at[k]) for k, (a, b) in enumerate(zip(hbm, vmem))]
    for load in conc_loads + loads:
        load.start()
    beam = Ring("beam", bsend, brecv, bback, bdone, bsems)
    det = Ring("det", dsend, drecv, dback, ddone, dsems)
    barrier = pltpu.get_barrier_semaphore()
    det.greet(barrier)
    beam.greet(barrier)

    for ref in (bsend, dsend, mx_ref, my_ref, lx_ref, ly_ref, tx_ref, ty_ref, tab_ref, back_ref):
        ref[...] = jnp.zeros(ref.shape, F32)

    lane = iota((N, N), 1)

    def total(step, acc, z, e, c):
        beam.put(step, 0, beam.spot(z, e, ELEMENTS), jnp.sum(c, 0, keepdims=True))
        return jnp.where(lane == det.spot(z, e, ELEMENTS), jnp.sum(c, 1, keepdims=True), acc)

    def first_totals():
        acc = jnp.zeros((N, N), F32)
        for z in range(ZS):
            conc_loads[z].wait()
            for e in range(ELEMENTS):
                acc = total(0, acc, z, e, c_ref[e, z])
        det.put_all(0, 0, acc.T)

    first_totals()
    pl.semaphore_wait(barrier, beam.count + det.count - 2)
    det.start(0, 0)
    beam.start(0, 0)
    for load in loads:
        load.wait()

    def tables():
        first = axis_ref[0:1, 0:1] == 0
        one, two = inc_ref[0:1, :], inc_ref[1:2, :]
        s1 = jnp.where(first, one, two)
        s2 = jnp.where(first, two, one)
        scale = -LOG2E * step_y
        sig, yld, rate = sig_ref[...], yld_ref[...], rate_ref[...]
        cols = pl.ds(0, ELEMENTS)
        tab_ref[0:LINES, cols] = scale * sig
        tab_ref[LINES : LINES + 1, cols] = scale * s2
        tab_ref[LINES + 1 : LINES + 2, cols] = scale * s1
        tab_ref[LINES + 2 : FIELDS, cols] = yld
        back_ref[0:LINES, cols] = yld * rate
        back_ref[LINES : 2 * LINES, cols] = -sig * rate
        back_ref[2 * LINES : 2 * LINES + 1, cols] = -s1 * rate
        back_ref[2 * LINES + 1 : FIELDS, cols] = -s2 * rate

        tab, back = tab_ref[...], back_ref[...]
        wide = 8 * ELEMENTS
        pick = one_hot((iota((8 * FIELDS, 32), 0) >> 3) == iota((8 * FIELDS, 32), 1))
        col = iota((N, 256), 1)
        part = (col >= wide).astype(jnp.int32) + (col >= 2 * wide).astype(jnp.int32)
        spread = one_hot(((col - wide * part) >> 3) == iota((N, 256), 0))
        spread = jnp.where(col < 3 * wide, spread, 0.0)
        full = exact(pick, exact(tab, spread))
        shape = (8 * FIELDS, 256)
        full = jnp.where((iota(shape, 0) & 7) == (iota(shape, 1) & 7), full, 0.0)
        high, low = split(full)
        part = iota(shape, 1)
        mix_ref[...] = jnp.where((part >= wide) & (part < 2 * wide), low.astype(F32), high.astype(F32)).astype(BF16)

        pick = one_hot((iota((wide, N), 0) >> 3) == iota((wide, N), 1))
        shape = (wide, 8 * FIELDS)
        spread = one_hot((iota((32, 8 * FIELDS), 1) >> 3) == iota((32, 8 * FIELDS), 0))
        full = exact(exact_nt(pick, back), spread)
        full = jnp.where((iota(shape, 0) & 7) == (iota(shape, 1) & 7), full, 0.0)
        high, low = split(full)
        unmix_ref[0:wide] = high
        unmix_ref[wide : 2 * wide] = low

        r, m = iota((16 * ZS, 32), 0) & 15, iota((16 * ZS, 32), 1)
        rates = exact(one_hot((r == m) & (r < LINES + 2)), tab)
        sums_x = exact(one_hot(m == jnp.where(r < LINES, r + LINES, 2 * LINES)), back)
        sums_y = exact(one_hot(m == jnp.where(r < LINES, r + LINES, 2 * LINES + 1)), back)
        r = iota((16 * ZS, N), 0) & 15
        sums_x = jnp.where(r <= LINES, -step_x * sums_x, 0.0)
        sums_y = jnp.where(r <= LINES, -step_y * sums_y, 0.0)

        def place(ring):
            shape = (8 * ring.count, N)
            per = -(-ELEMENTS // ring.tiles)
            row = iota(shape, 0) & (ring.wide - 1)
            inside = row & 7
            return one_hot((inside < per) & ((row >> 3) * per + inside == iota(shape, 1)))

        def same(shape, rows, cols):
            shift = lambda n: n.bit_length() - 1
            return (iota(shape, 0) >> shift(rows)) == (iota(shape, 1) >> shift(cols))

        place_x, place_y = place(beam), place(det)
        wax_ref[...] = jnp.where(
            same(wax_ref.shape, 16, beam.wide), exact_nt(rates * (step_x / step_y), place_x), 0.0
        )
        way_ref[...] = jnp.where(same(way_ref.shape, 16, det.wide), exact_nt(rates, place_y), 0.0)
        wcx_ref[...] = jnp.where(same(wcx_ref.shape, beam.wide, 16), exact_nt(place_x, sums_x), 0.0)
        wcy_ref[...] = jnp.where(same(wcy_ref.shape, det.wide, 16), exact_nt(place_y, sums_y), 0.0)

        r, c = iota((2 * N, N), 0) & (N - 1), iota((2 * N, N), 1)
        up_ref[...] = one_hot(r < c).astype(BF16)
        down_ref[...] = (step_y * one_hot(r > c)).astype(BF16)
        r, c = iota((N, 2 * N), 0), iota((N, 2 * N), 1) & (N - 1)
        left_ref[...] = (step_x / step_y * one_hot(c < r)).astype(BF16)
        right_ref[...] = (step_x * one_hot(c > r)).astype(BF16)
        for z in range(ZS):
            live1 = live1_ref[z : z + 1, :].astype(F32)
            live2 = live2_ref[z : z + 1, :].astype(F32)
            for l in range(LINES):
                x, y = beam.spot(z, l, LINES), det.spot(z, l, LINES)
                lx_ref[x : x + 1, :] = live1
                ly_ref[y : y + 1, :] = live2
                mx_ref[x : x + 1, :] = m1_ref[l, z : z + 1, :]
                my_ref[y : y + 1, :] = m2_ref[l, z : z + 1, :]

    tables()

    def blocks(body):
        def one(n, carry):
            body(n // 4, pl.multiple_of((n % 4) * 32, 32))
            return carry

        lax.fori_loop(0, 4 * ZS, one, 0)

    def mix(z, r0):
        parts = []
        for b in range(4):
            high, low = split(c_ref[:, z, pl.ds(r0 + 8 * b, 8), :].reshape(8 * ELEMENTS, N))
            parts.append(jnp.concatenate([high, high, low, jnp.zeros((16, N), BF16)], 0))
        out = dot(mix_ref[...], jnp.concatenate(parts, 1))
        for b in range(4):
            f_ref[z, :, pl.ds(r0 + 8 * b, 8), :] = out[:, b * N : (b + 1) * N].reshape(FIELDS, 8, N)

    def unmix(z, r0):
        highs, lows = [], []
        for b in range(4):
            rows = pl.ds(r0 + 8 * b, 8)
            w = a1_ref[z, :, rows, :].reshape(8 * LINES, N)
            v = f_ref[z, 0 : LINES + 2, rows, :].reshape(8 * (LINES + 2), N)
            high, low = split(jnp.concatenate([w, v], 0))
            highs.append(high)
            lows.append(low)
        wide = 8 * ELEMENTS
        one = dot(unmix_ref[...], jnp.concatenate(highs, 1))
        two = dot(unmix_ref[0:wide], jnp.concatenate(lows, 1))
        out = one[0:wide] + (one[wide:] + two)
        for b in range(4):
            rows = pl.ds(r0 + 8 * b, 8)
            c_ref[:, z, rows, :] = c_ref[:, z, rows, :] - out[:, b * N : (b + 1) * N].reshape(ELEMENTS, 8, N)

    def attenuate(z, carry):
        tin1 = jnp.exp2(cum_rows(f_ref[z, LINES + 1], left_ref[...]))
        tin2 = jnp.exp2(cum_cols(f_ref[z, LINES], up_ref[...]))
        for l in range(0, LINES, 2):
            high0, low0 = split(f_ref[z, l])
            high1, low1 = split(f_ref[z, l + 1])
            across = jnp.concatenate(
                [jnp.concatenate([high0, low0], 1), jnp.concatenate([high1, low1], 1)], 0
            )
            along = jnp.concatenate(
                [jnp.concatenate([high0, high1], 1), jnp.concatenate([low0, low1], 1)], 0
            )
            over_y = jnp.exp2(dot(across, up_ref[...]))
            over_x = jnp.exp2(dot(left_ref[...], along))
            for k in range(2):
                a1_ref[z, l + k] = tin1 * over_y[k * N : (k + 1) * N]
                a2_ref[z, l + k] = tin2 * over_x[:, k * N : (k + 1) * N]
        return carry

    def times(rows, wide, factors, k):
        parts = [
            rows[wide * z : wide * (z + 1)] * factors[16 * z + k : 16 * z + k + 1] for z in range(ZS)
        ]
        return jnp.concatenate(parts, 0)

    def counts(step):
        ex = jnp.exp2(exact(wax_ref[...], beam.rows(bdone, step, 0)))
        ey = jnp.exp2(exact(way_ref[...], det.rows(ddone, step, 0)))
        ex_ref[...], ey_ref[...] = ex, ey
        cols = jnp.concatenate([ey, jnp.zeros((N - 16 * ZS, N), F32)], 0).T
        acc = jnp.zeros((N, N), F32)
        for z in range(ZS):
            enter = step_x * ex[16 * z + LINES + 1 : 16 * z + LINES + 2]
            for l in range(LINES):
                q = f_ref[z, LINES + 2 + l]
                k = 16 * z + l
                a1 = a1_ref[z, l] * cols[:, k : k + 1]
                a1_ref[z, l] = a1
                beam.put(step, 1, beam.spot(z, l, LINES), enter * jnp.sum(q * a1, 0, keepdims=True))
                seen = jnp.sum(q * (a2_ref[z, l] * ex[k : k + 1]), 1, keepdims=True)
                acc = jnp.where(lane == det.spot(z, l, LINES), seen, acc)
        det.put_all(step, 1, step_y * times(acc.T, det.wide, ey, LINES))

    def residuals(step):
        ex, ey = ex_ref[...], ey_ref[...]
        res1 = lx_ref[...] * (beam.rows(bdone, step, 1) - mx_ref[...])
        res2 = ly_ref[...] * (det.rows(ddone, step, 1) - my_ref[...])
        sum1 = res1 * beam.rows(bsend, step, 1) / step_x
        sum2 = res2 * det.rows(dsend, step, 1) / step_y
        r1 = times(res1, beam.wide, ex, LINES + 1)
        r1_ref[...] = r1
        cols = times(res2, det.wide, ey, LINES).T
        s2c_ref[...] = cols
        acc = jnp.zeros((N, N), F32)
        for z in range(ZS):
            for l in range(LINES):
                q = f_ref[z, LINES + 2 + l]
                k, x, y = 16 * z + l, beam.spot(z, l, LINES), det.spot(z, l, LINES)
                seen = jnp.sum(q * (a1_ref[z, l] * r1[x : x + 1]), 1, keepdims=True)
                acc = jnp.where(lane == k, seen, acc)
                seen = jnp.sum(q * (a2_ref[z, l] * cols[:, y : y + 1]), 0, keepdims=True)
                tx_ref[k : k + 1, :] = ex[k : k + 1] * seen
        ty_ref[...] = acc.T[0 : 16 * ZS]
        for z in range(ZS):
            k = 16 * z + LINES
            tx_ref[k : k + 1, :] = jnp.sum(sum1[beam.wide * z : beam.wide * (z + 1)], 0, keepdims=True)
            ty_ref[k : k + 1, :] = jnp.sum(sum2[det.wide * z : det.wide * (z + 1)], 0, keepdims=True)
        beam.put_all(step, 2, exact(wcx_ref[...], tx_ref[...]))
        det.put_all(step, 2, exact(wcy_ref[...], ty_ref[...]))

    def weights():
        ex, r1, cols = ex_ref[...], r1_ref[...], s2c_ref[...]
        for z in range(ZS):
            sum1 = jnp.zeros((N, N), F32)
            sum2 = jnp.zeros((N, N), F32)
            for l in range(LINES):
                q = f_ref[z, LINES + 2 + l]
                k, x, y = 16 * z + l, beam.spot(z, l, LINES), det.spot(z, l, LINES)
                w1 = a1_ref[z, l] * r1[x : x + 1]
                w2 = a2_ref[z, l] * ex[k : k + 1] * cols[:, y : y + 1]
                a1_ref[z, l] = w1 + w2
                p1, p2 = q * w1, q * w2
                sum1, sum2 = sum1 + p1, sum2 + p2
                f_ref[z, l] = cum_cols(p1, down_ref[...]) + cum_rows(p2, right_ref[...])
            f_ref[z, LINES] = cum_rows(sum1, right_ref[...])
            f_ref[z, LINES + 1] = cum_cols(sum2, down_ref[...])

    def update(step):
        cols = det.rows(ddone, step, 2).T
        rows = beam.rows(bdone, step, 2)
        acc = jnp.zeros((N, N), F32)
        for z in range(ZS):
            for e in range(ELEMENTS):
                x, y = beam.spot(z, e, ELEMENTS), det.spot(z, e, ELEMENTS)
                c = c_ref[e, z] + rows[x : x + 1] + cols[:, y : y + 1]
                c_ref[e, z] = c
                acc = total(step + 1, acc, z, e, c)
        det.put_all(step + 1, 0, acc.T)

    def turn(step, carry):
        last = step == STEPS - 1
        blocks(mix)
        det.middle(step, 0, "earlier")
        beam.middle(step, 0, "earlier")
        lax.fori_loop(0, ZS, attenuate, 0)
        det.finish(step, 0)
        beam.finish(step, 0)
        counts(step)
        det.start(step, 1)
        beam.start(step, 1)
        det.middle(step, 1, "sum")
        beam.middle(step, 1, "sum")
        det.finish(step, 1)
        beam.finish(step, 1)
        residuals(step)
        det.start(step, 2)
        beam.start(step, 2)
        weights()
        det.middle(step, 2, "later")
        beam.middle(step, 2, "later")
        blocks(unmix)

        @pl.when(last)
        def leave():
            stores = [
                pltpu.make_async_copy(c_ref.at[:, z], out_hbm.at[:, z], conc_sems.at[z]) for z in range(ZS)
            ]
            for store in stores:
                store.start()
            for store in stores:
                store.wait()

        det.finish(step, 2)
        beam.finish(step, 2)

        @pl.when(jnp.logical_not(last))
        def go_on():
            update(step)
            det.start(step + 1, 0)
            beam.start(step + 1, 0)

        return carry

    lax.fori_loop(0, STEPS, turn, 0)
    dx_ref[...] = bdone[STEPS - 1, 2]
    dy_ref[...] = ddone[STEPS - 1, 2]


def close(x_spots, y_spots, c_ref, dx_ref, dy_ref, out_ref):
    rows = dx_ref[...].reshape(-1, N)
    cols = dy_ref[...].reshape(-1, N)
    cols = jnp.concatenate([cols, jnp.zeros((N - cols.shape[0], N), F32)], 0).T
    for e in range(ELEMENTS):
        x, y = x_spots[e], y_spots[e]
        out_ref[e, 0] = c_ref[e, 0] + rows[x : x + 1] + cols[:, y : y + 1]


def solution(mesh):
    beams, dets = mesh.shape["beam"], mesh.shape["det"]

    def shards(conc, inc, sig, yld, rate, axis, m1, live1, m2, live2):
        step_x = 1.0 / (conc.shape[2] * beams)
        step_y = 1.0 / (conc.shape[3] * dets)

        def body(*refs):
            kernel(step_x, step_y, *refs)

        def exchange(count):
            tiles = pltpu.VMEM((STEPS, 3, count, 8, N), F32)
            return [tiles] * 4 + [pltpu.SemaphoreType.DMA((STEPS, 3, 2, 2))]

        def spots(tiles):
            per = -(-ELEMENTS // tiles)
            return [8 * (e // per) + e % per for e in range(ELEMENTS)]

        field = (N, N)
        anywhere = pl.BlockSpec(memory_space=pl.ANY)
        vmem = pl.BlockSpec(memory_space=pltpu.VMEM)
        small = (axis[None], inc, sig, yld, rate[None], m1, live1, m2, live2)
        inner, dx, dy = pl.pallas_call(
            body,
            out_shape=[
                jax.ShapeDtypeStruct(conc.shape, F32),
                jax.ShapeDtypeStruct((beams, 8, N), F32),
                jax.ShapeDtypeStruct((dets, 8, N), F32),
            ],
            in_specs=[anywhere] * (len(small) + 1),
            out_specs=[anywhere, vmem, vmem],
            scratch_shapes=[
                *[pltpu.VMEM(a.shape, a.dtype) for a in small + (conc,)],
                pltpu.SemaphoreType.DMA((len(small),)),
                pltpu.SemaphoreType.DMA((ZS,)),
                pltpu.VMEM((ZS, FIELDS) + field, F32),
                pltpu.VMEM((ZS, LINES) + field, F32),
                pltpu.VMEM((ZS, LINES) + field, F32),
                *[pltpu.VMEM((16 * ZS, N), F32)] * 2,
                pltpu.VMEM((8 * beams, N), F32),
                pltpu.VMEM(field, F32),
                pltpu.VMEM((8 * beams, N), F32),
                pltpu.VMEM((8 * dets, N), F32),
                pltpu.VMEM((8 * beams, N), F32),
                pltpu.VMEM((8 * dets, N), F32),
                *[pltpu.VMEM((16 * ZS, N), F32)] * 2,
                *[pltpu.VMEM((32, N), F32)] * 2,
                pltpu.VMEM((8 * FIELDS, 2 * N), BF16),
                pltpu.VMEM((16 * ELEMENTS, 8 * FIELDS), BF16),
                *[pltpu.VMEM((2 * N, N), BF16)] * 2,
                *[pltpu.VMEM((N, 2 * N), BF16)] * 2,
                pltpu.VMEM((16 * ZS, 8 * beams), F32),
                pltpu.VMEM((16 * ZS, 8 * dets), F32),
                pltpu.VMEM((8 * beams, 16 * ZS), F32),
                pltpu.VMEM((8 * dets, 16 * ZS), F32),
                *exchange(beams),
                *exchange(dets),
            ],
            compiler_params=pltpu.CompilerParams(
                collective_id=0, has_side_effects=True, vmem_limit_bytes=64 * 1024 * 1024
            ),
        )(*small, conc)

        x_tiles, y_tiles = beams // ZS, dets // ZS

        def last(*refs):
            close(spots(x_tiles), spots(y_tiles), *refs)

        block = pl.BlockSpec((ELEMENTS, 1, N, N), lambda z: (0, z, 0, 0))
        return pl.pallas_call(
            last,
            out_shape=jax.ShapeDtypeStruct(conc.shape, F32),
            grid=(ZS,),
            in_specs=[
                block,
                pl.BlockSpec((x_tiles, 8, N), lambda z: (z, 0, 0)),
                pl.BlockSpec((y_tiles, 8, N), lambda z: (z, 0, 0)),
            ],
            out_specs=block,
            compiler_params=pltpu.CompilerParams(vmem_limit_bytes=64 * 1024 * 1024),
        )(inner, dx, dy)

    in_specs = (
        P(None, None, "beam", "det"),
        P(),
        P(),
        P(),
        P(),
        P(),
        P(None, None, "det"),
        P(None, "det"),
        P(None, None, "beam"),
        P(None, "beam"),
    )
    out_specs = P(None, None, "beam", "det")
    return jax.shard_map(shards, mesh=mesh, in_specs=in_specs, out_specs=out_specs, check_vma=False)
```

time: 102 us -> 90 us (0.88)
  local copies, waits for them, and re-layouts: 9.75 us -> 0 us
  Pallas kernels: 90.3 us -> 89 us
    unnamed x19 -> x0, local copies, waits for them, and re-layouts: 9.75 us -> none
    pallas_call x1 -> x2, Pallas kernels: 90.3 us -> 89 us  [the longest x1 84.4 us: shards(): pl.pallas_call(body, out_shape=[jax.ShapeDtypeStruct(conc.shape, F32), ja...]
where the time goes in v2:
time: 90 us; the launch traced here: 89 us
  Pallas kernels  89 us (99%)
    pallas_call x1, Pallas kernels, shards(): pl.pallas_call(body, out_shape=[jax.ShapeDtypeStruct(conc.shape, F32), ja...  84.4 us
    pallas_call x1, Pallas kernels, shards(): pl.pallas_call(last, out_shape=jax.ShapeDtypeStruct(conc.shape, F32), gri...  4.64 us

profile of v2, /device:TPU:0, one launch (start us, length us, event | category | flops | bytes accessed | tf_op | source)
XLA Modules:
  0.0 89.0 jit_solution(1766700383994908402)
XLA Ops:
  0.0 84.4 %shard_map.100 = (f32[10,4,128,128]{3,2,1,0:T(8,128)}, f32[8,8,128]{2,1,0:T(8,128)}, f32[16,8,128]{2,1,0:T(8,128)}) custom-call(s32[1,2]{1,0:T(1,128)} %bitcast.2, f32[2,10]{1,0:T(2,128)} %refs_1_.1, f32[12,10]{1,0:T(8,128)} %refs_2_.1, f32[12,10]{1,0:T(8,128)} %refs_3_.1, f32[1,10]{1,0:T(1,128)} %bitcast.3, f32[12,4,128]{2,1,0:T(4,128)} %refs_5_.1, ...), custom_call_target="tpu_custom_call" | custom-call | tf_op jit(solution)/shard_map/pallas_call | solution.py:484
  84.4 4.6 %shard_map.101 = f32[10,4,128,128]{3,2,1,0:T(8,128)} custom-call(f32[10,4,128,128]{3,2,1,0:T(8,128)} %get-tuple-element.8.refs_0_, f32[8,8,128]{2,1,0:T(8,128)} %get-tuple-element.9.refs_1_, f32[16,8,128]{2,1,0:T(8,128)} %get-tuple-element.10.refs_2_), custom_call_target="tpu_custom_call" | custom-call | tf_op jit(solution)/shard_map/pallas_call | solution.py:531

commit v3 on v2

--- a/solution.py
+++ b/solution.py
@@ -270,11 +270,12 @@
     tables()
 
     def blocks(body):
-        def one(n, carry):
-            body(n // 4, pl.multiple_of((n % 4) * 32, 32))
+        def one(z, carry):
+            for r0 in range(0, N, 32):
+                body(z, r0)
             return carry
 
-        lax.fori_loop(0, 4 * ZS, one, 0)
+        lax.fori_loop(0, ZS, one, 0)
 
     def mix(z, r0):
         parts = []

time: 90 us -> 88.3 us (0.981)
  Pallas kernels: 89 us -> 87.3 us
    pallas_call x1, Pallas kernels: 84.4 us -> 82.6 us  [shards(): pl.pallas_call(body, out_shape=[jax.ShapeDtypeStruct(conc.shape, F32), ja...]
where the time goes in v3:
time: 88.3 us; the launch traced here: 87.3 us
  Pallas kernels  87.3 us (99%)
    pallas_call x1, Pallas kernels, shards(): pl.pallas_call(body, out_shape=[jax.ShapeDtypeStruct(conc.shape, F32), ja...  82.6 us
    pallas_call x1, Pallas kernels, shards(): pl.pallas_call(last, out_shape=jax.ShapeDtypeStruct(conc.shape, F32), gri...  4.64 us

profile of v3, /device:TPU:0, one launch (start us, length us, event | category | flops | bytes accessed | tf_op | source)
XLA Modules:
  0.0 87.3 jit_solution(11830971209041859084)
XLA Ops:
  0.0 82.6 %shard_map.100 = (f32[10,4,128,128]{3,2,1,0:T(8,128)}, f32[8,8,128]{2,1,0:T(8,128)}, f32[16,8,128]{2,1,0:T(8,128)}) custom-call(s32[1,2]{1,0:T(1,128)} %bitcast.2, f32[2,10]{1,0:T(2,128)} %refs_1_.1, f32[12,10]{1,0:T(8,128)} %refs_2_.1, f32[12,10]{1,0:T(8,128)} %refs_3_.1, f32[1,10]{1,0:T(1,128)} %bitcast.3, f32[12,4,128]{2,1,0:T(4,128)} %refs_5_.1, ...), custom_call_target="tpu_custom_call" | custom-call | tf_op jit(solution)/shard_map/pallas_call | solution.py:485
  82.6 4.6 %shard_map.101 = f32[10,4,128,128]{3,2,1,0:T(8,128)} custom-call(f32[10,4,128,128]{3,2,1,0:T(8,128)} %get-tuple-element.8.refs_0_, f32[8,8,128]{2,1,0:T(8,128)} %get-tuple-element.9.refs_1_, f32[16,8,128]{2,1,0:T(8,128)} %get-tuple-element.10.refs_2_), custom_call_target="tpu_custom_call" | custom-call | tf_op jit(solution)/shard_map/pallas_call | solution.py:532

commit v4 on v3

--- a/solution.py
+++ b/solution.py
@@ -17,6 +17,8 @@
 ZS = 4
 N = 128
 FIELDS = 26
+GROUPS = 2
+PER = ZS // GROUPS
 LOG2E = math.log2(math.e)
 
 
@@ -65,74 +67,98 @@
         self.send, self.recv, self.back, self.done, self.sems = send, recv, back, done, sems
         self.tiles = self.count // ZS
         self.wide = 8 * self.tiles
+        self.run = self.count // GROUPS
         half = self.count // 2
         self.hops = sorted(range(1, self.count), key=lambda d: (abs(d - half), d))
 
     def peer(self, d):
         return lax.rem(self.me + d, self.count)
+
+    def owns(self, g):
+        return (self.me >= g * self.run) & (self.me < (g + 1) * self.run)
 
     def greet(self, barrier):
         for d in self.hops:
             pl.semaphore_signal(barrier, inc=1, device_id={self.axis: self.peer(d)}, device_id_type=MESH)
 
-    def copy(self, src, dst, step, phase, leg, peer):
+    def copy(self, src, dst, step, phase, out, into, peer):
         return pltpu.make_async_remote_copy(
             src_ref=src,
             dst_ref=dst,
-            send_sem=self.sems.at[step, phase, leg, 0],
-            recv_sem=self.sems.at[step, phase, leg, 1],
+            send_sem=self.sems.at[step, phase, out],
+            recv_sem=self.sems.at[step, phase, into],
             device_id={self.axis: peer},
             device_id_type=MESH,
         )
 
-    def start(self, step, phase):
-        mine = (step, phase, pl.ds(self.me, 1))
-        self.recv[mine] = self.send[mine]
-        for d in self.hops:
-            peer = self.peer(d)
-            src, dst = self.send.at[step, phase, peer], self.recv.at[step, phase, self.me]
-            self.copy(src, dst, step, phase, 0, peer).start()
-
-    def wait(self, src, dst, step, phase, leg):
-        several = (step, phase, pl.ds(0, self.count - 1))
-        whole = self.copy(src.at[several], dst.at[several], step, phase, leg, self.peer(1))
-        whole.wait_send()
-        whole.wait_recv()
-
-    def middle(self, step, phase, mode):
-        self.wait(self.send, self.recv, step, phase, 0)
-        total = jnp.zeros((8, N), F32)
-        order = range(self.count)
-        for t in reversed(order) if mode == "later" else order:
-            if mode != "sum":
-                self.back[step, phase, t] = total
-            total = total + self.recv[step, phase, t]
-        mine = (step, phase, pl.ds(self.me, 1))
-        if mode == "sum":
-            self.back[step, phase, 0] = total
-            self.done[mine] = total[None]
-        else:
-            self.done[mine] = self.back[mine]
-        for d in self.hops:
-            peer = self.peer(d)
-            src = self.back.at[step, phase, 0 if mode == "sum" else peer]
-            self.copy(src, self.done.at[step, phase, self.me], step, phase, 1, peer).start()
-
-    def finish(self, step, phase):
-        self.wait(self.back, self.done, step, phase, 1)
+    def whole(self, src, dst, step, phase, out, into, tiles):
+        some = (step, phase, pl.ds(0, tiles))
+        return self.copy(src.at[some], dst.at[some], step, phase, out, into, self.peer(1))
+
+    def start(self, step, phase, g):
+        def one(d):
+            owner = g * self.run + lax.rem(self.me + d, self.run)
+            src, dst = self.send.at[step, phase, owner], self.recv.at[step, phase, self.me]
+            self.copy(src, dst, step, phase, 0, 1, owner).start()
+
+        @pl.when(self.owns(g))
+        def keep():
+            mine = (step, phase, pl.ds(self.me, 1))
+            self.recv[mine] = self.send[mine]
+
+        @pl.when(jnp.logical_not(self.owns(g)))
+        def first():
+            one(0)
+
+        for d in range(1, self.run):
+            one(d)
+
+    def middle(self, step, phase, g, mode):
+        @pl.when(self.owns(g))
+        def owner():
+            self.whole(self.send, self.recv, step, phase, 0, 1, self.count - 1).wait_recv()
+            total = jnp.zeros((8, N), F32)
+            order = range(self.count)
+            for t in reversed(order) if mode == "later" else order:
+                if mode != "sum":
+                    self.back[step, phase, t] = total
+                total = total + self.recv[step, phase, t]
+            mine = (step, phase, pl.ds(self.me, 1))
+            if mode == "sum":
+                self.back[step, phase, 0] = total
+                self.done[mine] = total[None]
+            else:
+                self.done[mine] = self.back[mine]
+            for d in self.hops:
+                peer = self.peer(d)
+                src = self.back.at[step, phase, 0 if mode == "sum" else peer]
+                self.copy(src, self.done.at[step, phase, self.me], step, phase, 2, 3 + g, peer).start()
+
+    def finish(self, step, phase, g):
+        @pl.when(self.owns(g))
+        def others():
+            self.whole(self.back, self.done, step, phase, 2, 3 + g, self.run - 1).wait_recv()
+
+        @pl.when(jnp.logical_not(self.owns(g)))
+        def all_of_them():
+            self.whole(self.back, self.done, step, phase, 2, 3 + g, self.run).wait_recv()
+
+    def settle(self, step, phase):
+        self.whole(self.send, self.recv, step, phase, 0, 1, self.count - 1).wait_send()
+        self.whole(self.back, self.done, step, phase, 2, 3, self.count - 1).wait_send()
 
     def spot(self, z, row, of):
         per = -(-of // self.tiles)
-        return self.wide * z + 8 * (row // per) + row % per
-
-    def rows(self, ref, step, phase):
-        return ref[step, phase].reshape(8 * self.count, N)
-
-    def put(self, step, phase, spot, value):
-        self.send[step, phase, spot // 8, spot % 8 : spot % 8 + 1, :] = value
-
-    def put_all(self, step, phase, rows):
-        self.send[step, phase] = rows.reshape(self.count, 8, N)
+        return self.wide * (z % PER) + 8 * (row // per) + row % per
+
+    def rows(self, ref, step, phase, g):
+        return ref[step, phase, g * self.run : (g + 1) * self.run].reshape(8 * self.run, N)
+
+    def put(self, step, phase, g, spot, value):
+        self.send[step, phase, g * self.run + spot // 8, spot % 8 : spot % 8 + 1, :] = value
+
+    def put_all(self, step, phase, g, rows):
+        self.send[step, phase, g * self.run : (g + 1) * self.run] = rows.reshape(self.run, 8, N)
 
 
 def kernel(
@@ -165,22 +191,38 @@
 
     lane = iota((N, N), 1)
 
+    def members(g):
+        return range(g * PER, (g + 1) * PER)
+
+    def send_off(step, phase, g):
+        det.start(step, phase, g)
+        beam.start(step, phase, g)
+
+    def pass_on(step, phase, g, mode):
+        det.middle(step, phase, g, mode)
+        beam.middle(step, phase, g, mode)
+
+    def take(step, phase, g):
+        det.finish(step, phase, g)
+        beam.finish(step, phase, g)
+
     def total(step, acc, z, e, c):
-        beam.put(step, 0, beam.spot(z, e, ELEMENTS), jnp.sum(c, 0, keepdims=True))
+        beam.put(step, 0, z // PER, beam.spot(z, e, ELEMENTS), jnp.sum(c, 0, keepdims=True))
         return jnp.where(lane == det.spot(z, e, ELEMENTS), jnp.sum(c, 1, keepdims=True), acc)
 
-    def first_totals():
+    def first_totals(g):
         acc = jnp.zeros((N, N), F32)
-        for z in range(ZS):
+        for z in members(g):
             conc_loads[z].wait()
             for e in range(ELEMENTS):
                 acc = total(0, acc, z, e, c_ref[e, z])
-        det.put_all(0, 0, acc.T)
-
-    first_totals()
+        det.put_all(0, 0, g, acc.T[0 : det.wide * PER])
+
+    first_totals(0)
     pl.semaphore_wait(barrier, beam.count + det.count - 2)
-    det.start(0, 0)
-    beam.start(0, 0)
+    send_off(0, 0, 0)
+    first_totals(1)
+    send_off(0, 0, 1)
     for load in loads:
         load.wait()
 
@@ -224,16 +266,16 @@
         unmix_ref[0:wide] = high
         unmix_ref[wide : 2 * wide] = low
 
-        r, m = iota((16 * ZS, 32), 0) & 15, iota((16 * ZS, 32), 1)
+        r, m = iota((16 * PER, 32), 0) & 15, iota((16 * PER, 32), 1)
         rates = exact(one_hot((r == m) & (r < LINES + 2)), tab)
         sums_x = exact(one_hot(m == jnp.where(r < LINES, r + LINES, 2 * LINES)), back)
         sums_y = exact(one_hot(m == jnp.where(r < LINES, r + LINES, 2 * LINES + 1)), back)
-        r = iota((16 * ZS, N), 0) & 15
+        r = iota((16 * PER, N), 0) & 15
         sums_x = jnp.where(r <= LINES, -step_x * sums_x, 0.0)
         sums_y = jnp.where(r <= LINES, -step_y * sums_y, 0.0)
 
         def place(ring):
-            shape = (8 * ring.count, N)
+            shape = (8 * ring.run, N)
             per = -(-ELEMENTS // ring.tiles)
             row = iota(shape, 0) & (ring.wide - 1)
             inside = row & 7
@@ -261,21 +303,22 @@
             live1 = live1_ref[z : z + 1, :].astype(F32)
             live2 = live2_ref[z : z + 1, :].astype(F32)
             for l in range(LINES):
-                x, y = beam.spot(z, l, LINES), det.spot(z, l, LINES)
-                lx_ref[x : x + 1, :] = live1
-                ly_ref[y : y + 1, :] = live2
-                mx_ref[x : x + 1, :] = m1_ref[l, z : z + 1, :]
-                my_ref[y : y + 1, :] = m2_ref[l, z : z + 1, :]
+                g, x, y = z // PER, beam.spot(z, l, LINES), det.spot(z, l, LINES)
+                lx_ref[g, x : x + 1, :] = live1
+                ly_ref[g, y : y + 1, :] = live2
+                mx_ref[g, x : x + 1, :] = m1_ref[l, z : z + 1, :]
+                my_ref[g, y : y + 1, :] = m2_ref[l, z : z + 1, :]
 
     tables()
-
-    def blocks(body):
+    pass_on(0, 0, 0, "earlier")
+
+    def blocks(g, body):
         def one(z, carry):
             for r0 in range(0, N, 32):
                 body(z, r0)
             return carry
 
-        lax.fori_loop(0, ZS, one, 0)
+        lax.fori_loop(g * PER, (g + 1) * PER, one, 0)
 
     def mix(z, r0):
         parts = []
@@ -324,126 +367,155 @@
 
     def times(rows, wide, factors, k):
         parts = [
-            rows[wide * z : wide * (z + 1)] * factors[16 * z + k : 16 * z + k + 1] for z in range(ZS)
+            rows[wide * z : wide * (z + 1)] * factors[16 * z + k : 16 * z + k + 1] for z in range(PER)
         ]
         return jnp.concatenate(parts, 0)
 
-    def counts(step):
-        ex = jnp.exp2(exact(wax_ref[...], beam.rows(bdone, step, 0)))
-        ey = jnp.exp2(exact(way_ref[...], det.rows(ddone, step, 0)))
-        ex_ref[...], ey_ref[...] = ex, ey
-        cols = jnp.concatenate([ey, jnp.zeros((N - 16 * ZS, N), F32)], 0).T
+    def counts(step, g):
+        ex = jnp.exp2(exact(wax_ref[...], beam.rows(bdone, step, 0, g)))
+        ey = jnp.exp2(exact(way_ref[...], det.rows(ddone, step, 0, g)))
+        ex_ref[g], ey_ref[g] = ex, ey
+        cols = jnp.concatenate([ey, jnp.zeros((N - 16 * PER, N), F32)], 0).T
         acc = jnp.zeros((N, N), F32)
-        for z in range(ZS):
-            enter = step_x * ex[16 * z + LINES + 1 : 16 * z + LINES + 2]
+        for z in members(g):
+            k = 16 * (z % PER) + LINES + 1
+            enter = step_x * ex[k : k + 1]
             for l in range(LINES):
                 q = f_ref[z, LINES + 2 + l]
-                k = 16 * z + l
+                k = 16 * (z % PER) + l
                 a1 = a1_ref[z, l] * cols[:, k : k + 1]
                 a1_ref[z, l] = a1
-                beam.put(step, 1, beam.spot(z, l, LINES), enter * jnp.sum(q * a1, 0, keepdims=True))
+                beam.put(step, 1, g, beam.spot(z, l, LINES), enter * jnp.sum(q * a1, 0, keepdims=True))
                 seen = jnp.sum(q * (a2_ref[z, l] * ex[k : k + 1]), 1, keepdims=True)
                 acc = jnp.where(lane == det.spot(z, l, LINES), seen, acc)
-        det.put_all(step, 1, step_y * times(acc.T, det.wide, ey, LINES))
-
-    def residuals(step):
-        ex, ey = ex_ref[...], ey_ref[...]
-        res1 = lx_ref[...] * (beam.rows(bdone, step, 1) - mx_ref[...])
-        res2 = ly_ref[...] * (det.rows(ddone, step, 1) - my_ref[...])
-        sum1 = res1 * beam.rows(bsend, step, 1) / step_x
-        sum2 = res2 * det.rows(dsend, step, 1) / step_y
+        det.put_all(step, 1, g, step_y * times(acc.T, det.wide, ey, LINES))
+
+    def residuals(step, g):
+        ex, ey = ex_ref[g], ey_ref[g]
+        res1 = lx_ref[g] * (beam.rows(bdone, step, 1, g) - mx_ref[g])
+        res2 = ly_ref[g] * (det.rows(ddone, step, 1, g) - my_ref[g])
+        sum1 = res1 * beam.rows(bsend, step, 1, g) / step_x
+        sum2 = res2 * det.rows(dsend, step, 1, g) / step_y
         r1 = times(res1, beam.wide, ex, LINES + 1)
-        r1_ref[...] = r1
-        cols = times(res2, det.wide, ey, LINES).T
-        s2c_ref[...] = cols
+        r1_ref[g] = r1
+        cols = jnp.concatenate([times(res2, det.wide, ey, LINES), jnp.zeros((N - det.wide * PER, N), F32)], 0).T
+        s2c_ref[g] = cols
         acc = jnp.zeros((N, N), F32)
-        for z in range(ZS):
+        for z in members(g):
             for l in range(LINES):
                 q = f_ref[z, LINES + 2 + l]
-                k, x, y = 16 * z + l, beam.spot(z, l, LINES), det.spot(z, l, LINES)
+                k, x, y = 16 * (z % PER) + l, beam.spot(z, l, LINES), det.spot(z, l, LINES)
                 seen = jnp.sum(q * (a1_ref[z, l] * r1[x : x + 1]), 1, keepdims=True)
                 acc = jnp.where(lane == k, seen, acc)
                 seen = jnp.sum(q * (a2_ref[z, l] * cols[:, y : y + 1]), 0, keepdims=True)
-                tx_ref[k : k + 1, :] = ex[k : k + 1] * seen
-        ty_ref[...] = acc.T[0 : 16 * ZS]
-        for z in range(ZS):
+                tx_ref[g, k : k + 1, :] = ex[k : k + 1] * seen
+        ty_ref[g] = acc.T[0 : 16 * PER]
+        for z in range(PER):
             k = 16 * z + LINES
-            tx_ref[k : k + 1, :] = jnp.sum(sum1[beam.wide * z : beam.wide * (z + 1)], 0, keepdims=True)
-            ty_ref[k : k + 1, :] = jnp.sum(sum2[det.wide * z : det.wide * (z + 1)], 0, keepdims=True)
-        beam.put_all(step, 2, exact(wcx_ref[...], tx_ref[...]))
-        det.put_all(step, 2, exact(wcy_ref[...], ty_ref[...]))
-
-    def weights():
-        ex, r1, cols = ex_ref[...], r1_ref[...], s2c_ref[...]
-        for z in range(ZS):
-            sum1 = jnp.zeros((N, N), F32)
-            sum2 = jnp.zeros((N, N), F32)
-            for l in range(LINES):
-                q = f_ref[z, LINES + 2 + l]
-                k, x, y = 16 * z + l, beam.spot(z, l, LINES), det.spot(z, l, LINES)
-                w1 = a1_ref[z, l] * r1[x : x + 1]
-                w2 = a2_ref[z, l] * ex[k : k + 1] * cols[:, y : y + 1]
-                a1_ref[z, l] = w1 + w2
-                p1, p2 = q * w1, q * w2
-                sum1, sum2 = sum1 + p1, sum2 + p2
-                f_ref[z, l] = cum_cols(p1, down_ref[...]) + cum_rows(p2, right_ref[...])
-            f_ref[z, LINES] = cum_rows(sum1, right_ref[...])
-            f_ref[z, LINES + 1] = cum_cols(sum2, down_ref[...])
-
-    def update(step):
-        cols = det.rows(ddone, step, 2).T
-        rows = beam.rows(bdone, step, 2)
+            tx_ref[g, k : k + 1, :] = jnp.sum(sum1[beam.wide * z : beam.wide * (z + 1)], 0, keepdims=True)
+            ty_ref[g, k : k + 1, :] = jnp.sum(sum2[det.wide * z : det.wide * (z + 1)], 0, keepdims=True)
+        beam.put_all(step, 2, g, exact(wcx_ref[...], tx_ref[g]))
+        det.put_all(step, 2, g, exact(wcy_ref[...], ty_ref[g]))
+
+    def weights(z):
+        g = z // PER
+        ex, r1, cols = ex_ref[g], r1_ref[g], s2c_ref[g]
+        sum1 = jnp.zeros((N, N), F32)
+        sum2 = jnp.zeros((N, N), F32)
+        for l in range(LINES):
+            q = f_ref[z, LINES + 2 + l]
+            k, x, y = 16 * (z % PER) + l, beam.spot(z, l, LINES), det.spot(z, l, LINES)
+            w1 = a1_ref[z, l] * r1[x : x + 1]
+            w2 = a2_ref[z, l] * ex[k : k + 1] * cols[:, y : y + 1]
+            a1_ref[z, l] = w1 + w2
+            p1, p2 = q * w1, q * w2
+            sum1, sum2 = sum1 + p1, sum2 + p2
+            f_ref[z, l] = cum_cols(p1, down_ref[...]) + cum_rows(p2, right_ref[...])
+        f_ref[z, LINES] = cum_rows(sum1, right_ref[...])
+        f_ref[z, LINES + 1] = cum_cols(sum2, down_ref[...])
+
+    def update(step, g):
+        cols = det.rows(ddone, step, 2, g)
+        cols = jnp.concatenate([cols, jnp.zeros((N - cols.shape[0], N), F32)], 0).T
+        rows = beam.rows(bdone, step, 2, g)
         acc = jnp.zeros((N, N), F32)
-        for z in range(ZS):
+        for z in members(g):
             for e in range(ELEMENTS):
                 x, y = beam.spot(z, e, ELEMENTS), det.spot(z, e, ELEMENTS)
                 c = c_ref[e, z] + rows[x : x + 1] + cols[:, y : y + 1]
                 c_ref[e, z] = c
                 acc = total(step + 1, acc, z, e, c)
-        det.put_all(step + 1, 0, acc.T)
+        det.put_all(step + 1, 0, g, acc.T[0 : det.wide * PER])
+
+    def leave(g):
+        stores = [pltpu.make_async_copy(c_ref.at[:, z], out_hbm.at[:, z], conc_sems.at[z]) for z in members(g)]
+        return stores
 
     def turn(step, carry):
         last = step == STEPS - 1
-        blocks(mix)
-        det.middle(step, 0, "earlier")
-        beam.middle(step, 0, "earlier")
-        lax.fori_loop(0, ZS, attenuate, 0)
-        det.finish(step, 0)
-        beam.finish(step, 0)
-        counts(step)
-        det.start(step, 1)
-        beam.start(step, 1)
-        det.middle(step, 1, "sum")
-        beam.middle(step, 1, "sum")
-        det.finish(step, 1)
-        beam.finish(step, 1)
-        residuals(step)
-        det.start(step, 2)
-        beam.start(step, 2)
-        weights()
-        det.middle(step, 2, "later")
-        beam.middle(step, 2, "later")
-        blocks(unmix)
+        more = jnp.logical_not(last)
+        blocks(0, mix)
+        pass_on(step, 0, 1, "earlier")
+        lax.fori_loop(0, PER, attenuate, 0)
+        take(step, 0, 0)
+        counts(step, 0)
+        send_off(step, 1, 0)
+        blocks(1, mix)
+        pass_on(step, 1, 0, "sum")
+        lax.fori_loop(PER, ZS, attenuate, 0)
+        take(step, 0, 1)
+        counts(step, 1)
+        send_off(step, 1, 1)
+        take(step, 1, 0)
+        residuals(step, 0)
+        send_off(step, 2, 0)
+        weights(0)
+        pass_on(step, 1, 1, "sum")
+        weights(1)
+        pass_on(step, 2, 0, "later")
+        take(step, 1, 1)
+        residuals(step, 1)
+        send_off(step, 2, 1)
+        blocks(0, unmix)
 
         @pl.when(last)
-        def leave():
-            stores = [
-                pltpu.make_async_copy(c_ref.at[:, z], out_hbm.at[:, z], conc_sems.at[z]) for z in range(ZS)
-            ]
-            for store in stores:
+        def part():
+            for store in leave(0):
                 store.start()
-            for store in stores:
+
+        take(step, 2, 0)
+
+        @pl.when(more)
+        def again():
+            update(step, 0)
+            send_off(step + 1, 0, 0)
+
+        weights(2)
+        pass_on(step, 2, 1, "later")
+        weights(3)
+
+        @pl.when(more)
+        def early():
+            pass_on(step + 1, 0, 0, "earlier")
+
+        blocks(1, unmix)
+        take(step, 2, 1)
+
+        @pl.when(more)
+        def once_more():
+            update(step, 1)
+            send_off(step + 1, 0, 1)
+
+        @pl.when(last)
+        def finish():
+            for store in leave(1):
+                store.start()
+            for store in leave(0) + leave(1):
                 store.wait()
 
-        det.finish(step, 2)
-        beam.finish(step, 2)
-
-        @pl.when(jnp.logical_not(last))
-        def go_on():
-            update(step)
-            det.start(step + 1, 0)
-            beam.start(step + 1, 0)
-
+        for phase in range(3):
+            det.settle(step, phase)
+            beam.settle(step, phase)
         return carry
 
     lax.fori_loop(0, STEPS, turn, 0)
@@ -472,7 +544,10 @@
 
         def exchange(count):
             tiles = pltpu.VMEM((STEPS, 3, count, 8, N), F32)
-            return [tiles] * 4 + [pltpu.SemaphoreType.DMA((STEPS, 3, 2, 2))]
+            return [tiles] * 4 + [pltpu.SemaphoreType.DMA((STEPS, 3, 3 + GROUPS))]
+
+        def per_group(rows):
+            return pltpu.VMEM((GROUPS, rows, N), F32)
 
         def spots(tiles):
             per = -(-ELEMENTS // tiles)
@@ -498,23 +573,23 @@
                 pltpu.VMEM((ZS, FIELDS) + field, F32),
                 pltpu.VMEM((ZS, LINES) + field, F32),
                 pltpu.VMEM((ZS, LINES) + field, F32),
-                *[pltpu.VMEM((16 * ZS, N), F32)] * 2,
-                pltpu.VMEM((8 * beams, N), F32),
-                pltpu.VMEM(field, F32),
-                pltpu.VMEM((8 * beams, N), F32),
-                pltpu.VMEM((8 * dets, N), F32),
-                pltpu.VMEM((8 * beams, N), F32),
-                pltpu.VMEM((8 * dets, N), F32),
-                *[pltpu.VMEM((16 * ZS, N), F32)] * 2,
+                *[per_group(16 * PER)] * 2,
+                per_group(8 * beams // GROUPS),
+                per_group(N),
+                per_group(8 * beams // GROUPS),
+                per_group(8 * dets // GROUPS),
+                per_group(8 * beams // GROUPS),
+                per_group(8 * dets // GROUPS),
+                *[per_group(16 * PER)] * 2,
                 *[pltpu.VMEM((32, N), F32)] * 2,
                 pltpu.VMEM((8 * FIELDS, 2 * N), BF16),
                 pltpu.VMEM((16 * ELEMENTS, 8 * FIELDS), BF16),
                 *[pltpu.VMEM((2 * N, N), BF16)] * 2,
                 *[pltpu.VMEM((N, 2 * N), BF16)] * 2,
-                pltpu.VMEM((16 * ZS, 8 * beams), F32),
-                pltpu.VMEM((16 * ZS, 8 * dets), F32),
-                pltpu.VMEM((8 * beams, 16 * ZS), F32),
-                pltpu.VMEM((8 * dets, 16 * ZS), F32),
+                pltpu.VMEM((16 * PER, 8 * beams // GROUPS), F32),
+                pltpu.VMEM((16 * PER, 8 * dets // GROUPS), F32),
+                pltpu.VMEM((8 * beams // GROUPS, 16 * PER), F32),
+                pltpu.VMEM((8 * dets // GROUPS, 16 * PER), F32),
                 *exchange(beams),
                 *exchange(dets),
             ],

time: 88.3 us -> 94.1 us (1.066)
  Pallas kernels: 87.3 us -> 93.2 us
    pallas_call x1, Pallas kernels: 82.6 us -> 88.6 us  [shards(): pl.pallas_call(body, out_shape=[jax.ShapeDtypeStruct(conc.shape, F32), ja...]
where the time goes in v4:
time: 94.1 us; the launch traced here: 93.2 us
  Pallas kernels  93.2 us (99%)
    pallas_call x1, Pallas kernels, shards(): pl.pallas_call(body, out_shape=[jax.ShapeDtypeStruct(conc.shape, F32), ja...  88.6 us
    pallas_call x1, Pallas kernels, shards(): pl.pallas_call(last, out_shape=jax.ShapeDtypeStruct(conc.shape, F32), gri...  4.64 us

profile of v4, /device:TPU:0, one launch (start us, length us, event | category | flops | bytes accessed | tf_op | source)
XLA Modules:
  0.0 93.2 jit_solution(17339826910888302092)
XLA Ops:
  0.0 88.6 %shard_map.100 = (f32[10,4,128,128]{3,2,1,0:T(8,128)}, f32[8,8,128]{2,1,0:T(8,128)}, f32[16,8,128]{2,1,0:T(8,128)}) custom-call(s32[1,2]{1,0:T(1,128)} %bitcast.2, f32[2,10]{1,0:T(2,128)} %refs_1_.1, f32[12,10]{1,0:T(8,128)} %refs_2_.1, f32[12,10]{1,0:T(8,128)} %refs_3_.1, f32[1,10]{1,0:T(1,128)} %bitcast.3, f32[12,4,128]{2,1,0:T(4,128)} %refs_5_.1, ...), custom_call_target="tpu_custom_call" | custom-call | tf_op jit(solution)/shard_map/pallas_call | solution.py:560
  88.6 4.6 %shard_map.101 = f32[10,4,128,128]{3,2,1,0:T(8,128)} custom-call(f32[10,4,128,128]{3,2,1,0:T(8,128)} %get-tuple-element.8.refs_0_, f32[8,8,128]{2,1,0:T(8,128)} %get-tuple-element.9.refs_1_, f32[16,8,128]{2,1,0:T(8,128)} %get-tuple-element.10.refs_2_), custom_call_target="tpu_custom_call" | custom-call | tf_op jit(solution)/shard_map/pallas_call | solution.py:607

commit v5 on v2

--- a/solution.py
+++ b/solution.py
@@ -17,6 +17,7 @@
 ZS = 4
 N = 128
 FIELDS = 26
+CHUNK = 32
 LOG2E = math.log2(math.e)
 
 
@@ -45,16 +46,6 @@
 
 def one_hot(condition):
     return jnp.where(condition, 1.0, 0.0).astype(F32)
-
-
-def cum_cols(value, table):
-    high, low = split(value)
-    return dot(jnp.concatenate([high, low], 1), table)
-
-
-def cum_rows(value, table):
-    high, low = split(value)
-    return dot(table, jnp.concatenate([high, low], 0))
 
 
 class Ring:
@@ -121,15 +112,18 @@
     def finish(self, step, phase):
         self.wait(self.back, self.done, step, phase, 1)
 
-    def spot(self, z, row, of):
+    def spot(self, row, of):
         per = -(-of // self.tiles)
-        return self.wide * z + 8 * (row // per) + row % per
+        return 8 * (row // per) + row % per
 
     def rows(self, ref, step, phase):
         return ref[step, phase].reshape(8 * self.count, N)
 
-    def put(self, step, phase, spot, value):
-        self.send[step, phase, spot // 8, spot % 8 : spot % 8 + 1, :] = value
+    def put(self, step, phase, z, spot, value):
+        self.send[step, phase, z * self.tiles + spot // 8, spot % 8 : spot % 8 + 1, :] = value
+
+    def put_z(self, step, phase, z, rows):
+        self.send[step, phase, z * self.tiles : (z + 1) * self.tiles] = rows.reshape(self.tiles, 8, N)
 
     def put_all(self, step, phase, rows):
         self.send[step, phase] = rows.reshape(self.count, 8, N)
@@ -141,18 +135,19 @@
     out_hbm, dx_ref, dy_ref,
     axis_ref, inc_ref, sig_ref, yld_ref, rate_ref, m1_ref, live1_ref, m2_ref, live2_ref, c_ref,
     load_sems, conc_sems,
-    f_ref, a1_ref, a2_ref, ex_ref, ey_ref, r1_ref, s2c_ref, mx_ref, my_ref, lx_ref, ly_ref,
+    m_ref, q_ref, a1_ref, a2_ref, p1_ref, p2_ref, v_ref, rows_ref, cols_ref, acc_ref,
+    mx_ref, my_ref, lx_ref, ly_ref,
     tx_ref, ty_ref, tab_ref, back_ref, mix_ref, unmix_ref, up_ref, down_ref, left_ref, right_ref,
     wax_ref, way_ref, wcx_ref, wcy_ref,
     bsend, brecv, bback, bdone, bsems, dsend, drecv, dback, ddone, dsems,
 ):
-    conc_loads = [
-        pltpu.make_async_copy(conc_hbm.at[:, z], c_ref.at[:, z], conc_sems.at[z]) for z in range(ZS)
-    ]
+    def conc_load(z):
+        return pltpu.make_async_copy(conc_hbm.at[:, z], c_ref.at[:, z], conc_sems.at[z])
+
     hbm = (axis_hbm, inc_hbm, sig_hbm, yld_hbm, rate_hbm, m1_hbm, live1_hbm, m2_hbm, live2_hbm)
     vmem = (axis_ref, inc_ref, sig_ref, yld_ref, rate_ref, m1_ref, live1_ref, m2_ref, live2_ref)
     loads = [pltpu.make_async_copy(a, b, load_sems.at[k]) for k, (a, b) in enumerate(zip(hbm, vmem))]
-    for load in conc_loads + loads:
+    for load in [conc_load(z) for z in range(ZS)] + loads:
         load.start()
     beam = Ring("beam", bsend, brecv, bback, bdone, bsems)
     det = Ring("det", dsend, drecv, dback, ddone, dsems)
@@ -160,24 +155,57 @@
     det.greet(barrier)
     beam.greet(barrier)
 
-    for ref in (bsend, dsend, mx_ref, my_ref, lx_ref, ly_ref, tx_ref, ty_ref, tab_ref, back_ref):
+    for ref in (bsend, dsend, cols_ref, mx_ref, my_ref, lx_ref, ly_ref, tx_ref, ty_ref, tab_ref, back_ref):
         ref[...] = jnp.zeros(ref.shape, F32)
 
-    lane = iota((N, N), 1)
-
-    def total(step, acc, z, e, c):
-        beam.put(step, 0, beam.spot(z, e, ELEMENTS), jnp.sum(c, 0, keepdims=True))
-        return jnp.where(lane == det.spot(z, e, ELEMENTS), jnp.sum(c, 1, keepdims=True), acc)
-
-    def first_totals():
-        acc = jnp.zeros((N, N), F32)
+    lane = iota((CHUNK, N), 1)
+
+    def over_z(body):
+        def one(z, carry):
+            body(z)
+            return carry
+
+        lax.fori_loop(0, ZS, one, 0)
+
+    def chunks(count, body):
+        def one(r, sums):
+            new = body(pl.ds(pl.multiple_of(r * CHUNK, CHUNK), CHUNK))
+            return tuple(a + jnp.sum(b.reshape(CHUNK // 8, 8, N), 0) for a, b in zip(sums, new))
+
+        sums = lax.fori_loop(0, N // CHUNK, one, (jnp.zeros((8, N), F32),) * count)
+        return [jnp.sum(a, 0, keepdims=True) for a in sums]
+
+    def turned(rows):
+        return jnp.concatenate([rows, jnp.zeros((N - rows.shape[0], N), F32)], 0).T
+
+    def totals(step, add):
+        def one(z):
+            if not add:
+                conc_load(z).wait()
+
+            def chunk(rows):
+                sums = []
+                acc = jnp.zeros((CHUNK, N), F32)
+                cols = cols_ref[z, rows]
+                for e in range(ELEMENTS):
+                    x, y = beam.spot(e, ELEMENTS), det.spot(e, ELEMENTS)
+                    c = c_ref[e, z, rows]
+                    if add:
+                        c = c + rows_ref[z, x : x + 1] + cols[:, y : y + 1]
+                        c_ref[e, z, rows] = c
+                    sums.append(c)
+                    acc = jnp.where(lane == y, jnp.sum(c, 1, keepdims=True), acc)
+                acc_ref[z, rows] = acc
+                return sums
+
+            for e, row in enumerate(chunks(ELEMENTS, chunk)):
+                beam.put(step, 0, z, beam.spot(e, ELEMENTS), row)
+
+        over_z(one)
         for z in range(ZS):
-            conc_loads[z].wait()
-            for e in range(ELEMENTS):
-                acc = total(0, acc, z, e, c_ref[e, z])
-        det.put_all(0, 0, acc.T)
-
-    first_totals()
+            det.put_z(step, 0, z, acc_ref[z].T[0 : det.wide])
+
+    totals(0, False)
     pl.semaphore_wait(barrier, beam.count + det.count - 2)
     det.start(0, 0)
     beam.start(0, 0)
@@ -261,7 +289,7 @@
             live1 = live1_ref[z : z + 1, :].astype(F32)
             live2 = live2_ref[z : z + 1, :].astype(F32)
             for l in range(LINES):
-                x, y = beam.spot(z, l, LINES), det.spot(z, l, LINES)
+                x, y = beam.wide * z + beam.spot(l, LINES), det.wide * z + det.spot(l, LINES)
                 lx_ref[x : x + 1, :] = live1
                 ly_ref[y : y + 1, :] = live2
                 mx_ref[x : x + 1, :] = m1_ref[l, z : z + 1, :]
@@ -269,28 +297,37 @@
 
     tables()
 
-    def blocks(body):
+    def groups(body):
         def one(n, carry):
-            body(n // 4, pl.multiple_of((n % 4) * 32, 32))
+            r0 = (n % 4) * 32
+            for b in range(2):
+                body(n // 4, pl.multiple_of(r0 + 16 * b, 16))
             return carry
 
         lax.fori_loop(0, 4 * ZS, one, 0)
 
     def mix(z, r0):
         parts = []
-        for b in range(4):
+        for b in range(2):
             high, low = split(c_ref[:, z, pl.ds(r0 + 8 * b, 8), :].reshape(8 * ELEMENTS, N))
             parts.append(jnp.concatenate([high, high, low, jnp.zeros((16, N), BF16)], 0))
         out = dot(mix_ref[...], jnp.concatenate(parts, 1))
-        for b in range(4):
-            f_ref[z, :, pl.ds(r0 + 8 * b, 8), :] = out[:, b * N : (b + 1) * N].reshape(FIELDS, 8, N)
+        rows = pl.ds(r0, 16)
+        for f in range(FIELDS):
+            field = jnp.concatenate([out[8 * f : 8 * f + 8, b * N : (b + 1) * N] for b in range(2)], 0)
+            if f < LINES + 2:
+                high, low = split(field)
+                m_ref[z, f, rows, 0:N] = high
+                m_ref[z, f, rows, N : 2 * N] = low
+            else:
+                q_ref[z, f - LINES - 2, rows, :] = field
 
     def unmix(z, r0):
         highs, lows = [], []
-        for b in range(4):
+        for b in range(2):
             rows = pl.ds(r0 + 8 * b, 8)
-            w = a1_ref[z, :, rows, :].reshape(8 * LINES, N)
-            v = f_ref[z, 0 : LINES + 2, rows, :].reshape(8 * (LINES + 2), N)
+            w = a1_ref[z, 0:LINES, rows, :].reshape(8 * LINES, N)
+            v = v_ref[z, :, rows, :].reshape(8 * (LINES + 2), N)
             high, low = split(jnp.concatenate([w, v], 0))
             highs.append(high)
             lows.append(low)
@@ -298,115 +335,131 @@
         one = dot(unmix_ref[...], jnp.concatenate(highs, 1))
         two = dot(unmix_ref[0:wide], jnp.concatenate(lows, 1))
         out = one[0:wide] + (one[wide:] + two)
-        for b in range(4):
+        for b in range(2):
             rows = pl.ds(r0 + 8 * b, 8)
             c_ref[:, z, rows, :] = c_ref[:, z, rows, :] - out[:, b * N : (b + 1) * N].reshape(ELEMENTS, 8, N)
 
-    def attenuate(z, carry):
-        tin1 = jnp.exp2(cum_rows(f_ref[z, LINES + 1], left_ref[...]))
-        tin2 = jnp.exp2(cum_cols(f_ref[z, LINES], up_ref[...]))
+    def stacked(ref, z, fields):
+        value = [ref[z, f] for f in fields]
+        high = jnp.concatenate([v[:, 0:N] for v in value], 1)
+        low = jnp.concatenate([v[:, N : 2 * N] for v in value], 1)
+        return jnp.concatenate([high, low], 0)
+
+    def prefixes(z):
         for l in range(0, LINES, 2):
-            high0, low0 = split(f_ref[z, l])
-            high1, low1 = split(f_ref[z, l + 1])
-            across = jnp.concatenate(
-                [jnp.concatenate([high0, low0], 1), jnp.concatenate([high1, low1], 1)], 0
-            )
-            along = jnp.concatenate(
-                [jnp.concatenate([high0, high1], 1), jnp.concatenate([low0, low1], 1)], 0
-            )
-            over_y = jnp.exp2(dot(across, up_ref[...]))
-            over_x = jnp.exp2(dot(left_ref[...], along))
-            for k in range(2):
-                a1_ref[z, l + k] = tin1 * over_y[k * N : (k + 1) * N]
-                a2_ref[z, l + k] = tin2 * over_x[:, k * N : (k + 1) * N]
-        return carry
-
-    def times(rows, wide, factors, k):
-        parts = [
-            rows[wide * z : wide * (z + 1)] * factors[16 * z + k : 16 * z + k + 1] for z in range(ZS)
-        ]
-        return jnp.concatenate(parts, 0)
+            out = dot(m_ref[z, l : l + 2].reshape(2 * N, 2 * N), up_ref[...])
+            a1_ref[z, l : l + 2] = out.reshape(2, N, N)
+            out = dot(left_ref[...], stacked(m_ref, z, (l, l + 1)))
+            a2_ref[z, l] = out[:, 0:N]
+            a2_ref[z, l + 1] = out[:, N : 2 * N]
+        a1_ref[z, LINES] = dot(m_ref[z, LINES], up_ref[...])
+        a2_ref[z, LINES] = dot(left_ref[...], stacked(m_ref, z, (LINES + 1,)))
+
+    def suffixes(z):
+        for l in range(0, LINES, 2):
+            over_y = dot(p1_ref[z, l : l + 2].reshape(2 * N, 2 * N), down_ref[...])
+            over_x = dot(right_ref[...], stacked(p2_ref, z, (l, l + 1)))
+            v_ref[z, l] = over_y[0:N] + over_x[:, 0:N]
+            v_ref[z, l + 1] = over_y[N : 2 * N] + over_x[:, N : 2 * N]
+        v_ref[z, LINES] = dot(right_ref[...], stacked(p2_ref, z, (LINES,)))
+        v_ref[z, LINES + 1] = dot(p1_ref[z, LINES], down_ref[...])
 
     def counts(step):
-        ex = jnp.exp2(exact(wax_ref[...], beam.rows(bdone, step, 0)))
-        ey = jnp.exp2(exact(way_ref[...], det.rows(ddone, step, 0)))
-        ex_ref[...], ey_ref[...] = ex, ey
-        cols = jnp.concatenate([ey, jnp.zeros((N - 16 * ZS, N), F32)], 0).T
-        acc = jnp.zeros((N, N), F32)
+        enter_x = exact(wax_ref[...], beam.rows(bdone, step, 0))
+        enter_y = exact(way_ref[...], det.rows(ddone, step, 0))
+        rows_ref[:, 0:16] = enter_x.reshape(ZS, 16, N)
         for z in range(ZS):
-            enter = step_x * ex[16 * z + LINES + 1 : 16 * z + LINES + 2]
-            for l in range(LINES):
-                q = f_ref[z, LINES + 2 + l]
-                k = 16 * z + l
-                a1 = a1_ref[z, l] * cols[:, k : k + 1]
-                a1_ref[z, l] = a1
-                beam.put(step, 1, beam.spot(z, l, LINES), enter * jnp.sum(q * a1, 0, keepdims=True))
-                seen = jnp.sum(q * (a2_ref[z, l] * ex[k : k + 1]), 1, keepdims=True)
-                acc = jnp.where(lane == det.spot(z, l, LINES), seen, acc)
-        det.put_all(step, 1, step_y * times(acc.T, det.wide, ey, LINES))
+            cols_ref[z] = turned(enter_y[16 * z : 16 * (z + 1)])
+
+        def one(z):
+            def chunk(rows):
+                cols = cols_ref[z, rows]
+                tin1 = jnp.exp2(a2_ref[z, LINES, rows] + rows_ref[z, LINES + 1 : LINES + 2])
+                tin2 = jnp.exp2(a1_ref[z, LINES, rows] + cols[:, LINES : LINES + 1])
+                sums = []
+                acc = jnp.zeros((CHUNK, N), F32)
+                for l in range(LINES):
+                    a1 = tin1 * jnp.exp2(a1_ref[z, l, rows] + cols[:, l : l + 1])
+                    a2 = tin2 * jnp.exp2(a2_ref[z, l, rows] + rows_ref[z, l : l + 1])
+                    a1_ref[z, l, rows] = a1
+                    a2_ref[z, l, rows] = a2
+                    q = q_ref[z, l, rows]
+                    sums.append(q * a1)
+                    acc = jnp.where(lane == det.spot(l, LINES), jnp.sum(q * a2, 1, keepdims=True), acc)
+                acc_ref[z, rows] = acc
+                return sums
+
+            for l, row in enumerate(chunks(LINES, chunk)):
+                beam.put(step, 1, z, beam.spot(l, LINES), step_x * row)
+
+        over_z(one)
+        for z in range(ZS):
+            det.put_z(step, 1, z, step_y * acc_ref[z].T[0 : det.wide])
 
     def residuals(step):
-        ex, ey = ex_ref[...], ey_ref[...]
         res1 = lx_ref[...] * (beam.rows(bdone, step, 1) - mx_ref[...])
         res2 = ly_ref[...] * (det.rows(ddone, step, 1) - my_ref[...])
         sum1 = res1 * beam.rows(bsend, step, 1) / step_x
         sum2 = res2 * det.rows(dsend, step, 1) / step_y
-        r1 = times(res1, beam.wide, ex, LINES + 1)
-        r1_ref[...] = r1
-        cols = times(res2, det.wide, ey, LINES).T
-        s2c_ref[...] = cols
-        acc = jnp.zeros((N, N), F32)
+        rows_ref[:, 0 : beam.wide] = res1.reshape(ZS, beam.wide, N)
         for z in range(ZS):
-            for l in range(LINES):
-                q = f_ref[z, LINES + 2 + l]
-                k, x, y = 16 * z + l, beam.spot(z, l, LINES), det.spot(z, l, LINES)
-                seen = jnp.sum(q * (a1_ref[z, l] * r1[x : x + 1]), 1, keepdims=True)
-                acc = jnp.where(lane == k, seen, acc)
-                seen = jnp.sum(q * (a2_ref[z, l] * cols[:, y : y + 1]), 0, keepdims=True)
-                tx_ref[k : k + 1, :] = ex[k : k + 1] * seen
-        ty_ref[...] = acc.T[0 : 16 * ZS]
+            cols_ref[z] = turned(res2[det.wide * z : det.wide * (z + 1)])
+
+        def one(z):
+            def chunk(rows):
+                cols = cols_ref[z, rows]
+                sums = []
+                acc = jnp.zeros((CHUNK, N), F32)
+                all1 = jnp.zeros((CHUNK, N), F32)
+                all2 = jnp.zeros((CHUNK, N), F32)
+
+                def keep(ref, f, value):
+                    high, low = split(value)
+                    ref[z, f, rows, 0:N] = high
+                    ref[z, f, rows, N : 2 * N] = low
+
+                for l in range(LINES):
+                    x, y = beam.spot(l, LINES), det.spot(l, LINES)
+                    w1 = a1_ref[z, l, rows] * rows_ref[z, x : x + 1]
+                    w2 = a2_ref[z, l, rows] * cols[:, y : y + 1]
+                    a1_ref[z, l, rows] = w1 + w2
+                    q = q_ref[z, l, rows]
+                    p1, p2 = q * w1, q * w2
+                    all1, all2 = all1 + p1, all2 + p2
+                    sums.append(p2)
+                    acc = jnp.where(lane == l, jnp.sum(p1, 1, keepdims=True), acc)
+                    keep(p1_ref, l, p1)
+                    keep(p2_ref, l, p2)
+                keep(p1_ref, LINES, all2)
+                keep(p2_ref, LINES, all1)
+                acc_ref[z, rows] = acc
+                return sums
+
+            for l, row in enumerate(chunks(LINES, chunk)):
+                tx_ref[z, l : l + 1] = row
+
+        over_z(one)
         for z in range(ZS):
-            k = 16 * z + LINES
-            tx_ref[k : k + 1, :] = jnp.sum(sum1[beam.wide * z : beam.wide * (z + 1)], 0, keepdims=True)
-            ty_ref[k : k + 1, :] = jnp.sum(sum2[det.wide * z : det.wide * (z + 1)], 0, keepdims=True)
-        beam.put_all(step, 2, exact(wcx_ref[...], tx_ref[...]))
-        det.put_all(step, 2, exact(wcy_ref[...], ty_ref[...]))
-
-    def weights():
-        ex, r1, cols = ex_ref[...], r1_ref[...], s2c_ref[...]
+            ty_ref[z] = acc_ref[z].T[0:16]
+            k = slice(LINES, LINES + 1)
+            tx_ref[z, k] = jnp.sum(sum1[beam.wide * z : beam.wide * (z + 1)], 0, keepdims=True)
+            ty_ref[z, k] = jnp.sum(sum2[det.wide * z : det.wide * (z + 1)], 0, keepdims=True)
+        beam.put_all(step, 2, exact(wcx_ref[...], tx_ref[...].reshape(16 * ZS, N)))
+        det.put_all(step, 2, exact(wcy_ref[...], ty_ref[...].reshape(16 * ZS, N)))
+
+    def update(step):
+        rows_ref[:, 0 : beam.wide] = beam.rows(bdone, step, 2).reshape(ZS, beam.wide, N)
+        enter = det.rows(ddone, step, 2)
         for z in range(ZS):
-            sum1 = jnp.zeros((N, N), F32)
-            sum2 = jnp.zeros((N, N), F32)
-            for l in range(LINES):
-                q = f_ref[z, LINES + 2 + l]
-                k, x, y = 16 * z + l, beam.spot(z, l, LINES), det.spot(z, l, LINES)
-                w1 = a1_ref[z, l] * r1[x : x + 1]
-                w2 = a2_ref[z, l] * ex[k : k + 1] * cols[:, y : y + 1]
-                a1_ref[z, l] = w1 + w2
-                p1, p2 = q * w1, q * w2
-                sum1, sum2 = sum1 + p1, sum2 + p2
-                f_ref[z, l] = cum_cols(p1, down_ref[...]) + cum_rows(p2, right_ref[...])
-            f_ref[z, LINES] = cum_rows(sum1, right_ref[...])
-            f_ref[z, LINES + 1] = cum_cols(sum2, down_ref[...])
-
-    def update(step):
-        cols = det.rows(ddone, step, 2).T
-        rows = beam.rows(bdone, step, 2)
-        acc = jnp.zeros((N, N), F32)
-        for z in range(ZS):
-            for e in range(ELEMENTS):
-                x, y = beam.spot(z, e, ELEMENTS), det.spot(z, e, ELEMENTS)
-                c = c_ref[e, z] + rows[x : x + 1] + cols[:, y : y + 1]
-                c_ref[e, z] = c
-                acc = total(step + 1, acc, z, e, c)
-        det.put_all(step + 1, 0, acc.T)
+            cols_ref[z] = turned(enter[det.wide * z : det.wide * (z + 1)])
+        totals(step + 1, True)
 
     def turn(step, carry):
         last = step == STEPS - 1
-        blocks(mix)
+        groups(mix)
         det.middle(step, 0, "earlier")
         beam.middle(step, 0, "earlier")
-        lax.fori_loop(0, ZS, attenuate, 0)
+        over_z(prefixes)
         det.finish(step, 0)
         beam.finish(step, 0)
         counts(step)
@@ -419,23 +472,26 @@
         residuals(step)
         det.start(step, 2)
         beam.start(step, 2)
-        weights()
+        over_z(suffixes)
         det.middle(step, 2, "later")
         beam.middle(step, 2, "later")
-        blocks(unmix)
+        groups(unmix)
+
+        def stores():
+            return [pltpu.make_async_copy(c_ref.at[:, z], out_hbm.at[:, z], conc_sems.at[z]) for z in range(ZS)]
 
         @pl.when(last)
         def leave():
-            stores = [
-                pltpu.make_async_copy(c_ref.at[:, z], out_hbm.at[:, z], conc_sems.at[z]) for z in range(ZS)
-            ]
-            for store in stores:
+            for store in stores():
                 store.start()
-            for store in stores:
-                store.wait()
 
         det.finish(step, 2)
         beam.finish(step, 2)
+
+        @pl.when(last)
+        def left():
+            for store in stores():
+                store.wait()
 
         @pl.when(jnp.logical_not(last))
         def go_on():
@@ -494,17 +550,18 @@
                 *[pltpu.VMEM(a.shape, a.dtype) for a in small + (conc,)],
                 pltpu.SemaphoreType.DMA((len(small),)),
                 pltpu.SemaphoreType.DMA((ZS,)),
-                pltpu.VMEM((ZS, FIELDS) + field, F32),
+                pltpu.VMEM((ZS, LINES + 2, N, 2 * N), BF16),
                 pltpu.VMEM((ZS, LINES) + field, F32),
-                pltpu.VMEM((ZS, LINES) + field, F32),
-                *[pltpu.VMEM((16 * ZS, N), F32)] * 2,
-                pltpu.VMEM((8 * beams, N), F32),
-                pltpu.VMEM(field, F32),
+                *[pltpu.VMEM((ZS, LINES + 1) + field, F32)] * 2,
+                *[pltpu.VMEM((ZS, LINES + 1, N, 2 * N), BF16)] * 2,
+                pltpu.VMEM((ZS, LINES + 2) + field, F32),
+                pltpu.VMEM((ZS, 16, N), F32),
+                *[pltpu.VMEM((ZS,) + field, F32)] * 2,
                 pltpu.VMEM((8 * beams, N), F32),
                 pltpu.VMEM((8 * dets, N), F32),
                 pltpu.VMEM((8 * beams, N), F32),
                 pltpu.VMEM((8 * dets, N), F32),
-                *[pltpu.VMEM((16 * ZS, N), F32)] * 2,
+                *[pltpu.VMEM((ZS, 16, N), F32)] * 2,
                 *[pltpu.VMEM((32, N), F32)] * 2,
                 pltpu.VMEM((8 * FIELDS, 2 * N), BF16),
                 pltpu.VMEM((16 * ELEMENTS, 8 * FIELDS), BF16),

time: 90 us -> 118 us (1.31)
  Pallas kernels: 89 us -> 117 us
    pallas_call x1, Pallas kernels: 84.4 us -> 112 us  [shards(): pl.pallas_call(body, out_shape=[jax.ShapeDtypeStruct(conc.shape, F32), ja...]
where the time goes in v5:
time: 118 us; the launch traced here: 117 us
  Pallas kernels  117 us (99%)
    pallas_call x1, Pallas kernels, shards(): pl.pallas_call(body, out_shape=[jax.ShapeDtypeStruct(conc.shape, F32), ja...  112 us
    pallas_call x1, Pallas kernels, shards(): pl.pallas_call(last, out_shape=jax.ShapeDtypeStruct(conc.shape, F32), gri...  4.64 us

profile of v5, /device:TPU:0, one launch (start us, length us, event | category | flops | bytes accessed | tf_op | source)
XLA Modules:
  0.0 117.0 jit_solution(9484331464700916659)
XLA Ops:
  0.0 112.3 %shard_map.100 = (f32[10,4,128,128]{3,2,1,0:T(8,128)}, f32[8,8,128]{2,1,0:T(8,128)}, f32[16,8,128]{2,1,0:T(8,128)}) custom-call(s32[1,2]{1,0:T(1,128)} %bitcast.2, f32[2,10]{1,0:T(2,128)} %refs_1_.1, f32[12,10]{1,0:T(8,128)} %refs_2_.1, f32[12,10]{1,0:T(8,128)} %refs_3_.1, f32[1,10]{1,0:T(1,128)} %bitcast.3, f32[12,4,128]{2,1,0:T(4,128)} %refs_5_.1, ...), custom_call_target="tpu_custom_call" | custom-call | tf_op jit(solution)/shard_map/pallas_call | solution.py:540
  112.4 4.6 %shard_map.101 = f32[10,4,128,128]{3,2,1,0:T(8,128)} custom-call(f32[10,4,128,128]{3,2,1,0:T(8,128)} %get-tuple-element.8.refs_0_, f32[8,8,128]{2,1,0:T(8,128)} %get-tuple-element.9.refs_1_, f32[16,8,128]{2,1,0:T(8,128)} %get-tuple-element.10.refs_2_), custom_call_target="tpu_custom_call" | custom-call | tf_op jit(solution)/shard_map/pallas_call | solution.py:588

commit v6 on v5

--- a/solution.py
+++ b/solution.py
@@ -17,7 +17,7 @@
 ZS = 4
 N = 128
 FIELDS = 26
-CHUNK = 32
+CHUNK = 64
 LOG2E = math.log2(math.e)
 
 
@@ -51,7 +51,7 @@
 class Ring:
     def __init__(self, axis, send, recv, back, done, sems):
         self.axis = axis
-        self.count = recv.shape[2]
+        self.count = recv.shape[1]
         self.me = lax.axis_index(axis)
         self.send, self.recv, self.back, self.done, self.sems = send, recv, back, done, sems
         self.tiles = self.count // ZS
@@ -66,67 +66,67 @@
         for d in self.hops:
             pl.semaphore_signal(barrier, inc=1, device_id={self.axis: self.peer(d)}, device_id_type=MESH)
 
-    def copy(self, src, dst, step, phase, leg, peer):
+    def copy(self, src, dst, phase, leg, peer):
         return pltpu.make_async_remote_copy(
             src_ref=src,
             dst_ref=dst,
-            send_sem=self.sems.at[step, phase, leg, 0],
-            recv_sem=self.sems.at[step, phase, leg, 1],
+            send_sem=self.sems.at[phase, leg, 0],
+            recv_sem=self.sems.at[phase, leg, 1],
             device_id={self.axis: peer},
             device_id_type=MESH,
         )
 
-    def start(self, step, phase):
-        mine = (step, phase, pl.ds(self.me, 1))
+    def start(self, phase):
+        mine = (phase, pl.ds(self.me, 1))
         self.recv[mine] = self.send[mine]
         for d in self.hops:
             peer = self.peer(d)
-            src, dst = self.send.at[step, phase, peer], self.recv.at[step, phase, self.me]
-            self.copy(src, dst, step, phase, 0, peer).start()
-
-    def wait(self, src, dst, step, phase, leg):
-        several = (step, phase, pl.ds(0, self.count - 1))
-        whole = self.copy(src.at[several], dst.at[several], step, phase, leg, self.peer(1))
+            src, dst = self.send.at[phase, peer], self.recv.at[phase, self.me]
+            self.copy(src, dst, phase, 0, peer).start()
+
+    def wait(self, src, dst, phase, leg):
+        several = (phase, pl.ds(0, self.count - 1))
+        whole = self.copy(src.at[several], dst.at[several], phase, leg, self.peer(1))
         whole.wait_send()
         whole.wait_recv()
 
-    def middle(self, step, phase, mode):
-        self.wait(self.send, self.recv, step, phase, 0)
+    def middle(self, phase, mode):
+        self.wait(self.send, self.recv, phase, 0)
         total = jnp.zeros((8, N), F32)
         order = range(self.count)
         for t in reversed(order) if mode == "later" else order:
             if mode != "sum":
-                self.back[step, phase, t] = total
-            total = total + self.recv[step, phase, t]
-        mine = (step, phase, pl.ds(self.me, 1))
+                self.back[phase, t] = total
+            total = total + self.recv[phase, t]
+        mine = (phase, pl.ds(self.me, 1))
         if mode == "sum":
-            self.back[step, phase, 0] = total
+            self.back[phase, 0] = total
             self.done[mine] = total[None]
         else:
             self.done[mine] = self.back[mine]
         for d in self.hops:
             peer = self.peer(d)
-            src = self.back.at[step, phase, 0 if mode == "sum" else peer]
-            self.copy(src, self.done.at[step, phase, self.me], step, phase, 1, peer).start()
-
-    def finish(self, step, phase):
-        self.wait(self.back, self.done, step, phase, 1)
+            src = self.back.at[phase, 0 if mode == "sum" else peer]
+            self.copy(src, self.done.at[phase, self.me], phase, 1, peer).start()
+
+    def finish(self, phase):
+        self.wait(self.back, self.done, phase, 1)
 
     def spot(self, row, of):
         per = -(-of // self.tiles)
         return 8 * (row // per) + row % per
 
-    def rows(self, ref, step, phase):
-        return ref[step, phase].reshape(8 * self.count, N)
-
-    def put(self, step, phase, z, spot, value):
-        self.send[step, phase, z * self.tiles + spot // 8, spot % 8 : spot % 8 + 1, :] = value
-
-    def put_z(self, step, phase, z, rows):
-        self.send[step, phase, z * self.tiles : (z + 1) * self.tiles] = rows.reshape(self.tiles, 8, N)
-
-    def put_all(self, step, phase, rows):
-        self.send[step, phase] = rows.reshape(self.count, 8, N)
+    def rows(self, ref, phase):
+        return ref[phase].reshape(8 * self.count, N)
+
+    def put(self, phase, z, spot, value):
+        self.send[phase, z * self.tiles + spot // 8, spot % 8 : spot % 8 + 1, :] = value
+
+    def put_z(self, phase, z, rows):
+        self.send[phase, z * self.tiles : (z + 1) * self.tiles] = rows.reshape(self.tiles, 8, N)
+
+    def put_all(self, phase, rows):
+        self.send[phase] = rows.reshape(self.count, 8, N)
 
 
 def kernel(
@@ -135,7 +135,7 @@
     out_hbm, dx_ref, dy_ref,
     axis_ref, inc_ref, sig_ref, yld_ref, rate_ref, m1_ref, live1_ref, m2_ref, live2_ref, c_ref,
     load_sems, conc_sems,
-    m_ref, q_ref, a1_ref, a2_ref, p1_ref, p2_ref, v_ref, rows_ref, cols_ref, acc_ref,
+    m_ref, q_ref, e1_ref, e2_ref, a1_ref, a2_ref, w_ref, p1_ref, p2_ref, v_ref, d_ref, rows_ref, cols_ref, acc_ref,
     mx_ref, my_ref, lx_ref, ly_ref,
     tx_ref, ty_ref, tab_ref, back_ref, mix_ref, unmix_ref, up_ref, down_ref, left_ref, right_ref,
     wax_ref, way_ref, wcx_ref, wcy_ref,
@@ -161,24 +161,20 @@
     lane = iota((CHUNK, N), 1)
 
     def over_z(body):
-        def one(z, carry):
+        for z in range(ZS):
             body(z)
-            return carry
-
-        lax.fori_loop(0, ZS, one, 0)
 
     def chunks(count, body):
-        def one(r, sums):
-            new = body(pl.ds(pl.multiple_of(r * CHUNK, CHUNK), CHUNK))
-            return tuple(a + jnp.sum(b.reshape(CHUNK // 8, 8, N), 0) for a, b in zip(sums, new))
-
-        sums = lax.fori_loop(0, N // CHUNK, one, (jnp.zeros((8, N), F32),) * count)
+        sums = [jnp.zeros((8, N), F32)] * count
+        for r in range(0, N, CHUNK):
+            new = body(pl.ds(r, CHUNK))
+            sums = [a + jnp.sum(b.reshape(CHUNK // 8, 8, N), 0) for a, b in zip(sums, new)]
         return [jnp.sum(a, 0, keepdims=True) for a in sums]
 
     def turned(rows):
         return jnp.concatenate([rows, jnp.zeros((N - rows.shape[0], N), F32)], 0).T
 
-    def totals(step, add):
+    def totals(add):
         def one(z):
             if not add:
                 conc_load(z).wait()
@@ -189,7 +185,7 @@
                 cols = cols_ref[z, rows]
                 for e in range(ELEMENTS):
                     x, y = beam.spot(e, ELEMENTS), det.spot(e, ELEMENTS)
-                    c = c_ref[e, z, rows]
+                    c = d_ref[e, z, rows] if add else c_ref[e, z, rows]
                     if add:
                         c = c + rows_ref[z, x : x + 1] + cols[:, y : y + 1]
                         c_ref[e, z, rows] = c
@@ -199,16 +195,16 @@
                 return sums
 
             for e, row in enumerate(chunks(ELEMENTS, chunk)):
-                beam.put(step, 0, z, beam.spot(e, ELEMENTS), row)
+                beam.put(0, z, beam.spot(e, ELEMENTS), row)
 
         over_z(one)
         for z in range(ZS):
-            det.put_z(step, 0, z, acc_ref[z].T[0 : det.wide])
-
-    totals(0, False)
+            det.put_z(0, z, acc_ref[z].T[0 : det.wide])
+
+    totals(False)
     pl.semaphore_wait(barrier, beam.count + det.count - 2)
-    det.start(0, 0)
-    beam.start(0, 0)
+    det.start(0)
+    beam.start(0)
     for load in loads:
         load.wait()
 
@@ -298,23 +294,19 @@
     tables()
 
     def groups(body):
-        def one(n, carry):
-            r0 = (n % 4) * 32
-            for b in range(2):
-                body(n // 4, pl.multiple_of(r0 + 16 * b, 16))
-            return carry
-
-        lax.fori_loop(0, 4 * ZS, one, 0)
+        for z in range(ZS):
+            for r0 in range(0, N, 32):
+                body(z, r0)
 
     def mix(z, r0):
         parts = []
-        for b in range(2):
+        for b in range(4):
             high, low = split(c_ref[:, z, pl.ds(r0 + 8 * b, 8), :].reshape(8 * ELEMENTS, N))
             parts.append(jnp.concatenate([high, high, low, jnp.zeros((16, N), BF16)], 0))
         out = dot(mix_ref[...], jnp.concatenate(parts, 1))
-        rows = pl.ds(r0, 16)
+        rows = pl.ds(r0, 32)
         for f in range(FIELDS):
-            field = jnp.concatenate([out[8 * f : 8 * f + 8, b * N : (b + 1) * N] for b in range(2)], 0)
+            field = jnp.concatenate([out[8 * f : 8 * f + 8, b * N : (b + 1) * N] for b in range(4)], 0)
             if f < LINES + 2:
                 high, low = split(field)
                 m_ref[z, f, rows, 0:N] = high
@@ -324,9 +316,9 @@
 
     def unmix(z, r0):
         highs, lows = [], []
-        for b in range(2):
+        for b in range(4):
             rows = pl.ds(r0 + 8 * b, 8)
-            w = a1_ref[z, 0:LINES, rows, :].reshape(8 * LINES, N)
+            w = w_ref[z, :, rows, :].reshape(8 * LINES, N)
             v = v_ref[z, :, rows, :].reshape(8 * (LINES + 2), N)
             high, low = split(jnp.concatenate([w, v], 0))
             highs.append(high)
@@ -335,9 +327,9 @@
         one = dot(unmix_ref[...], jnp.concatenate(highs, 1))
         two = dot(unmix_ref[0:wide], jnp.concatenate(lows, 1))
         out = one[0:wide] + (one[wide:] + two)
-        for b in range(2):
+        for b in range(4):
             rows = pl.ds(r0 + 8 * b, 8)
-            c_ref[:, z, rows, :] = c_ref[:, z, rows, :] - out[:, b * N : (b + 1) * N].reshape(ELEMENTS, 8, N)
+            d_ref[:, z, rows, :] = c_ref[:, z, rows, :] - out[:, b * N : (b + 1) * N].reshape(ELEMENTS, 8, N)
 
     def stacked(ref, z, fields):
         value = [ref[z, f] for f in fields]
@@ -348,12 +340,12 @@
     def prefixes(z):
         for l in range(0, LINES, 2):
             out = dot(m_ref[z, l : l + 2].reshape(2 * N, 2 * N), up_ref[...])
-            a1_ref[z, l : l + 2] = out.reshape(2, N, N)
+            e1_ref[z, l : l + 2] = out.reshape(2, N, N)
             out = dot(left_ref[...], stacked(m_ref, z, (l, l + 1)))
-            a2_ref[z, l] = out[:, 0:N]
-            a2_ref[z, l + 1] = out[:, N : 2 * N]
-        a1_ref[z, LINES] = dot(m_ref[z, LINES], up_ref[...])
-        a2_ref[z, LINES] = dot(left_ref[...], stacked(m_ref, z, (LINES + 1,)))
+            e2_ref[z, l] = out[:, 0:N]
+            e2_ref[z, l + 1] = out[:, N : 2 * N]
+        e1_ref[z, LINES] = dot(m_ref[z, LINES], up_ref[...])
+        e2_ref[z, LINES] = dot(left_ref[...], stacked(m_ref, z, (LINES + 1,)))
 
     def suffixes(z):
         for l in range(0, LINES, 2):
@@ -364,9 +356,9 @@
         v_ref[z, LINES] = dot(right_ref[...], stacked(p2_ref, z, (LINES,)))
         v_ref[z, LINES + 1] = dot(p1_ref[z, LINES], down_ref[...])
 
-    def counts(step):
-        enter_x = exact(wax_ref[...], beam.rows(bdone, step, 0))
-        enter_y = exact(way_ref[...], det.rows(ddone, step, 0))
+    def counts():
+        enter_x = exact(wax_ref[...], beam.rows(bdone, 0))
+        enter_y = exact(way_ref[...], det.rows(ddone, 0))
         rows_ref[:, 0:16] = enter_x.reshape(ZS, 16, N)
         for z in range(ZS):
             cols_ref[z] = turned(enter_y[16 * z : 16 * (z + 1)])
@@ -374,13 +366,13 @@
         def one(z):
             def chunk(rows):
                 cols = cols_ref[z, rows]
-                tin1 = jnp.exp2(a2_ref[z, LINES, rows] + rows_ref[z, LINES + 1 : LINES + 2])
-                tin2 = jnp.exp2(a1_ref[z, LINES, rows] + cols[:, LINES : LINES + 1])
+                tin1 = jnp.exp2(e2_ref[z, LINES, rows] + rows_ref[z, LINES + 1 : LINES + 2])
+                tin2 = jnp.exp2(e1_ref[z, LINES, rows] + cols[:, LINES : LINES + 1])
                 sums = []
                 acc = jnp.zeros((CHUNK, N), F32)
                 for l in range(LINES):
-                    a1 = tin1 * jnp.exp2(a1_ref[z, l, rows] + cols[:, l : l + 1])
-                    a2 = tin2 * jnp.exp2(a2_ref[z, l, rows] + rows_ref[z, l : l + 1])
+                    a1 = tin1 * jnp.exp2(e1_ref[z, l, rows] + cols[:, l : l + 1])
+                    a2 = tin2 * jnp.exp2(e2_ref[z, l, rows] + rows_ref[z, l : l + 1])
                     a1_ref[z, l, rows] = a1
                     a2_ref[z, l, rows] = a2
                     q = q_ref[z, l, rows]
@@ -390,17 +382,17 @@
                 return sums
 
             for l, row in enumerate(chunks(LINES, chunk)):
-                beam.put(step, 1, z, beam.spot(l, LINES), step_x * row)
+                beam.put(1, z, beam.spot(l, LINES), step_x * row)
 
         over_z(one)
         for z in range(ZS):
-            det.put_z(step, 1, z, step_y * acc_ref[z].T[0 : det.wide])
-
-    def residuals(step):
-        res1 = lx_ref[...] * (beam.rows(bdone, step, 1) - mx_ref[...])
-        res2 = ly_ref[...] * (det.rows(ddone, step, 1) - my_ref[...])
-        sum1 = res1 * beam.rows(bsend, step, 1) / step_x
-        sum2 = res2 * det.rows(dsend, step, 1) / step_y
+            det.put_z(1, z, step_y * acc_ref[z].T[0 : det.wide])
+
+    def residuals():
+        res1 = lx_ref[...] * (beam.rows(bdone, 1) - mx_ref[...])
+        res2 = ly_ref[...] * (det.rows(ddone, 1) - my_ref[...])
+        sum1 = res1 * beam.rows(bsend, 1) / step_x
+        sum2 = res2 * det.rows(dsend, 1) / step_y
         rows_ref[:, 0 : beam.wide] = res1.reshape(ZS, beam.wide, N)
         for z in range(ZS):
             cols_ref[z] = turned(res2[det.wide * z : det.wide * (z + 1)])
@@ -422,7 +414,7 @@
                     x, y = beam.spot(l, LINES), det.spot(l, LINES)
                     w1 = a1_ref[z, l, rows] * rows_ref[z, x : x + 1]
                     w2 = a2_ref[z, l, rows] * cols[:, y : y + 1]
-                    a1_ref[z, l, rows] = w1 + w2
+                    w_ref[z, l, rows] = w1 + w2
                     q = q_ref[z, l, rows]
                     p1, p2 = q * w1, q * w2
                     all1, all2 = all1 + p1, all2 + p2
@@ -444,49 +436,49 @@
             k = slice(LINES, LINES + 1)
             tx_ref[z, k] = jnp.sum(sum1[beam.wide * z : beam.wide * (z + 1)], 0, keepdims=True)
             ty_ref[z, k] = jnp.sum(sum2[det.wide * z : det.wide * (z + 1)], 0, keepdims=True)
-        beam.put_all(step, 2, exact(wcx_ref[...], tx_ref[...].reshape(16 * ZS, N)))
-        det.put_all(step, 2, exact(wcy_ref[...], ty_ref[...].reshape(16 * ZS, N)))
-
-    def update(step):
-        rows_ref[:, 0 : beam.wide] = beam.rows(bdone, step, 2).reshape(ZS, beam.wide, N)
-        enter = det.rows(ddone, step, 2)
+        beam.put_all(2, exact(wcx_ref[...], tx_ref[...].reshape(16 * ZS, N)))
+        det.put_all(2, exact(wcy_ref[...], ty_ref[...].reshape(16 * ZS, N)))
+
+    def update():
+        rows_ref[:, 0 : beam.wide] = beam.rows(bdone, 2).reshape(ZS, beam.wide, N)
+        enter = det.rows(ddone, 2)
         for z in range(ZS):
             cols_ref[z] = turned(enter[det.wide * z : det.wide * (z + 1)])
-        totals(step + 1, True)
+        totals(True)
 
     def turn(step, carry):
         last = step == STEPS - 1
         groups(mix)
-        det.middle(step, 0, "earlier")
-        beam.middle(step, 0, "earlier")
+        det.middle(0, "earlier")
+        beam.middle(0, "earlier")
         over_z(prefixes)
-        det.finish(step, 0)
-        beam.finish(step, 0)
-        counts(step)
-        det.start(step, 1)
-        beam.start(step, 1)
-        det.middle(step, 1, "sum")
-        beam.middle(step, 1, "sum")
-        det.finish(step, 1)
-        beam.finish(step, 1)
-        residuals(step)
-        det.start(step, 2)
-        beam.start(step, 2)
+        det.finish(0)
+        beam.finish(0)
+        counts()
+        det.start(1)
+        beam.start(1)
+        det.middle(1, "sum")
+        beam.middle(1, "sum")
+        det.finish(1)
+        beam.finish(1)
+        residuals()
+        det.start(2)
+        beam.start(2)
         over_z(suffixes)
-        det.middle(step, 2, "later")
-        beam.middle(step, 2, "later")
+        det.middle(2, "later")
+        beam.middle(2, "later")
         groups(unmix)
 
         def stores():
-            return [pltpu.make_async_copy(c_ref.at[:, z], out_hbm.at[:, z], conc_sems.at[z]) for z in range(ZS)]
+            return [pltpu.make_async_copy(d_ref.at[:, z], out_hbm.at[:, z], conc_sems.at[z]) for z in range(ZS)]
 
         @pl.when(last)
         def leave():
             for store in stores():
                 store.start()
 
-        det.finish(step, 2)
-        beam.finish(step, 2)
+        det.finish(2)
+        beam.finish(2)
 
         @pl.when(last)
         def left():
@@ -495,15 +487,15 @@
 
         @pl.when(jnp.logical_not(last))
         def go_on():
-            update(step)
-            det.start(step + 1, 0)
-            beam.start(step + 1, 0)
+            update()
+            det.start(0)
+            beam.start(0)
 
         return carry
 
     lax.fori_loop(0, STEPS, turn, 0)
-    dx_ref[...] = bdone[STEPS - 1, 2]
-    dy_ref[...] = ddone[STEPS - 1, 2]
+    dx_ref[...] = bdone[2]
+    dy_ref[...] = ddone[2]
 
 
 def close(x_spots, y_spots, c_ref, dx_ref, dy_ref, out_ref):
@@ -526,8 +518,8 @@
             kernel(step_x, step_y, *refs)
 
         def exchange(count):
-            tiles = pltpu.VMEM((STEPS, 3, count, 8, N), F32)
-            return [tiles] * 4 + [pltpu.SemaphoreType.DMA((STEPS, 3, 2, 2))]
+            tiles = pltpu.VMEM((3, count, 8, N), F32)
+            return [tiles] * 4 + [pltpu.SemaphoreType.DMA((3, 2, 2))]
 
         def spots(tiles):
             per = -(-ELEMENTS // tiles)
@@ -553,8 +545,10 @@
                 pltpu.VMEM((ZS, LINES + 2, N, 2 * N), BF16),
                 pltpu.VMEM((ZS, LINES) + field, F32),
                 *[pltpu.VMEM((ZS, LINES + 1) + field, F32)] * 2,
+                *[pltpu.VMEM((ZS, LINES) + field, F32)] * 3,
                 *[pltpu.VMEM((ZS, LINES + 1, N, 2 * N), BF16)] * 2,
                 pltpu.VMEM((ZS, LINES + 2) + field, F32),
+                pltpu.VMEM(conc.shape, F32),
                 pltpu.VMEM((ZS, 16, N), F32),
                 *[pltpu.VMEM((ZS,) + field, F32)] * 2,
                 pltpu.VMEM((8 * beams, N), F32),

time: 118 us -> 90.6 us (0.77)
  Pallas kernels: 117 us -> 89.6 us
    pallas_call x1, Pallas kernels: 112 us -> 84.9 us  [shards(): pl.pallas_call(body, out_shape=[jax.ShapeDtypeStruct(conc.shape, F32), ja...]
where the time goes in v6:
time: 90.6 us; the launch traced here: 89.6 us
  Pallas kernels  89.6 us (99%)
    pallas_call x1, Pallas kernels, shards(): pl.pallas_call(body, out_shape=[jax.ShapeDtypeStruct(conc.shape, F32), ja...  84.9 us
    pallas_call x1, Pallas kernels, shards(): pl.pallas_call(last, out_shape=jax.ShapeDtypeStruct(conc.shape, F32), gri...  4.64 us

profile of v6, /device:TPU:0, one launch (start us, length us, event | category | flops | bytes accessed | tf_op | source)
XLA Modules:
  0.0 89.6 jit_solution(2357713570231829609)
XLA Ops:
  0.0 84.9 %shard_map.100 = (f32[10,4,128,128]{3,2,1,0:T(8,128)}, f32[8,8,128]{2,1,0:T(8,128)}, f32[16,8,128]{2,1,0:T(8,128)}) custom-call(s32[1,2]{1,0:T(1,128)} %bitcast.2, f32[2,10]{1,0:T(2,128)} %refs_1_.1, f32[12,10]{1,0:T(8,128)} %refs_2_.1, f32[12,10]{1,0:T(8,128)} %refs_3_.1, f32[1,10]{1,0:T(1,128)} %bitcast.3, f32[12,4,128]{2,1,0:T(4,128)} %refs_5_.1, ...), custom_call_target="tpu_custom_call" | custom-call | tf_op jit(solution)/shard_map/pallas_call | solution.py:532
  84.9 4.6 %shard_map.101 = f32[10,4,128,128]{3,2,1,0:T(8,128)} custom-call(f32[10,4,128,128]{3,2,1,0:T(8,128)} %get-tuple-element.8.refs_0_, f32[8,8,128]{2,1,0:T(8,128)} %get-tuple-element.9.refs_1_, f32[16,8,128]{2,1,0:T(8,128)} %get-tuple-element.10.refs_2_), custom_call_target="tpu_custom_call" | custom-call | tf_op jit(solution)/shard_map/pallas_call | solution.py:582

commit v7 on v6

v7 whole, which is shorter than its diff:
```python
import math

import jax
import jax.numpy as jnp
from jax import lax
from jax.experimental import pallas as pl
from jax.experimental.pallas import tpu as pltpu
from jax.sharding import PartitionSpec as P

STEPS = 2
HIGH = lax.Precision.HIGHEST
MESH = pl.DeviceIdType.MESH
F32 = jnp.float32
BF16 = jnp.bfloat16
ELEMENTS = 10
LINES = 12
ZS = 4
N = 128
FIELDS = 26
CHUNK = 64
AHEAD = 4
ROWS = (ELEMENTS * ZS, LINES * ZS, ELEMENTS * ZS)
LOG2E = math.log2(math.e)


def split(value):
    high = value.astype(BF16)
    return high, (value - high.astype(F32)).astype(BF16)


def iota(shape, dim):
    return lax.broadcasted_iota(jnp.int32, shape, dim)


def dot(a, b):
    return jnp.dot(a, b, preferred_element_type=F32)


def exact(a, b):
    return jnp.dot(a, b, preferred_element_type=F32, precision=HIGH)


def exact_nt(a, b):
    return lax.dot_general(
        a, b, (((1,), (1,)), ((), ())), preferred_element_type=F32, precision=HIGH
    )


def one_hot(condition):
    return jnp.where(condition, 1.0, 0.0).astype(F32)


class Ring:
    def __init__(self, axis, count, send, near, out, far, sems):
        self.axis, self.count = axis, count
        self.send, self.near, self.out, self.far, self.sems = send, near, out, far, sems
        self.slots = count // AHEAD
        self.cores = self.slots // 2
        me = lax.axis_index(axis)
        self.c = lax.rem(me, self.cores)
        self.x = lax.rem(me // self.cores, AHEAD)
        self.y = me // (self.cores * AHEAD)
        self.slot = self.y * self.cores + self.c

    def index(self, y, x, c):
        return (y * AHEAD + x) * self.cores + c

    def near_peers(self):
        slots = [lax.rem(self.slot + d, self.slots) for d in range(1, self.slots)]
        return [self.index(k // self.cores, self.x, lax.rem(k, self.cores)) for k in slots]

    def far_peers(self):
        return [(d, self.index(self.y, lax.rem(self.x + d, AHEAD), self.c)) for d in (2, 1, 3)]

    def greet(self, barrier):
        peers = self.near_peers() + [peer for _, peer in self.far_peers()]
        for peer in peers:
            pl.semaphore_signal(barrier, inc=1, device_id={self.axis: peer}, device_id_type=MESH)
        return len(peers)

    def copy(self, src, dst, phase, leg, peer):
        return pltpu.make_async_remote_copy(
            src_ref=src,
            dst_ref=dst,
            send_sem=self.sems.at[phase, leg, 0],
            recv_sem=self.sems.at[phase, leg, 1],
            device_id={self.axis: peer},
            device_id_type=MESH,
        )

    def start(self, phase):
        rows = pl.ds(0, ROWS[phase])
        self.near[phase, pl.ds(self.slot, 1), rows] = self.send[phase, rows][None]
        for peer in self.near_peers():
            self.copy(self.send.at[phase, rows], self.near.at[phase, self.slot, rows], phase, 0, peer).start()

    def wait(self, ref, phase, leg, count):
        some = ref.at[phase, pl.ds(0, count), pl.ds(0, ROWS[phase])]
        whole = self.copy(some, some, phase, leg, self.near_peers()[0])
        whole.wait_send()
        whole.wait_recv()

    def middle(self, phase, mode):
        rows = pl.ds(0, ROWS[phase])
        self.wait(self.near, phase, 0, self.slots - 1)
        have = [[self.near[phase, y * self.cores + c, rows] for c in range(self.cores)] for y in range(2)]
        sums = [sum(cores[1:], cores[0]) for cores in have]
        if mode == "sum":
            mine = sums[0] + sums[1]
            self.out[phase, 0, rows] = mine
        else:
            earlier = mode == "earlier"

            def chosen(other, own):
                return (other < own if earlier else other > own).astype(F32)

            base = sum(sums[y] * chosen(y, self.y) for y in range(2))
            same = sum(sums[y] * (self.y == y).astype(F32) for y in range(2))
            mine = base
            for y in range(2):
                for c in range(self.cores):
                    mine = mine + have[y][c] * ((self.y == y).astype(F32) * chosen(c, self.c))
            self.out[phase, 0, rows] = base
            self.out[phase, 1, rows] = base + same
        self.far[phase, pl.ds(self.x, 1), rows] = mine[None]
        for d, peer in self.far_peers():
            wrap = (self.x + d) // AHEAD
            which = {"sum": 0, "earlier": 1 - wrap, "later": wrap}[mode]
            self.copy(self.out.at[phase, which, rows], self.far.at[phase, self.x, rows], phase, 1, peer).start()

    def finish(self, phase):
        self.wait(self.far, phase, 1, AHEAD - 1)
        rows = pl.ds(0, ROWS[phase])
        return (self.far[phase, 0, rows] + self.far[phase, 1, rows]) + (
            self.far[phase, 2, rows] + self.far[phase, 3, rows]
        )

    def put(self, phase, row, value):
        self.send[phase, row : row + 1, :] = value


def kernel(
    beams, dets, step_x, step_y,
    axis_hbm, inc_hbm, sig_hbm, yld_hbm, rate_hbm, m1_hbm, live1_hbm, m2_hbm, live2_hbm, conc_hbm,
    out_hbm, dx_ref, dy_ref,
    axis_ref, inc_ref, sig_ref, yld_ref, rate_ref, m1_ref, live1_ref, m2_ref, live2_ref, c_ref,
    load_sems, conc_sems,
    m_ref, q_ref, e1_ref, e2_ref, a1_ref, a2_ref, w_ref, p1_ref, p2_ref, v_ref, d_ref, rows_ref, cols_ref, acc_ref,
    mx_ref, my_ref, lx_ref, ly_ref,
    tx_ref, ty_ref, tab_ref, back_ref, mix_ref, unmix_ref, up_ref, down_ref, left_ref, right_ref,
    wax_ref, way_ref, wcx_ref, wcy_ref,
    bsend, bnear, bout, bfar, bsems, dsend, dnear, dout, dfar, dsems,
):
    def conc_load(z):
        return pltpu.make_async_copy(conc_hbm.at[:, z], c_ref.at[:, z], conc_sems.at[z])

    hbm = (axis_hbm, inc_hbm, sig_hbm, yld_hbm, rate_hbm, m1_hbm, live1_hbm, m2_hbm, live2_hbm)
    vmem = (axis_ref, inc_ref, sig_ref, yld_ref, rate_ref, m1_ref, live1_ref, m2_ref, live2_ref)
    loads = [pltpu.make_async_copy(a, b, load_sems.at[k]) for k, (a, b) in enumerate(zip(hbm, vmem))]
    for load in [conc_load(z) for z in range(ZS)] + loads:
        load.start()
    beam = Ring("beam", beams, bsend, bnear, bout, bfar, bsems)
    det = Ring("det", dets, dsend, dnear, dout, dfar, dsems)
    barrier = pltpu.get_barrier_semaphore()
    greeted = det.greet(barrier) + beam.greet(barrier)

    for ref in (bsend, dsend, cols_ref, mx_ref, my_ref, lx_ref, ly_ref, tx_ref, ty_ref, tab_ref, back_ref):
        ref[...] = jnp.zeros(ref.shape, F32)

    lane = iota((CHUNK, N), 1)

    def over_z(body):
        for z in range(ZS):
            body(z)

    def sweep(body):
        sums = [None] * ZS
        for r in range(0, N, CHUNK):
            acc = jnp.zeros((CHUNK, N), F32)
            for z in range(ZS):
                new, acc = body(z, pl.ds(r, CHUNK), acc)
                new = [jnp.sum(a.reshape(CHUNK // 8, 8, N), 0) for a in new]
                sums[z] = new if r == 0 else [a + b for a, b in zip(sums[z], new)]
            acc_ref[pl.ds(r, CHUNK)] = acc
        return [[jnp.sum(a, 0, keepdims=True) for a in part] for part in sums]

    def turned(rows):
        return jnp.concatenate([rows, jnp.zeros((N - rows.shape[0], N), F32)], 0).T

    def totals(add):
        if add is not None:
            rows_ref[0 : ELEMENTS * ZS] = add

        def body(z, rows, acc):
            if add is None and rows.start == 0:
                conc_load(z).wait()
            sums = []
            cols = cols_ref[rows]
            for e in range(ELEMENTS):
                k = ELEMENTS * z + e
                if add is None:
                    c = c_ref[e, z, rows]
                else:
                    c = d_ref[e, z, rows] + rows_ref[k : k + 1] + cols[:, k : k + 1]
                    c_ref[e, z, rows] = c
                sums.append(c)
                acc = jnp.where(lane == k, jnp.sum(c, 1, keepdims=True), acc)
            return sums, acc

        for z, sums in enumerate(sweep(body)):
            for e, row in enumerate(sums):
                beam.put(0, ELEMENTS * z + e, row)
        dsend[0, 0 : ELEMENTS * ZS] = acc_ref[...].T[0 : ELEMENTS * ZS]

    totals(None)
    pl.semaphore_wait(barrier, greeted)
    det.start(0)
    beam.start(0)
    for load in loads:
        load.wait()

    def tables():
        first = axis_ref[0:1, 0:1] == 0
        one, two = inc_ref[0:1, :], inc_ref[1:2, :]
        s1 = jnp.where(first, one, two)
        s2 = jnp.where(first, two, one)
        scale = -LOG2E * step_y
        sig, yld, rate = sig_ref[...], yld_ref[...], rate_ref[...]
        cols = pl.ds(0, ELEMENTS)
        tab_ref[0:LINES, cols] = scale * sig
        tab_ref[LINES : LINES + 1, cols] = scale * s2
        tab_ref[LINES + 1 : LINES + 2, cols] = scale * s1
        tab_ref[LINES + 2 : FIELDS, cols] = yld
        back_ref[0:LINES, cols] = yld * rate
        back_ref[LINES : 2 * LINES, cols] = -sig * rate
        back_ref[2 * LINES : 2 * LINES + 1, cols] = -s1 * rate
        back_ref[2 * LINES + 1 : FIELDS, cols] = -s2 * rate

        tab, back = tab_ref[...], back_ref[...]
        wide = 8 * ELEMENTS
        pick = one_hot((iota((8 * FIELDS, 32), 0) >> 3) == iota((8 * FIELDS, 32), 1))
        col = iota((N, 256), 1)
        part = (col >= wide).astype(jnp.int32) + (col >= 2 * wide).astype(jnp.int32)
        spread = one_hot(((col - wide * part) >> 3) == iota((N, 256), 0))
        spread = jnp.where(col < 3 * wide, spread, 0.0)
        full = exact(pick, exact(tab, spread))
        shape = (8 * FIELDS, 256)
        full = jnp.where((iota(shape, 0) & 7) == (iota(shape, 1) & 7), full, 0.0)
        high, low = split(full)
        part = iota(shape, 1)
        mix_ref[...] = jnp.where((part >= wide) & (part < 2 * wide), low.astype(F32), high.astype(F32)).astype(BF16)

        pick = one_hot((iota((wide, N), 0) >> 3) == iota((wide, N), 1))
        shape = (wide, 8 * FIELDS)
        spread = one_hot((iota((32, 8 * FIELDS), 1) >> 3) == iota((32, 8 * FIELDS), 0))
        full = exact(exact_nt(pick, back), spread)
        full = jnp.where((iota(shape, 0) & 7) == (iota(shape, 1) & 7), full, 0.0)
        high, low = split(full)
        unmix_ref[0:wide] = high
        unmix_ref[wide : 2 * wide] = low

        r, m = iota((16 * ZS, 32), 0) & 15, iota((16 * ZS, 32), 1)
        rates = exact(one_hot((r == m) & (r < LINES + 2)), tab)
        sums_x = exact(one_hot(m == jnp.where(r < LINES, r + LINES, 2 * LINES)), back)
        sums_y = exact(one_hot(m == jnp.where(r < LINES, r + LINES, 2 * LINES + 1)), back)
        r = iota((16 * ZS, N), 0) & 15
        sums_x = jnp.where(r <= LINES, -step_x * sums_x, 0.0)
        sums_y = jnp.where(r <= LINES, -step_y * sums_y, 0.0)

        def slice_of(shape, dim):
            row = iota(shape, dim)
            return sum((row >= ELEMENTS * z).astype(jnp.int32) for z in range(1, ZS))

        shape = (ELEMENTS * ZS, N)
        place = one_hot(iota(shape, 0) - ELEMENTS * slice_of(shape, 0) == iota(shape, 1))
        shape = wax_ref.shape
        same = (iota(shape, 0) >> 4) == slice_of(shape, 1)
        wax_ref[...] = jnp.where(same, exact_nt(rates * (step_x / step_y), place), 0.0)
        way_ref[...] = jnp.where(same, exact_nt(rates, place), 0.0)
        shape = wcx_ref.shape
        same = slice_of(shape, 0) == (iota(shape, 1) >> 4)
        wcx_ref[...] = jnp.where(same, exact_nt(place, sums_x), 0.0)
        wcy_ref[...] = jnp.where(same, exact_nt(place, sums_y), 0.0)

        r, c = iota((2 * N, N), 0) & (N - 1), iota((2 * N, N), 1)
        up_ref[...] = one_hot(r < c).astype(BF16)
        down_ref[...] = (step_y * one_hot(r > c)).astype(BF16)
        r, c = iota((N, 2 * N), 0), iota((N, 2 * N), 1) & (N - 1)
        left_ref[...] = (step_x / step_y * one_hot(c < r)).astype(BF16)
        right_ref[...] = (step_x * one_hot(c > r)).astype(BF16)
        for z in range(ZS):
            live1 = live1_ref[z : z + 1, :].astype(F32)
            live2 = live2_ref[z : z + 1, :].astype(F32)
            for l in range(LINES):
                k = LINES * z + l
                lx_ref[k : k + 1, :] = live1
                ly_ref[k : k + 1, :] = live2
                mx_ref[k : k + 1, :] = m1_ref[l, z : z + 1, :]
                my_ref[k : k + 1, :] = m2_ref[l, z : z + 1, :]

    tables()

    def groups(body):
        for z in range(ZS):
            for r0 in range(0, N, 32):
                body(z, r0)

    def mix(z, r0):
        parts = []
        for b in range(4):
            high, low = split(c_ref[:, z, pl.ds(r0 + 8 * b, 8), :].reshape(8 * ELEMENTS, N))
            parts.append(jnp.concatenate([high, high, low, jnp.zeros((16, N), BF16)], 0))
        out = dot(mix_ref[...], jnp.concatenate(parts, 1))
        rows = pl.ds(r0, 32)
        for f in range(FIELDS):
            field = jnp.concatenate([out[8 * f : 8 * f + 8, b * N : (b + 1) * N] for b in range(4)], 0)
            if f < LINES + 2:
                high, low = split(field)
                m_ref[z, f, rows, 0:N] = high
                m_ref[z, f, rows, N : 2 * N] = low
            else:
                q_ref[z, f - LINES - 2, rows, :] = field

    def unmix(z, r0):
        highs, lows = [], []
        for b in range(4):
            rows = pl.ds(r0 + 8 * b, 8)
            w = w_ref[z, :, rows, :].reshape(8 * LINES, N)
            v = v_ref[z, :, rows, :].reshape(8 * (LINES + 2), N)
            high, low = split(jnp.concatenate([w, v], 0))
            highs.append(high)
            lows.append(low)
        wide = 8 * ELEMENTS
        one = dot(unmix_ref[...], jnp.concatenate(highs, 1))
        two = dot(unmix_ref[0:wide], jnp.concatenate(lows, 1))
        out = one[0:wide] + (one[wide:] + two)
        for b in range(4):
            rows = pl.ds(r0 + 8 * b, 8)
            d_ref[:, z, rows, :] = c_ref[:, z, rows, :] - out[:, b * N : (b + 1) * N].reshape(ELEMENTS, 8, N)

    def stacked(ref, z, fields):
        value = [ref[z, f] for f in fields]
        high = jnp.concatenate([v[:, 0:N] for v in value], 1)
        low = jnp.concatenate([v[:, N : 2 * N] for v in value], 1)
        return jnp.concatenate([high, low], 0)

    def prefixes(z):
        for l in range(0, LINES, 2):
            out = dot(m_ref[z, l : l + 2].reshape(2 * N, 2 * N), up_ref[...])
            e1_ref[z, l : l + 2] = out.reshape(2, N, N)
            out = dot(left_ref[...], stacked(m_ref, z, (l, l + 1)))
            e2_ref[z, l] = out[:, 0:N]
            e2_ref[z, l + 1] = out[:, N : 2 * N]
        e1_ref[z, LINES] = dot(m_ref[z, LINES], up_ref[...])
        e2_ref[z, LINES] = dot(left_ref[...], stacked(m_ref, z, (LINES + 1,)))

    def suffixes(z):
        for l in range(0, LINES, 2):
            over_y = dot(p1_ref[z, l : l + 2].reshape(2 * N, 2 * N), down_ref[...])
            over_x = dot(right_ref[...], stacked(p2_ref, z, (l, l + 1)))
            v_ref[z, l] = over_y[0:N] + over_x[:, 0:N]
            v_ref[z, l + 1] = over_y[N : 2 * N] + over_x[:, N : 2 * N]
        v_ref[z, LINES] = dot(right_ref[...], stacked(p2_ref, z, (LINES,)))
        v_ref[z, LINES + 1] = dot(p1_ref[z, LINES], down_ref[...])

    def counts(enter_x, enter_y):
        rows_ref[...] = exact(wax_ref[...], enter_x)
        cols_ref[...] = turned(exact(way_ref[...], enter_y))

        def body(z, rows, acc):
            cols = cols_ref[rows]
            k = 16 * z + LINES
            tin1 = jnp.exp2(e2_ref[z, LINES, rows] + rows_ref[k + 1 : k + 2])
            tin2 = jnp.exp2(e1_ref[z, LINES, rows] + cols[:, k : k + 1])
            sums = []
            for l in range(LINES):
                k = 16 * z + l
                a1 = tin1 * jnp.exp2(e1_ref[z, l, rows] + cols[:, k : k + 1])
                a2 = tin2 * jnp.exp2(e2_ref[z, l, rows] + rows_ref[k : k + 1])
                a1_ref[z, l, rows] = a1
                a2_ref[z, l, rows] = a2
                q = q_ref[z, l, rows]
                sums.append(q * a1)
                acc = jnp.where(lane == LINES * z + l, jnp.sum(q * a2, 1, keepdims=True), acc)
            return sums, acc

        for z, sums in enumerate(sweep(body)):
            for l, row in enumerate(sums):
                beam.put(1, LINES * z + l, step_x * row)
        dsend[1] = step_y * acc_ref[...].T[0 : LINES * ZS]

    def residuals(pred1, pred2):
        res1 = lx_ref[...] * (pred1 - mx_ref[...])
        res2 = ly_ref[...] * (pred2 - my_ref[...])
        sum1 = res1 * bsend[1] / step_x
        sum2 = res2 * dsend[1] / step_y
        rows_ref[0 : LINES * ZS] = res1
        cols_ref[...] = turned(res2)

        def body(z, rows, acc):
            cols = cols_ref[rows]
            sums = []
            all1 = jnp.zeros((CHUNK, N), F32)
            all2 = jnp.zeros((CHUNK, N), F32)

            def keep(ref, f, value):
                high, low = split(value)
                ref[z, f, rows, 0:N] = high
                ref[z, f, rows, N : 2 * N] = low

            for l in range(LINES):
                k = LINES * z + l
                w1 = a1_ref[z, l, rows] * rows_ref[k : k + 1]
                w2 = a2_ref[z, l, rows] * cols[:, k : k + 1]
                w_ref[z, l, rows] = w1 + w2
                q = q_ref[z, l, rows]
                p1, p2 = q * w1, q * w2
                all1, all2 = all1 + p1, all2 + p2
                sums.append(p2)
                acc = jnp.where(lane == 16 * z + l, jnp.sum(p1, 1, keepdims=True), acc)
                keep(p1_ref, l, p1)
                keep(p2_ref, l, p2)
            keep(p1_ref, LINES, all2)
            keep(p2_ref, LINES, all1)
            return sums, acc

        for z, sums in enumerate(sweep(body)):
            for l, row in enumerate(sums):
                tx_ref[16 * z + l : 16 * z + l + 1] = row
        ty_ref[...] = acc_ref[...].T[0 : 16 * ZS]
        for z in range(ZS):
            k, part = 16 * z + LINES, slice(LINES * z, LINES * (z + 1))
            tx_ref[k : k + 1] = jnp.sum(sum1[part], 0, keepdims=True)
            ty_ref[k : k + 1] = jnp.sum(sum2[part], 0, keepdims=True)
        bsend[2, 0 : ELEMENTS * ZS] = exact(wcx_ref[...], tx_ref[...])
        dsend[2, 0 : ELEMENTS * ZS] = exact(wcy_ref[...], ty_ref[...])

    def turn(step, carry):
        last = step == STEPS - 1
        groups(mix)
        det.middle(0, "earlier")
        beam.middle(0, "earlier")
        over_z(prefixes)
        enter_y = det.finish(0)
        enter_x = beam.finish(0)
        counts(enter_x, enter_y)
        det.start(1)
        beam.start(1)
        det.middle(1, "sum")
        beam.middle(1, "sum")
        pred2 = det.finish(1)
        pred1 = beam.finish(1)
        residuals(pred1, pred2)
        det.start(2)
        beam.start(2)
        over_z(suffixes)
        det.middle(2, "later")
        beam.middle(2, "later")
        groups(unmix)

        def stores():
            return [pltpu.make_async_copy(d_ref.at[:, z], out_hbm.at[:, z], conc_sems.at[z]) for z in range(ZS)]

        @pl.when(last)
        def leave():
            for store in stores():
                store.start()

        after_y = det.finish(2)
        after_x = beam.finish(2)

        @pl.when(last)
        def left():
            for z in range(ZS):
                part = slice(ELEMENTS * z, ELEMENTS * (z + 1))
                dx_ref[z, 0:ELEMENTS] = after_x[part]
                dy_ref[z, 0:ELEMENTS] = after_y[part]
            for store in stores():
                store.wait()

        @pl.when(jnp.logical_not(last))
        def go_on():
            cols_ref[...] = turned(after_y)
            totals(after_x)
            det.start(0)
            beam.start(0)

        return carry

    lax.fori_loop(0, STEPS, turn, 0)


def close(c_ref, dx_ref, dy_ref, out_ref):
    cols = jnp.concatenate([dy_ref[0], jnp.zeros((N - 16, N), F32)], 0).T
    for e in range(ELEMENTS):
        out_ref[e, 0] = c_ref[e, 0] + dx_ref[0, e : e + 1] + cols[:, e : e + 1]


def solution(mesh):
    beams, dets = mesh.shape["beam"], mesh.shape["det"]

    def shards(conc, inc, sig, yld, rate, axis, m1, live1, m2, live2):
        step_x = 1.0 / (conc.shape[2] * beams)
        step_y = 1.0 / (conc.shape[3] * dets)

        def body(*refs):
            kernel(beams, dets, step_x, step_y, *refs)

        def exchange(count):
            def rows(slots):
                return pltpu.VMEM((3, slots, max(ROWS), N), F32)

            own = pltpu.VMEM((3, max(ROWS), N), F32)
            return [own, rows(count // AHEAD), rows(2), rows(AHEAD), pltpu.SemaphoreType.DMA((3, 2, 2))]

        field = (N, N)
        anywhere = pl.BlockSpec(memory_space=pl.ANY)
        vmem = pl.BlockSpec(memory_space=pltpu.VMEM)
        small = (axis[None], inc, sig, yld, rate[None], m1, live1, m2, live2)
        inner, dx, dy = pl.pallas_call(
            body,
            out_shape=[
                jax.ShapeDtypeStruct(conc.shape, F32),
                jax.ShapeDtypeStruct((ZS, 16, N), F32),
                jax.ShapeDtypeStruct((ZS, 16, N), F32),
            ],
            in_specs=[anywhere] * (len(small) + 1),
            out_specs=[anywhere, vmem, vmem],
            scratch_shapes=[
                *[pltpu.VMEM(a.shape, a.dtype) for a in small + (conc,)],
                pltpu.SemaphoreType.DMA((len(small),)),
                pltpu.SemaphoreType.DMA((ZS,)),
                pltpu.VMEM((ZS, LINES + 2, N, 2 * N), BF16),
                pltpu.VMEM((ZS, LINES) + field, F32),
                *[pltpu.VMEM((ZS, LINES + 1) + field, F32)] * 2,
                *[pltpu.VMEM((ZS, LINES) + field, F32)] * 3,
                *[pltpu.VMEM((ZS, LINES + 1, N, 2 * N), BF16)] * 2,
                pltpu.VMEM((ZS, LINES + 2) + field, F32),
                pltpu.VMEM(conc.shape, F32),
                pltpu.VMEM((16 * ZS, N), F32),
                *[pltpu.VMEM(field, F32)] * 2,
                *[pltpu.VMEM((LINES * ZS, N), F32)] * 4,
                *[pltpu.VMEM((16 * ZS, N), F32)] * 2,
                *[pltpu.VMEM((32, N), F32)] * 2,
                pltpu.VMEM((8 * FIELDS, 2 * N), BF16),
                pltpu.VMEM((16 * ELEMENTS, 8 * FIELDS), BF16),
                *[pltpu.VMEM((2 * N, N), BF16)] * 2,
                *[pltpu.VMEM((N, 2 * N), BF16)] * 2,
                *[pltpu.VMEM((16 * ZS, ELEMENTS * ZS), F32)] * 2,
                *[pltpu.VMEM((ELEMENTS * ZS, 16 * ZS), F32)] * 2,
                *exchange(beams),
                *exchange(dets),
            ],
            compiler_params=pltpu.CompilerParams(
                collective_id=0, has_side_effects=True, vmem_limit_bytes=64 * 1024 * 1024
            ),
        )(*small, conc)

        block = pl.BlockSpec((ELEMENTS, 1, N, N), lambda z: (0, z, 0, 0))
        return pl.pallas_call(
            close,
            out_shape=jax.ShapeDtypeStruct(conc.shape, F32),
            grid=(ZS,),
            in_specs=[
                block,
                pl.BlockSpec((1, 16, N), lambda z: (z, 0, 0)),
                pl.BlockSpec((1, 16, N), lambda z: (z, 0, 0)),
            ],
            out_specs=block,
            compiler_params=pltpu.CompilerParams(vmem_limit_bytes=64 * 1024 * 1024),
        )(inner, dx, dy)

    in_specs = (
        P(None, None, "beam", "det"),
        P(),
        P(),
        P(),
        P(),
        P(),
        P(None, None, "det"),
        P(None, "det"),
        P(None, None, "beam"),
        P(None, "beam"),
    )
    out_specs = P(None, None, "beam", "det")
    return jax.shard_map(shards, mesh=mesh, in_specs=in_specs, out_specs=out_specs, check_vma=False)
```

time: 90.6 us -> 80.4 us (0.89)
  Pallas kernels: 89.6 us -> 79.7 us
    pallas_call x1, Pallas kernels: 84.9 us -> 75.1 us  [shards(): pl.pallas_call(body, out_shape=[jax.ShapeDtypeStruct(conc.shape, F32), ja...]
where the time goes in v7:
time: 80.4 us; the launch traced here: 79.7 us
  Pallas kernels  79.7 us (99%)
    pallas_call x1, Pallas kernels, shards(): pl.pallas_call(body, out_shape=[jax.ShapeDtypeStruct(conc.shape, F32), ja...  75.1 us
    pallas_call x1, Pallas kernels, shards(): pl.pallas_call(close, out_shape=jax.ShapeDtypeStruct(conc.shape, F32), gr...  4.64 us

profile of v7, /device:TPU:0, one launch (start us, length us, event | category | flops | bytes accessed | tf_op | source)
XLA Modules:
  0.0 79.7 jit_solution(8775134039154929938)
XLA Ops:
  0.0 75.1 %shard_map.100 = (f32[10,4,128,128]{3,2,1,0:T(8,128)}, f32[4,16,128]{2,1,0:T(8,128)}, f32[4,16,128]{2,1,0:T(8,128)}) custom-call(s32[1,2]{1,0:T(1,128)} %bitcast.2, f32[2,10]{1,0:T(2,128)} %refs_1_.1, f32[12,10]{1,0:T(8,128)} %refs_2_.1, f32[12,10]{1,0:T(8,128)} %refs_3_.1, f32[1,10]{1,0:T(1,128)} %bitcast.3, f32[12,4,128]{2,1,0:T(4,128)} %refs_5_.1, ...), custom_call_target="tpu_custom_call" | custom-call | tf_op jit(solution)/shard_map/pallas_call | solution.py:520
  75.1 4.6 %shard_map.101 = f32[10,4,128,128]{3,2,1,0:T(8,128)} custom-call(f32[10,4,128,128]{3,2,1,0:T(8,128)} %get-tuple-element.8.c_ref, f32[4,16,128]{2,1,0:T(8,128)} %get-tuple-element.9.dx_ref, f32[4,16,128]{2,1,0:T(8,128)} %get-tuple-element.10.dy_ref), custom_call_target="tpu_custom_call" | custom-call | tf_op jit(solution)/shard_map/pallas_call | solution.py:560

commit v8 on v7

--- a/solution.py
+++ b/solution.py
@@ -16,9 +16,11 @@
 LINES = 12
 ZS = 4
 N = 128
-FIELDS = 26
+PATHS = LINES + 1
+FIELDS = 3 * PATHS + LINES
 CHUNK = 64
 AHEAD = 4
+PARTS = 2 * LINES + 2
 ROWS = (ELEMENTS * ZS, LINES * ZS, ELEMENTS * ZS)
 LOG2E = math.log2(math.e)
 
@@ -145,9 +147,9 @@
     out_hbm, dx_ref, dy_ref,
     axis_ref, inc_ref, sig_ref, yld_ref, rate_ref, m1_ref, live1_ref, m2_ref, live2_ref, c_ref,
     load_sems, conc_sems,
-    m_ref, q_ref, e1_ref, e2_ref, a1_ref, a2_ref, w_ref, p1_ref, p2_ref, v_ref, d_ref, rows_ref, cols_ref, acc_ref,
+    m_ref, q_ref, e1_ref, e2_ref, a1_ref, a2_ref, w_ref, p1_ref, p2_ref, vx_ref, vy_ref, d_ref, rows_ref, cols_ref, acc_ref,
     mx_ref, my_ref, lx_ref, ly_ref,
-    tx_ref, ty_ref, tab_ref, back_ref, mix_ref, unmix_ref, up_ref, down_ref, left_ref, right_ref,
+    tx_ref, ty_ref, tab_ref, back_ref, mix_ref, unmix_ref, up_ref, down_ref, right_ref,
     wax_ref, way_ref, wcx_ref, wcy_ref,
     bsend, bnear, bout, bfar, bsems, dsend, dnear, dout, dfar, dsems,
 ):
@@ -228,39 +230,46 @@
         sig, yld, rate = sig_ref[...], yld_ref[...], rate_ref[...]
         cols = pl.ds(0, ELEMENTS)
         tab_ref[0:LINES, cols] = scale * sig
-        tab_ref[LINES : LINES + 1, cols] = scale * s2
-        tab_ref[LINES + 1 : LINES + 2, cols] = scale * s1
-        tab_ref[LINES + 2 : FIELDS, cols] = yld
+        tab_ref[LINES:PATHS, cols] = scale * s2
+        for k in (PATHS, 2 * PATHS):
+            tab_ref[k : k + LINES, cols] = -LOG2E * step_x * sig
+            tab_ref[k + LINES : k + PATHS, cols] = -LOG2E * step_x * s1
+        tab_ref[3 * PATHS : FIELDS, cols] = yld
         back_ref[0:LINES, cols] = yld * rate
         back_ref[LINES : 2 * LINES, cols] = -sig * rate
         back_ref[2 * LINES : 2 * LINES + 1, cols] = -s1 * rate
-        back_ref[2 * LINES + 1 : FIELDS, cols] = -s2 * rate
+        back_ref[2 * LINES + 1 : 2 * LINES + 2, cols] = -s2 * rate
 
         tab, back = tab_ref[...], back_ref[...]
         wide = 8 * ELEMENTS
-        pick = one_hot((iota((8 * FIELDS, 32), 0) >> 3) == iota((8 * FIELDS, 32), 1))
+        pick = one_hot((iota((8 * FIELDS, 64), 0) >> 3) == iota((8 * FIELDS, 64), 1))
         col = iota((N, 256), 1)
         part = (col >= wide).astype(jnp.int32) + (col >= 2 * wide).astype(jnp.int32)
         spread = one_hot(((col - wide * part) >> 3) == iota((N, 256), 0))
         spread = jnp.where(col < 3 * wide, spread, 0.0)
         full = exact(pick, exact(tab, spread))
         shape = (8 * FIELDS, 256)
-        full = jnp.where((iota(shape, 0) & 7) == (iota(shape, 1) & 7), full, 0.0)
+        field, gap = iota(shape, 0) >> 3, (iota(shape, 0) & 7) - (iota(shape, 1) & 7)
+        within = (field >= PATHS) & (field < 2 * PATHS)
+        whole = (field >= 2 * PATHS) & (field < 3 * PATHS)
+        full = jnp.where(whole | (within & (gap > 0)) | ((gap == 0) & jnp.logical_not(within)), full, 0.0)
         high, low = split(full)
         part = iota(shape, 1)
         mix_ref[...] = jnp.where((part >= wide) & (part < 2 * wide), low.astype(F32), high.astype(F32)).astype(BF16)
 
         pick = one_hot((iota((wide, N), 0) >> 3) == iota((wide, N), 1))
-        shape = (wide, 8 * FIELDS)
-        spread = one_hot((iota((32, 8 * FIELDS), 1) >> 3) == iota((32, 8 * FIELDS), 0))
+        shape = (wide, 8 * PARTS)
+        spread = one_hot((iota((32, 8 * PARTS), 1) >> 3) == iota((32, 8 * PARTS), 0))
         full = exact(exact_nt(pick, back), spread)
         full = jnp.where((iota(shape, 0) & 7) == (iota(shape, 1) & 7), full, 0.0)
         high, low = split(full)
         unmix_ref[0:wide] = high
         unmix_ref[wide : 2 * wide] = low
 
+        r, m = iota((16 * ZS, 64), 0) & 15, iota((16 * ZS, 64), 1)
+        rates_x = exact(one_hot((r < PATHS) & (m == r + PATHS)), tab)
+        rates_y = exact(one_hot((r < PATHS) & (m == r)), tab)
         r, m = iota((16 * ZS, 32), 0) & 15, iota((16 * ZS, 32), 1)
-        rates = exact(one_hot((r == m) & (r < LINES + 2)), tab)
         sums_x = exact(one_hot(m == jnp.where(r < LINES, r + LINES, 2 * LINES)), back)
         sums_y = exact(one_hot(m == jnp.where(r < LINES, r + LINES, 2 * LINES + 1)), back)
         r = iota((16 * ZS, N), 0) & 15
@@ -275,8 +284,8 @@
         place = one_hot(iota(shape, 0) - ELEMENTS * slice_of(shape, 0) == iota(shape, 1))
         shape = wax_ref.shape
         same = (iota(shape, 0) >> 4) == slice_of(shape, 1)
-        wax_ref[...] = jnp.where(same, exact_nt(rates * (step_x / step_y), place), 0.0)
-        way_ref[...] = jnp.where(same, exact_nt(rates, place), 0.0)
+        wax_ref[...] = jnp.where(same, exact_nt(rates_x, place), 0.0)
+        way_ref[...] = jnp.where(same, exact_nt(rates_y, place), 0.0)
         shape = wcx_ref.shape
         same = slice_of(shape, 0) == (iota(shape, 1) >> 4)
         wcx_ref[...] = jnp.where(same, exact_nt(place, sums_x), 0.0)
@@ -286,7 +295,6 @@
         up_ref[...] = one_hot(r < c).astype(BF16)
         down_ref[...] = (step_y * one_hot(r > c)).astype(BF16)
         r, c = iota((N, 2 * N), 0), iota((N, 2 * N), 1) & (N - 1)
-        left_ref[...] = (step_x / step_y * one_hot(c < r)).astype(BF16)
         right_ref[...] = (step_x * one_hot(c > r)).astype(BF16)
         for z in range(ZS):
             live1 = live1_ref[z : z + 1, :].astype(F32)
@@ -300,43 +308,49 @@
 
     tables()
 
-    def groups(body):
-        for z in range(ZS):
-            for r0 in range(0, N, 32):
-                body(z, r0)
-
-    def mix(z, r0):
-        parts = []
-        for b in range(4):
-            high, low = split(c_ref[:, z, pl.ds(r0 + 8 * b, 8), :].reshape(8 * ELEMENTS, N))
-            parts.append(jnp.concatenate([high, high, low, jnp.zeros((16, N), BF16)], 0))
-        out = dot(mix_ref[...], jnp.concatenate(parts, 1))
-        rows = pl.ds(r0, 32)
-        for f in range(FIELDS):
-            field = jnp.concatenate([out[8 * f : 8 * f + 8, b * N : (b + 1) * N] for b in range(4)], 0)
-            if f < LINES + 2:
-                high, low = split(field)
-                m_ref[z, f, rows, 0:N] = high
-                m_ref[z, f, rows, N : 2 * N] = low
-            else:
-                q_ref[z, f - LINES - 2, rows, :] = field
-
-    def unmix(z, r0):
-        highs, lows = [], []
-        for b in range(4):
-            rows = pl.ds(r0 + 8 * b, 8)
-            w = w_ref[z, :, rows, :].reshape(8 * LINES, N)
-            v = v_ref[z, :, rows, :].reshape(8 * (LINES + 2), N)
-            high, low = split(jnp.concatenate([w, v], 0))
-            highs.append(high)
-            lows.append(low)
+    def mix(z):
+        run = [jnp.zeros((8, N), F32)] * PATHS
+        for r0 in range(0, N, 16):
+            parts = []
+            for b in range(2):
+                high, low = split(c_ref[:, z, pl.ds(r0 + 8 * b, 8), :].reshape(8 * ELEMENTS, N))
+                parts.append(jnp.concatenate([high, high, low, jnp.zeros((16, N), BF16)], 0))
+            out = dot(mix_ref[...], jnp.concatenate(parts, 1))
+
+            def field(f):
+                return [out[8 * f : 8 * f + 8, b * N : (b + 1) * N] for b in range(2)]
+
+            rows = pl.ds(r0, 16)
+            for l in range(PATHS):
+                high, low = split(jnp.concatenate(field(l), 0))
+                m_ref[z, l, rows, 0:N] = high
+                m_ref[z, l, rows, N : 2 * N] = low
+                within, whole = field(PATHS + l), field(2 * PATHS + l)
+                for b in range(2):
+                    e2_ref[z, l, pl.ds(r0 + 8 * b, 8)] = run[l] + within[b]
+                    run[l] = run[l] + whole[b]
+            for l in range(LINES):
+                q_ref[z, l, rows, :] = jnp.concatenate(field(3 * PATHS + l), 0)
+
+    def unmix(z):
         wide = 8 * ELEMENTS
-        one = dot(unmix_ref[...], jnp.concatenate(highs, 1))
-        two = dot(unmix_ref[0:wide], jnp.concatenate(lows, 1))
-        out = one[0:wide] + (one[wide:] + two)
-        for b in range(4):
-            rows = pl.ds(r0 + 8 * b, 8)
-            d_ref[:, z, rows, :] = c_ref[:, z, rows, :] - out[:, b * N : (b + 1) * N].reshape(ELEMENTS, 8, N)
+        for r0 in range(0, N, 16):
+            highs, lows = [], []
+            for b in range(2):
+                rows = pl.ds(r0 + 8 * b, 8)
+                w = w_ref[z, :, rows, :].reshape(8 * LINES, N)
+                along_x, along_y = vx_ref[z, :, rows, :], vy_ref[z, :, rows, :]
+                both = (along_x[0:LINES] + along_y[0:LINES]).reshape(8 * LINES, N)
+                high, low = split(jnp.concatenate([w, both, along_x[LINES], along_y[LINES]], 0))
+                highs.append(high)
+                lows.append(low)
+            one = dot(unmix_ref[...], jnp.concatenate(highs, 1))
+            two = dot(unmix_ref[0:wide], jnp.concatenate(lows, 1))
+            out = one[0:wide] + (one[wide:] + two)
+            for b in range(2):
+                rows = pl.ds(r0 + 8 * b, 8)
+                new = c_ref[:, z, rows, :] - out[:, b * N : (b + 1) * N].reshape(ELEMENTS, 8, N)
+                d_ref[:, z, rows, :] = new
 
     def stacked(ref, z, fields):
         value = [ref[z, f] for f in fields]
@@ -345,23 +359,15 @@
         return jnp.concatenate([high, low], 0)
 
     def prefixes(z):
+        e1_ref[z] = dot(m_ref[z].reshape(PATHS * N, 2 * N), up_ref[...]).reshape(PATHS, N, N)
+
+    def suffixes(z):
+        vy_ref[z] = dot(p1_ref[z].reshape(PATHS * N, 2 * N), down_ref[...]).reshape(PATHS, N, N)
         for l in range(0, LINES, 2):
-            out = dot(m_ref[z, l : l + 2].reshape(2 * N, 2 * N), up_ref[...])
-            e1_ref[z, l : l + 2] = out.reshape(2, N, N)
-            out = dot(left_ref[...], stacked(m_ref, z, (l, l + 1)))
-            e2_ref[z, l] = out[:, 0:N]
-            e2_ref[z, l + 1] = out[:, N : 2 * N]
-        e1_ref[z, LINES] = dot(m_ref[z, LINES], up_ref[...])
-        e2_ref[z, LINES] = dot(left_ref[...], stacked(m_ref, z, (LINES + 1,)))
-
-    def suffixes(z):
-        for l in range(0, LINES, 2):
-            over_y = dot(p1_ref[z, l : l + 2].reshape(2 * N, 2 * N), down_ref[...])
             over_x = dot(right_ref[...], stacked(p2_ref, z, (l, l + 1)))
-            v_ref[z, l] = over_y[0:N] + over_x[:, 0:N]
-            v_ref[z, l + 1] = over_y[N : 2 * N] + over_x[:, N : 2 * N]
-        v_ref[z, LINES] = dot(right_ref[...], stacked(p2_ref, z, (LINES,)))
-        v_ref[z, LINES + 1] = dot(p1_ref[z, LINES], down_ref[...])
+            vx_ref[z, l] = over_x[:, 0:N]
+            vx_ref[z, l + 1] = over_x[:, N : 2 * N]
+        vx_ref[z, LINES] = dot(right_ref[...], stacked(p2_ref, z, (LINES,)))
 
     def counts(enter_x, enter_y):
         rows_ref[...] = exact(wax_ref[...], enter_x)
@@ -370,7 +376,7 @@
         def body(z, rows, acc):
             cols = cols_ref[rows]
             k = 16 * z + LINES
-            tin1 = jnp.exp2(e2_ref[z, LINES, rows] + rows_ref[k + 1 : k + 2])
+            tin1 = jnp.exp2(e2_ref[z, LINES, rows] + rows_ref[k : k + 1])
             tin2 = jnp.exp2(e1_ref[z, LINES, rows] + cols[:, k : k + 1])
             sums = []
             for l in range(LINES):
@@ -437,7 +443,7 @@
 
     def turn(step, carry):
         last = step == STEPS - 1
-        groups(mix)
+        over_z(mix)
         det.middle(0, "earlier")
         beam.middle(0, "earlier")
         over_z(prefixes)
@@ -456,7 +462,7 @@
         over_z(suffixes)
         det.middle(2, "later")
         beam.middle(2, "later")
-        groups(unmix)
+        over_z(unmix)
 
         def stores():
             return [pltpu.make_async_copy(d_ref.at[:, z], out_hbm.at[:, z], conc_sems.at[z]) for z in range(ZS)]
@@ -490,10 +496,23 @@
     lax.fori_loop(0, STEPS, turn, 0)
 
 
-def close(c_ref, dx_ref, dy_ref, out_ref):
-    cols = jnp.concatenate([dy_ref[0], jnp.zeros((N - 16, N), F32)], 0).T
-    for e in range(ELEMENTS):
-        out_ref[e, 0] = c_ref[e, 0] + dx_ref[0, e : e + 1] + cols[:, e : e + 1]
+def close(c_hbm, dx_hbm, dy_hbm, out_hbm, c_ref, dx_ref, dy_ref, sems):
+    loads = [pltpu.make_async_copy(a, b, sems.at[k]) for k, (a, b) in enumerate(((dx_hbm, dx_ref), (dy_hbm, dy_ref)))]
+    loads += [pltpu.make_async_copy(c_hbm.at[:, z], c_ref.at[:, z], sems.at[2 + z]) for z in range(ZS)]
+    for load in loads:
+        load.start()
+    loads[0].wait()
+    loads[1].wait()
+    stores = []
+    for z in range(ZS):
+        cols = jnp.concatenate([dy_ref[z], jnp.zeros((N - 16, N), F32)], 0).T
+        loads[2 + z].wait()
+        for e in range(ELEMENTS):
+            c_ref[e, z] = c_ref[e, z] + dx_ref[z, e : e + 1] + cols[:, e : e + 1]
+        stores.append(pltpu.make_async_copy(c_ref.at[:, z], out_hbm.at[:, z], sems.at[2 + z]))
+        stores[z].start()
+    for store in stores:
+        store.wait()
 
 
 def solution(mesh):
@@ -530,22 +549,23 @@
                 *[pltpu.VMEM(a.shape, a.dtype) for a in small + (conc,)],
                 pltpu.SemaphoreType.DMA((len(small),)),
                 pltpu.SemaphoreType.DMA((ZS,)),
-                pltpu.VMEM((ZS, LINES + 2, N, 2 * N), BF16),
+                pltpu.VMEM((ZS, PATHS, N, 2 * N), BF16),
                 pltpu.VMEM((ZS, LINES) + field, F32),
                 *[pltpu.VMEM((ZS, LINES + 1) + field, F32)] * 2,
                 *[pltpu.VMEM((ZS, LINES) + field, F32)] * 3,
                 *[pltpu.VMEM((ZS, LINES + 1, N, 2 * N), BF16)] * 2,
-                pltpu.VMEM((ZS, LINES + 2) + field, F32),
+                *[pltpu.VMEM((ZS, PATHS) + field, F32)] * 2,
                 pltpu.VMEM(conc.shape, F32),
                 pltpu.VMEM((16 * ZS, N), F32),
                 *[pltpu.VMEM(field, F32)] * 2,
                 *[pltpu.VMEM((LINES * ZS, N), F32)] * 4,
                 *[pltpu.VMEM((16 * ZS, N), F32)] * 2,
-                *[pltpu.VMEM((32, N), F32)] * 2,
+                pltpu.VMEM((64, N), F32),
+                pltpu.VMEM((32, N), F32),
                 pltpu.VMEM((8 * FIELDS, 2 * N), BF16),
-                pltpu.VMEM((16 * ELEMENTS, 8 * FIELDS), BF16),
+                pltpu.VMEM((16 * ELEMENTS, 8 * PARTS), BF16),
                 *[pltpu.VMEM((2 * N, N), BF16)] * 2,
-                *[pltpu.VMEM((N, 2 * N), BF16)] * 2,
+                pltpu.VMEM((N, 2 * N), BF16),
                 *[pltpu.VMEM((16 * ZS, ELEMENTS * ZS), F32)] * 2,
                 *[pltpu.VMEM((ELEMENTS * ZS, 16 * ZS), F32)] * 2,
                 *exchange(beams),
@@ -556,17 +576,16 @@
             ),
         )(*small, conc)
 
-        block = pl.BlockSpec((ELEMENTS, 1, N, N), lambda z: (0, z, 0, 0))
         return pl.pallas_call(
             close,
             out_shape=jax.ShapeDtypeStruct(conc.shape, F32),
-            grid=(ZS,),
-            in_specs=[
-                block,
-                pl.BlockSpec((1, 16, N), lambda z: (z, 0, 0)),
-                pl.BlockSpec((1, 16, N), lambda z: (z, 0, 0)),
+            in_specs=[anywhere] * 3,
+            out_specs=anywhere,
+            scratch_shapes=[
+                pltpu.VMEM(conc.shape, F32),
+                *[pltpu.VMEM((ZS, 16, N), F32)] * 2,
+                pltpu.SemaphoreType.DMA((2 + ZS,)),
             ],
-            out_specs=block,
             compiler_params=pltpu.CompilerParams(vmem_limit_bytes=64 * 1024 * 1024),
         )(inner, dx, dy)
 

time: 80.4 us -> 79.1 us (0.984)
  Pallas kernels: 79.7 us -> 78.3 us
    pallas_call x1, Pallas kernels: 4.64 us -> 3.2 us  [shards(): pl.pallas_call(close, out_shape=jax.ShapeDtypeStruct(conc.shape, F32), in...]
where the time goes in v8:
time: 79.1 us; the launch traced here: 78.5 us
  Pallas kernels  78.3 us (99%)
    pallas_call x1, Pallas kernels, shards(): pl.pallas_call(body, out_shape=[jax.ShapeDtypeStruct(conc.shape, F32), ja...  75.1 us
    pallas_call x1, Pallas kernels, shards(): pl.pallas_call(close, out_shape=jax.ShapeDtypeStruct(conc.shape, F32), in...  3.2 us

profile of v8, /device:TPU:0, one launch (start us, length us, event | category | flops | bytes accessed | tf_op | source)
XLA Modules:
  0.0 78.5 jit_solution(12577436460010033708)
XLA Ops:
  0.0 75.1 %shard_map.100 = (f32[10,4,128,128]{3,2,1,0:T(8,128)}, f32[4,16,128]{2,1,0:T(8,128)}, f32[4,16,128]{2,1,0:T(8,128)}) custom-call(s32[1,2]{1,0:T(1,128)} %bitcast.2, f32[2,10]{1,0:T(2,128)} %refs_1_.1, f32[12,10]{1,0:T(8,128)} %refs_2_.1, f32[12,10]{1,0:T(8,128)} %refs_3_.1, f32[1,10]{1,0:T(1,128)} %bitcast.3, f32[12,4,128]{2,1,0:T(4,128)} %refs_5_.1, ...), custom_call_target="tpu_custom_call" | custom-call | tf_op jit(solution)/shard_map/pallas_call | solution.py:539
  75.1 3.2 %shard_map.101 = f32[10,4,128,128]{3,2,1,0:T(8,128)} custom-call(f32[10,4,128,128]{3,2,1,0:T(8,128)} %get-tuple-element.8.c_hbm, f32[4,16,128]{2,1,0:T(8,128)} %get-tuple-element.9.dx_hbm, f32[4,16,128]{2,1,0:T(8,128)} %get-tuple-element.10.dy_hbm), custom_call_target="tpu_custom_call" | custom-call | tf_op jit(solution)/shard_map/pallas_call | solution.py:579

commit v9 on v8

--- a/solution.py
+++ b/solution.py
@@ -46,6 +46,16 @@
     return lax.dot_general(
         a, b, (((1,), (1,)), ((), ())), preferred_element_type=F32, precision=HIGH
     )
+
+
+def triple(table):
+    high, low = split(table)
+    return jnp.concatenate([high, high, low], 1)
+
+
+def rows_of(value):
+    high, low = split(jnp.concatenate([value, jnp.zeros((-value.shape[0] % 128, value.shape[1]), F32)], 0))
+    return jnp.concatenate([high, low, high], 0)
 
 
 def one_hot(condition):
@@ -280,16 +290,19 @@
             row = iota(shape, dim)
             return sum((row >= ELEMENTS * z).astype(jnp.int32) for z in range(1, ZS))
 
-        shape = (ELEMENTS * ZS, N)
-        place = one_hot(iota(shape, 0) - ELEMENTS * slice_of(shape, 0) == iota(shape, 1))
-        shape = wax_ref.shape
+        shape = (N, N)
+        place = one_hot((iota(shape, 0) - ELEMENTS * slice_of(shape, 0) == iota(shape, 1)) & (iota(shape, 1) < ELEMENTS))
+        shape = (16 * ZS, N)
         same = (iota(shape, 0) >> 4) == slice_of(shape, 1)
-        wax_ref[...] = jnp.where(same, exact_nt(rates_x, place), 0.0)
-        way_ref[...] = jnp.where(same, exact_nt(rates_y, place), 0.0)
-        shape = wcx_ref.shape
+        wax_ref[...] = triple(jnp.where(same, exact_nt(rates_x, place), 0.0))
+        way_ref[...] = triple(jnp.where(same, exact_nt(rates_y, place), 0.0))
+        shape = (LINES * ZS, N)
         same = slice_of(shape, 0) == (iota(shape, 1) >> 4)
-        wcx_ref[...] = jnp.where(same, exact_nt(place, sums_x), 0.0)
-        wcy_ref[...] = jnp.where(same, exact_nt(place, sums_y), 0.0)
+        fill = jnp.zeros((N - 16 * ZS, N), F32)
+        for ref, sums in ((wcx_ref, sums_x), (wcy_ref, sums_y)):
+            ref[0 : LINES * ZS] = triple(
+                jnp.where(same, exact_nt(place[0 : LINES * ZS], jnp.concatenate([sums, fill], 0)), 0.0)
+            )
 
         r, c = iota((2 * N, N), 0) & (N - 1), iota((2 * N, N), 1)
         up_ref[...] = one_hot(r < c).astype(BF16)
@@ -307,6 +320,8 @@
                 my_ref[k : k + 1, :] = m2_ref[l, z : z + 1, :]
 
     tables()
+    det.middle(0, "earlier")
+    beam.middle(0, "earlier")
 
     def mix(z):
         run = [jnp.zeros((8, N), F32)] * PATHS
@@ -370,8 +385,8 @@
         vx_ref[z, LINES] = dot(right_ref[...], stacked(p2_ref, z, (LINES,)))
 
     def counts(enter_x, enter_y):
-        rows_ref[...] = exact(wax_ref[...], enter_x)
-        cols_ref[...] = turned(exact(way_ref[...], enter_y))
+        rows_ref[...] = dot(wax_ref[...], rows_of(enter_x))
+        cols_ref[...] = turned(dot(way_ref[...], rows_of(enter_y)))
 
         def body(z, rows, acc):
             cols = cols_ref[rows]
@@ -438,14 +453,20 @@
             k, part = 16 * z + LINES, slice(LINES * z, LINES * (z + 1))
             tx_ref[k : k + 1] = jnp.sum(sum1[part], 0, keepdims=True)
             ty_ref[k : k + 1] = jnp.sum(sum2[part], 0, keepdims=True)
-        bsend[2, 0 : ELEMENTS * ZS] = exact(wcx_ref[...], tx_ref[...])
-        dsend[2, 0 : ELEMENTS * ZS] = exact(wcy_ref[...], ty_ref[...])
+        bsend[2] = dot(wcx_ref[0 : LINES * ZS], rows_of(tx_ref[...]))
+        dsend[2] = dot(wcy_ref[0 : LINES * ZS], rows_of(ty_ref[...]))
 
     def turn(step, carry):
         last = step == STEPS - 1
-        over_z(mix)
-        det.middle(0, "earlier")
-        beam.middle(0, "earlier")
+        for z in range(ZS):
+            mix(z)
+            if z == 1:
+
+                @pl.when(step > 0)
+                def halfway():
+                    det.middle(0, "earlier")
+                    beam.middle(0, "earlier")
+
         over_z(prefixes)
         enter_y = det.finish(0)
         enter_x = beam.finish(0)
@@ -566,8 +587,7 @@
                 pltpu.VMEM((16 * ELEMENTS, 8 * PARTS), BF16),
                 *[pltpu.VMEM((2 * N, N), BF16)] * 2,
                 pltpu.VMEM((N, 2 * N), BF16),
-                *[pltpu.VMEM((16 * ZS, ELEMENTS * ZS), F32)] * 2,
-                *[pltpu.VMEM((ELEMENTS * ZS, 16 * ZS), F32)] * 2,
+                *[pltpu.VMEM((16 * ZS, 3 * N), BF16)] * 4,
                 *exchange(beams),
                 *exchange(dets),
             ],

time: 79.1 us -> 79 us (level)
  no operation moved by 1% of the time
where the time goes in v9:
time: 79 us; the launch traced here: 78.4 us
  Pallas kernels  78.2 us (99%)
    pallas_call x1, Pallas kernels, shards(): pl.pallas_call(body, out_shape=[jax.ShapeDtypeStruct(conc.shape, F32), ja...  75 us
    pallas_call x1, Pallas kernels, shards(): pl.pallas_call(close, out_shape=jax.ShapeDtypeStruct(conc.shape, F32), in...  3.2 us

profile of v9, /device:TPU:0, one launch (start us, length us, event | category | flops | bytes accessed | tf_op | source)
XLA Modules:
  0.0 78.4 jit_solution(1565153330070822445)
XLA Ops:
  0.0 75.0 %shard_map.100 = (f32[10,4,128,128]{3,2,1,0:T(8,128)}, f32[4,16,128]{2,1,0:T(8,128)}, f32[4,16,128]{2,1,0:T(8,128)}) custom-call(s32[1,2]{1,0:T(1,128)} %bitcast.2, f32[2,10]{1,0:T(2,128)} %refs_1_.1, f32[12,10]{1,0:T(8,128)} %refs_2_.1, f32[12,10]{1,0:T(8,128)} %refs_3_.1, f32[1,10]{1,0:T(1,128)} %bitcast.3, f32[12,4,128]{2,1,0:T(4,128)} %refs_5_.1, ...), custom_call_target="tpu_custom_call" | custom-call | tf_op jit(solution)/shard_map/pallas_call | solution.py:560
  75.0 3.2 %shard_map.101 = f32[10,4,128,128]{3,2,1,0:T(8,128)} custom-call(f32[10,4,128,128]{3,2,1,0:T(8,128)} %get-tuple-element.8.c_hbm, f32[4,16,128]{2,1,0:T(8,128)} %get-tuple-element.9.dx_hbm, f32[4,16,128]{2,1,0:T(8,128)} %get-tuple-element.10.dy_hbm), custom_call_target="tpu_custom_call" | custom-call | tf_op jit(solution)/shard_map/pallas_call | solution.py:599

commit v10 on v9

--- a/solution.py
+++ b/solution.py
@@ -21,7 +21,9 @@
 CHUNK = 64
 AHEAD = 4
 PARTS = 2 * LINES + 2
-ROWS = (ELEMENTS * ZS, LINES * ZS, ELEMENTS * ZS)
+GROUPS = 2
+PER = ZS // GROUPS
+ROWS = LINES * PER
 LOG2E = math.log2(math.e)
 
 
@@ -90,36 +92,34 @@
             pl.semaphore_signal(barrier, inc=1, device_id={self.axis: peer}, device_id_type=MESH)
         return len(peers)
 
-    def copy(self, src, dst, phase, leg, peer):
+    def copy(self, src, dst, phase, g, leg, peer):
         return pltpu.make_async_remote_copy(
             src_ref=src,
             dst_ref=dst,
-            send_sem=self.sems.at[phase, leg, 0],
-            recv_sem=self.sems.at[phase, leg, 1],
+            send_sem=self.sems.at[phase, g, leg, 0],
+            recv_sem=self.sems.at[phase, g, leg, 1],
             device_id={self.axis: peer},
             device_id_type=MESH,
         )
 
-    def start(self, phase):
-        rows = pl.ds(0, ROWS[phase])
-        self.near[phase, pl.ds(self.slot, 1), rows] = self.send[phase, rows][None]
+    def start(self, phase, g):
+        self.near[phase, g, pl.ds(self.slot, 1)] = self.send[phase, g][None]
         for peer in self.near_peers():
-            self.copy(self.send.at[phase, rows], self.near.at[phase, self.slot, rows], phase, 0, peer).start()
-
-    def wait(self, ref, phase, leg, count):
-        some = ref.at[phase, pl.ds(0, count), pl.ds(0, ROWS[phase])]
-        whole = self.copy(some, some, phase, leg, self.near_peers()[0])
+            self.copy(self.send.at[phase, g], self.near.at[phase, g, self.slot], phase, g, 0, peer).start()
+
+    def wait(self, ref, phase, g, leg, count):
+        some = ref.at[phase, g, pl.ds(0, count)]
+        whole = self.copy(some, some, phase, g, leg, self.near_peers()[0])
         whole.wait_send()
         whole.wait_recv()
 
-    def middle(self, phase, mode):
-        rows = pl.ds(0, ROWS[phase])
-        self.wait(self.near, phase, 0, self.slots - 1)
-        have = [[self.near[phase, y * self.cores + c, rows] for c in range(self.cores)] for y in range(2)]
+    def middle(self, phase, g, mode):
+        self.wait(self.near, phase, g, 0, self.slots - 1)
+        have = [[self.near[phase, g, y * self.cores + c] for c in range(self.cores)] for y in range(2)]
         sums = [sum(cores[1:], cores[0]) for cores in have]
         if mode == "sum":
             mine = sums[0] + sums[1]
-            self.out[phase, 0, rows] = mine
+            self.out[phase, g, 0] = mine
         else:
             earlier = mode == "earlier"
 
@@ -132,23 +132,21 @@
             for y in range(2):
                 for c in range(self.cores):
                     mine = mine + have[y][c] * ((self.y == y).astype(F32) * chosen(c, self.c))
-            self.out[phase, 0, rows] = base
-            self.out[phase, 1, rows] = base + same
-        self.far[phase, pl.ds(self.x, 1), rows] = mine[None]
+            self.out[phase, g, 0] = base
+            self.out[phase, g, 1] = base + same
+        self.far[phase, g, pl.ds(self.x, 1)] = mine[None]
         for d, peer in self.far_peers():
             wrap = (self.x + d) // AHEAD
             which = {"sum": 0, "earlier": 1 - wrap, "later": wrap}[mode]
-            self.copy(self.out.at[phase, which, rows], self.far.at[phase, self.x, rows], phase, 1, peer).start()
-
-    def finish(self, phase):
-        self.wait(self.far, phase, 1, AHEAD - 1)
-        rows = pl.ds(0, ROWS[phase])
-        return (self.far[phase, 0, rows] + self.far[phase, 1, rows]) + (
-            self.far[phase, 2, rows] + self.far[phase, 3, rows]
-        )
-
-    def put(self, phase, row, value):
-        self.send[phase, row : row + 1, :] = value
+            self.copy(self.out.at[phase, g, which], self.far.at[phase, g, self.x], phase, g, 1, peer).start()
+
+    def finish(self, phase, g):
+        self.wait(self.far, phase, g, 1, AHEAD - 1)
+        far = [self.far[phase, g, x] for x in range(AHEAD)]
+        return (far[0] + far[1]) + (far[2] + far[3])
+
+    def put(self, phase, g, row, value):
+        self.send[phase, g, row : row + 1, :] = value
 
 
 def kernel(
@@ -181,53 +179,65 @@
 
     lane = iota((CHUNK, N), 1)
 
-    def over_z(body):
-        for z in range(ZS):
-            body(z)
-
-    def sweep(body):
-        sums = [None] * ZS
+    def members(g):
+        return range(g * PER, (g + 1) * PER)
+
+    def sweep(g, body):
+        sums = {}
         for r in range(0, N, CHUNK):
             acc = jnp.zeros((CHUNK, N), F32)
-            for z in range(ZS):
+            for z in members(g):
                 new, acc = body(z, pl.ds(r, CHUNK), acc)
                 new = [jnp.sum(a.reshape(CHUNK // 8, 8, N), 0) for a in new]
                 sums[z] = new if r == 0 else [a + b for a, b in zip(sums[z], new)]
-            acc_ref[pl.ds(r, CHUNK)] = acc
-        return [[jnp.sum(a, 0, keepdims=True) for a in part] for part in sums]
+            acc_ref[g, pl.ds(r, CHUNK)] = acc
+        return [[jnp.sum(a, 0, keepdims=True) for a in sums[z]] for z in members(g)]
+
+    def send_off(phase, g):
+        det.start(phase, g)
+        beam.start(phase, g)
+
+    def pass_on(phase, g, mode):
+        det.middle(phase, g, mode)
+        beam.middle(phase, g, mode)
+
+    def take(phase, g):
+        across = det.finish(phase, g)
+        return beam.finish(phase, g), across
 
     def turned(rows):
         return jnp.concatenate([rows, jnp.zeros((N - rows.shape[0], N), F32)], 0).T
 
-    def totals(add):
+    def totals(g, add):
         if add is not None:
-            rows_ref[0 : ELEMENTS * ZS] = add
+            rows_ref[g, 0:ROWS] = add
 
         def body(z, rows, acc):
             if add is None and rows.start == 0:
                 conc_load(z).wait()
             sums = []
-            cols = cols_ref[rows]
+            cols = cols_ref[g, rows]
             for e in range(ELEMENTS):
-                k = ELEMENTS * z + e
+                k = ELEMENTS * (z % PER) + e
                 if add is None:
                     c = c_ref[e, z, rows]
                 else:
-                    c = d_ref[e, z, rows] + rows_ref[k : k + 1] + cols[:, k : k + 1]
+                    c = d_ref[e, z, rows] + rows_ref[g, k : k + 1] + cols[:, k : k + 1]
                     c_ref[e, z, rows] = c
                 sums.append(c)
                 acc = jnp.where(lane == k, jnp.sum(c, 1, keepdims=True), acc)
             return sums, acc
 
-        for z, sums in enumerate(sweep(body)):
+        for z, sums in enumerate(sweep(g, body)):
             for e, row in enumerate(sums):
-                beam.put(0, ELEMENTS * z + e, row)
-        dsend[0, 0 : ELEMENTS * ZS] = acc_ref[...].T[0 : ELEMENTS * ZS]
-
-    totals(None)
+                beam.put(0, g, ELEMENTS * z + e, row)
+        dsend[0, g] = acc_ref[g].T[0:ROWS]
+
+    totals(0, None)
     pl.semaphore_wait(barrier, greeted)
-    det.start(0)
-    beam.start(0)
+    send_off(0, 0)
+    totals(1, None)
+    send_off(0, 1)
     for load in loads:
         load.wait()
 
@@ -276,33 +286,30 @@
         unmix_ref[0:wide] = high
         unmix_ref[wide : 2 * wide] = low
 
-        r, m = iota((16 * ZS, 64), 0) & 15, iota((16 * ZS, 64), 1)
+        r, m = iota((16 * PER, 64), 0) & 15, iota((16 * PER, 64), 1)
         rates_x = exact(one_hot((r < PATHS) & (m == r + PATHS)), tab)
         rates_y = exact(one_hot((r < PATHS) & (m == r)), tab)
-        r, m = iota((16 * ZS, 32), 0) & 15, iota((16 * ZS, 32), 1)
+        r, m = iota((16 * PER, 32), 0) & 15, iota((16 * PER, 32), 1)
         sums_x = exact(one_hot(m == jnp.where(r < LINES, r + LINES, 2 * LINES)), back)
         sums_y = exact(one_hot(m == jnp.where(r < LINES, r + LINES, 2 * LINES + 1)), back)
-        r = iota((16 * ZS, N), 0) & 15
+        r = iota((16 * PER, N), 0) & 15
         sums_x = jnp.where(r <= LINES, -step_x * sums_x, 0.0)
         sums_y = jnp.where(r <= LINES, -step_y * sums_y, 0.0)
 
         def slice_of(shape, dim):
             row = iota(shape, dim)
-            return sum((row >= ELEMENTS * z).astype(jnp.int32) for z in range(1, ZS))
+            return sum((row >= ELEMENTS * z).astype(jnp.int32) for z in range(1, PER))
 
         shape = (N, N)
         place = one_hot((iota(shape, 0) - ELEMENTS * slice_of(shape, 0) == iota(shape, 1)) & (iota(shape, 1) < ELEMENTS))
-        shape = (16 * ZS, N)
+        shape = (16 * PER, N)
         same = (iota(shape, 0) >> 4) == slice_of(shape, 1)
         wax_ref[...] = triple(jnp.where(same, exact_nt(rates_x, place), 0.0))
         way_ref[...] = triple(jnp.where(same, exact_nt(rates_y, place), 0.0))
-        shape = (LINES * ZS, N)
         same = slice_of(shape, 0) == (iota(shape, 1) >> 4)
-        fill = jnp.zeros((N - 16 * ZS, N), F32)
+        fill = jnp.zeros((N - 16 * PER, N), F32)
         for ref, sums in ((wcx_ref, sums_x), (wcy_ref, sums_y)):
-            ref[0 : LINES * ZS] = triple(
-                jnp.where(same, exact_nt(place[0 : LINES * ZS], jnp.concatenate([sums, fill], 0)), 0.0)
-            )
+            ref[...] = triple(jnp.where(same, exact_nt(place[0 : 16 * PER], jnp.concatenate([sums, fill], 0)), 0.0))
 
         r, c = iota((2 * N, N), 0) & (N - 1), iota((2 * N, N), 1)
         up_ref[...] = one_hot(r < c).astype(BF16)
@@ -313,15 +320,14 @@
             live1 = live1_ref[z : z + 1, :].astype(F32)
             live2 = live2_ref[z : z + 1, :].astype(F32)
             for l in range(LINES):
-                k = LINES * z + l
-                lx_ref[k : k + 1, :] = live1
-                ly_ref[k : k + 1, :] = live2
-                mx_ref[k : k + 1, :] = m1_ref[l, z : z + 1, :]
-                my_ref[k : k + 1, :] = m2_ref[l, z : z + 1, :]
+                g, k = z // PER, LINES * (z % PER) + l
+                lx_ref[g, k : k + 1, :] = live1
+                ly_ref[g, k : k + 1, :] = live2
+                mx_ref[g, k : k + 1, :] = m1_ref[l, z : z + 1, :]
+                my_ref[g, k : k + 1, :] = m2_ref[l, z : z + 1, :]
 
     tables()
-    det.middle(0, "earlier")
-    beam.middle(0, "earlier")
+    pass_on(0, 0, "earlier")
 
     def mix(z):
         run = [jnp.zeros((8, N), F32)] * PATHS
@@ -384,42 +390,42 @@
             vx_ref[z, l + 1] = over_x[:, N : 2 * N]
         vx_ref[z, LINES] = dot(right_ref[...], stacked(p2_ref, z, (LINES,)))
 
-    def counts(enter_x, enter_y):
-        rows_ref[...] = dot(wax_ref[...], rows_of(enter_x))
-        cols_ref[...] = turned(dot(way_ref[...], rows_of(enter_y)))
+    def counts(g, enter_x, enter_y):
+        rows_ref[g] = dot(wax_ref[...], rows_of(enter_x))
+        cols_ref[g] = turned(dot(way_ref[...], rows_of(enter_y)))
 
         def body(z, rows, acc):
-            cols = cols_ref[rows]
-            k = 16 * z + LINES
-            tin1 = jnp.exp2(e2_ref[z, LINES, rows] + rows_ref[k : k + 1])
+            cols = cols_ref[g, rows]
+            k = 16 * (z % PER) + LINES
+            tin1 = jnp.exp2(e2_ref[z, LINES, rows] + rows_ref[g, k : k + 1])
             tin2 = jnp.exp2(e1_ref[z, LINES, rows] + cols[:, k : k + 1])
             sums = []
             for l in range(LINES):
-                k = 16 * z + l
+                k = 16 * (z % PER) + l
                 a1 = tin1 * jnp.exp2(e1_ref[z, l, rows] + cols[:, k : k + 1])
-                a2 = tin2 * jnp.exp2(e2_ref[z, l, rows] + rows_ref[k : k + 1])
+                a2 = tin2 * jnp.exp2(e2_ref[z, l, rows] + rows_ref[g, k : k + 1])
                 a1_ref[z, l, rows] = a1
                 a2_ref[z, l, rows] = a2
                 q = q_ref[z, l, rows]
                 sums.append(q * a1)
-                acc = jnp.where(lane == LINES * z + l, jnp.sum(q * a2, 1, keepdims=True), acc)
+                acc = jnp.where(lane == LINES * (z % PER) + l, jnp.sum(q * a2, 1, keepdims=True), acc)
             return sums, acc
 
-        for z, sums in enumerate(sweep(body)):
+        for z, sums in enumerate(sweep(g, body)):
             for l, row in enumerate(sums):
-                beam.put(1, LINES * z + l, step_x * row)
-        dsend[1] = step_y * acc_ref[...].T[0 : LINES * ZS]
-
-    def residuals(pred1, pred2):
-        res1 = lx_ref[...] * (pred1 - mx_ref[...])
-        res2 = ly_ref[...] * (pred2 - my_ref[...])
-        sum1 = res1 * bsend[1] / step_x
-        sum2 = res2 * dsend[1] / step_y
-        rows_ref[0 : LINES * ZS] = res1
-        cols_ref[...] = turned(res2)
+                beam.put(1, g, LINES * z + l, step_x * row)
+        dsend[1, g] = step_y * acc_ref[g].T[0:ROWS]
+
+    def residuals(g, pred1, pred2):
+        res1 = lx_ref[g] * (pred1 - mx_ref[g])
+        res2 = ly_ref[g] * (pred2 - my_ref[g])
+        sum1 = res1 * bsend[1, g] / step_x
+        sum2 = res2 * dsend[1, g] / step_y
+        rows_ref[g, 0:ROWS] = res1
+        cols_ref[g] = turned(res2)
 
         def body(z, rows, acc):
-            cols = cols_ref[rows]
+            cols = cols_ref[g, rows]
             sums = []
             all1 = jnp.zeros((CHUNK, N), F32)
             all2 = jnp.zeros((CHUNK, N), F32)
@@ -430,87 +436,114 @@
                 ref[z, f, rows, N : 2 * N] = low
 
             for l in range(LINES):
-                k = LINES * z + l
-                w1 = a1_ref[z, l, rows] * rows_ref[k : k + 1]
+                k = LINES * (z % PER) + l
+                w1 = a1_ref[z, l, rows] * rows_ref[g, k : k + 1]
                 w2 = a2_ref[z, l, rows] * cols[:, k : k + 1]
                 w_ref[z, l, rows] = w1 + w2
                 q = q_ref[z, l, rows]
                 p1, p2 = q * w1, q * w2
                 all1, all2 = all1 + p1, all2 + p2
                 sums.append(p2)
-                acc = jnp.where(lane == 16 * z + l, jnp.sum(p1, 1, keepdims=True), acc)
+                acc = jnp.where(lane == 16 * (z % PER) + l, jnp.sum(p1, 1, keepdims=True), acc)
                 keep(p1_ref, l, p1)
                 keep(p2_ref, l, p2)
             keep(p1_ref, LINES, all2)
             keep(p2_ref, LINES, all1)
             return sums, acc
 
-        for z, sums in enumerate(sweep(body)):
+        for z, sums in enumerate(sweep(g, body)):
             for l, row in enumerate(sums):
-                tx_ref[16 * z + l : 16 * z + l + 1] = row
-        ty_ref[...] = acc_ref[...].T[0 : 16 * ZS]
-        for z in range(ZS):
+                tx_ref[g, 16 * z + l : 16 * z + l + 1] = row
+        ty_ref[g] = acc_ref[g].T[0 : 16 * PER]
+        for z in range(PER):
             k, part = 16 * z + LINES, slice(LINES * z, LINES * (z + 1))
-            tx_ref[k : k + 1] = jnp.sum(sum1[part], 0, keepdims=True)
-            ty_ref[k : k + 1] = jnp.sum(sum2[part], 0, keepdims=True)
-        bsend[2] = dot(wcx_ref[0 : LINES * ZS], rows_of(tx_ref[...]))
-        dsend[2] = dot(wcy_ref[0 : LINES * ZS], rows_of(ty_ref[...]))
+            tx_ref[g, k : k + 1] = jnp.sum(sum1[part], 0, keepdims=True)
+            ty_ref[g, k : k + 1] = jnp.sum(sum2[part], 0, keepdims=True)
+        bsend[2, g] = dot(wcx_ref[...], rows_of(tx_ref[g]))[0:ROWS]
+        dsend[2, g] = dot(wcy_ref[...], rows_of(ty_ref[g]))[0:ROWS]
+
+    def store(z):
+        return pltpu.make_async_copy(d_ref.at[:, z], out_hbm.at[:, z], conc_sems.at[z])
+
+    def end(g, after_x, after_y):
+        for z in range(PER):
+            part = slice(ELEMENTS * z, ELEMENTS * (z + 1))
+            dx_ref[g * PER + z, 0:ELEMENTS] = after_x[part]
+            dy_ref[g * PER + z, 0:ELEMENTS] = after_y[part]
+
+    def renew(g, after_x, after_y):
+        cols_ref[g] = turned(after_y)
+        totals(g, after_x)
+        send_off(0, g)
 
     def turn(step, carry):
         last = step == STEPS - 1
-        for z in range(ZS):
-            mix(z)
-            if z == 1:
-
-                @pl.when(step > 0)
-                def halfway():
-                    det.middle(0, "earlier")
-                    beam.middle(0, "earlier")
-
-        over_z(prefixes)
-        enter_y = det.finish(0)
-        enter_x = beam.finish(0)
-        counts(enter_x, enter_y)
-        det.start(1)
-        beam.start(1)
-        det.middle(1, "sum")
-        beam.middle(1, "sum")
-        pred2 = det.finish(1)
-        pred1 = beam.finish(1)
-        residuals(pred1, pred2)
-        det.start(2)
-        beam.start(2)
-        over_z(suffixes)
-        det.middle(2, "later")
-        beam.middle(2, "later")
-        over_z(unmix)
-
-        def stores():
-            return [pltpu.make_async_copy(d_ref.at[:, z], out_hbm.at[:, z], conc_sems.at[z]) for z in range(ZS)]
+        more = jnp.logical_not(last)
+
+        def each(stage, g):
+            for z in members(g):
+                stage(z)
+
+        each(mix, 0)
+        pass_on(0, 1, "earlier")
+        each(prefixes, 0)
+        each(mix, 1)
+        counts(0, *take(0, 0))
+        send_off(1, 0)
+        each(prefixes, 1)
+        enter = take(0, 1)
+        pass_on(1, 0, "sum")
+        counts(1, *enter)
+        send_off(1, 1)
+        residuals(0, *take(1, 0))
+        send_off(2, 0)
+        pass_on(1, 1, "sum")
+        each(suffixes, 0)
+        pass_on(2, 0, "later")
+        residuals(1, *take(1, 1))
+        send_off(2, 1)
+        each(unmix, 0)
 
         @pl.when(last)
         def leave():
-            for store in stores():
-                store.start()
-
-        after_y = det.finish(2)
-        after_x = beam.finish(2)
+            for z in members(0):
+                store(z).start()
+
+        after = take(2, 0)
+
+        @pl.when(more)
+        def again():
+            renew(0, *after)
 
         @pl.when(last)
-        def left():
+        def part():
+            end(0, *after)
+
+        pass_on(2, 1, "later")
+        each(suffixes, 1)
+
+        @pl.when(more)
+        def early():
+            pass_on(0, 0, "earlier")
+
+        each(unmix, 1)
+
+        @pl.when(last)
+        def leave_too():
+            for z in members(1):
+                store(z).start()
+
+        rest = take(2, 1)
+
+        @pl.when(more)
+        def once_more():
+            renew(1, *rest)
+
+        @pl.when(last)
+        def finish():
+            end(1, *rest)
             for z in range(ZS):
-                part = slice(ELEMENTS * z, ELEMENTS * (z + 1))
-                dx_ref[z, 0:ELEMENTS] = after_x[part]
-                dy_ref[z, 0:ELEMENTS] = after_y[part]
-            for store in stores():
-                store.wait()
-
-        @pl.when(jnp.logical_not(last))
-        def go_on():
-            cols_ref[...] = turned(after_y)
-            totals(after_x)
-            det.start(0)
-            beam.start(0)
+                store(z).wait()
 
         return carry
 
@@ -547,11 +580,14 @@
             kernel(beams, dets, step_x, step_y, *refs)
 
         def exchange(count):
-            def rows(slots):
-                return pltpu.VMEM((3, slots, max(ROWS), N), F32)
-
-            own = pltpu.VMEM((3, max(ROWS), N), F32)
-            return [own, rows(count // AHEAD), rows(2), rows(AHEAD), pltpu.SemaphoreType.DMA((3, 2, 2))]
+            def rows(*slots):
+                return pltpu.VMEM((3, GROUPS) + slots + (ROWS, N), F32)
+
+            sems = pltpu.SemaphoreType.DMA((3, GROUPS, 2, 2))
+            return [rows(), rows(count // AHEAD), rows(2), rows(AHEAD), sems]
+
+        def grouped(rows):
+            return pltpu.VMEM((GROUPS, rows, N), F32)
 
         field = (N, N)
         anywhere = pl.BlockSpec(memory_space=pl.ANY)
@@ -577,17 +613,17 @@
                 *[pltpu.VMEM((ZS, LINES + 1, N, 2 * N), BF16)] * 2,
                 *[pltpu.VMEM((ZS, PATHS) + field, F32)] * 2,
                 pltpu.VMEM(conc.shape, F32),
-                pltpu.VMEM((16 * ZS, N), F32),
-                *[pltpu.VMEM(field, F32)] * 2,
-                *[pltpu.VMEM((LINES * ZS, N), F32)] * 4,
-                *[pltpu.VMEM((16 * ZS, N), F32)] * 2,
+                grouped(16 * PER),
+                *[grouped(N)] * 2,
+                *[grouped(ROWS)] * 4,
+                *[grouped(16 * PER)] * 2,
                 pltpu.VMEM((64, N), F32),
                 pltpu.VMEM((32, N), F32),
                 pltpu.VMEM((8 * FIELDS, 2 * N), BF16),
                 pltpu.VMEM((16 * ELEMENTS, 8 * PARTS), BF16),
                 *[pltpu.VMEM((2 * N, N), BF16)] * 2,
                 pltpu.VMEM((N, 2 * N), BF16),
-                *[pltpu.VMEM((16 * ZS, 3 * N), BF16)] * 4,
+                *[pltpu.VMEM((16 * PER, 3 * N), BF16)] * 4,
                 *exchange(beams),
                 *exchange(dets),
             ],

time: 79 us -> 77.2 us (0.977)
  Pallas kernels: 78.2 us -> 76.3 us
    pallas_call x1, Pallas kernels: 75 us -> 73.1 us  [shards(): pl.pallas_call(body, out_shape=[jax.ShapeDtypeStruct(conc.shape, F32), ja...]
where the time goes in v10:
time: 77.2 us; the launch traced here: 76.5 us
  Pallas kernels  76.3 us (99%)
    pallas_call x1, Pallas kernels, shards(): pl.pallas_call(body, out_shape=[jax.ShapeDtypeStruct(conc.shape, F32), ja...  73.1 us
    pallas_call x1, Pallas kernels, shards(): pl.pallas_call(close, out_shape=jax.ShapeDtypeStruct(conc.shape, F32), in...  3.2 us

profile of v10, /device:TPU:0, one launch (start us, length us, event | category | flops | bytes accessed | tf_op | source)
XLA Modules:
  0.0 76.5 jit_solution(961557429282889295)
XLA Ops:
  0.0 73.1 %shard_map.100 = (f32[10,4,128,128]{3,2,1,0:T(8,128)}, f32[4,16,128]{2,1,0:T(8,128)}, f32[4,16,128]{2,1,0:T(8,128)}) custom-call(s32[1,2]{1,0:T(1,128)} %bitcast.2, f32[2,10]{1,0:T(2,128)} %refs_1_.1, f32[12,10]{1,0:T(8,128)} %refs_2_.1, f32[12,10]{1,0:T(8,128)} %refs_3_.1, f32[1,10]{1,0:T(1,128)} %bitcast.3, f32[12,4,128]{2,1,0:T(4,128)} %refs_5_.1, ...), custom_call_target="tpu_custom_call" | custom-call | tf_op jit(solution)/shard_map/pallas_call | solution.py:596
  73.1 3.2 %shard_map.101 = f32[10,4,128,128]{3,2,1,0:T(8,128)} custom-call(f32[10,4,128,128]{3,2,1,0:T(8,128)} %get-tuple-element.8.c_hbm, f32[4,16,128]{2,1,0:T(8,128)} %get-tuple-element.9.dx_hbm, f32[4,16,128]{2,1,0:T(8,128)} %get-tuple-element.10.dy_hbm), custom_call_target="tpu_custom_call" | custom-call | tf_op jit(solution)/shard_map/pallas_call | solution.py:635

commit v11 on v10

--- a/solution.py
+++ b/solution.py
@@ -18,12 +18,11 @@
 N = 128
 PATHS = LINES + 1
 FIELDS = 3 * PATHS + LINES
-CHUNK = 64
 AHEAD = 4
 PARTS = 2 * LINES + 2
 GROUPS = 2
 PER = ZS // GROUPS
-ROWS = LINES * PER
+ROWS = 16 * PER
 LOG2E = math.log2(math.e)
 
 
@@ -155,10 +154,10 @@
     out_hbm, dx_ref, dy_ref,
     axis_ref, inc_ref, sig_ref, yld_ref, rate_ref, m1_ref, live1_ref, m2_ref, live2_ref, c_ref,
     load_sems, conc_sems,
-    m_ref, q_ref, e1_ref, e2_ref, a1_ref, a2_ref, w_ref, p1_ref, p2_ref, vx_ref, vy_ref, d_ref, rows_ref, cols_ref, acc_ref,
+    m_ref, q_ref, e1_ref, e2_ref, a1_ref, a2_ref, w_ref, p1_ref, p2_ref, vx_ref, vy_ref, d_ref, rows_ref, cols_ref, spread_ref,
     mx_ref, my_ref, lx_ref, ly_ref,
     tx_ref, ty_ref, tab_ref, back_ref, mix_ref, unmix_ref, up_ref, down_ref, right_ref,
-    wax_ref, way_ref, wcx_ref, wcy_ref,
+    wcx_ref, wcy_ref,
     bsend, bnear, bout, bfar, bsems, dsend, dnear, dout, dfar, dsems,
 ):
     def conc_load(z):
@@ -174,24 +173,13 @@
     barrier = pltpu.get_barrier_semaphore()
     greeted = det.greet(barrier) + beam.greet(barrier)
 
-    for ref in (bsend, dsend, cols_ref, mx_ref, my_ref, lx_ref, ly_ref, tx_ref, ty_ref, tab_ref, back_ref):
+    for ref in (bsend, dsend, mx_ref, my_ref, lx_ref, ly_ref, tx_ref, ty_ref, tab_ref, back_ref):
         ref[...] = jnp.zeros(ref.shape, F32)
 
-    lane = iota((CHUNK, N), 1)
+    lane = iota((N, N), 1)
 
     def members(g):
         return range(g * PER, (g + 1) * PER)
-
-    def sweep(g, body):
-        sums = {}
-        for r in range(0, N, CHUNK):
-            acc = jnp.zeros((CHUNK, N), F32)
-            for z in members(g):
-                new, acc = body(z, pl.ds(r, CHUNK), acc)
-                new = [jnp.sum(a.reshape(CHUNK // 8, 8, N), 0) for a in new]
-                sums[z] = new if r == 0 else [a + b for a, b in zip(sums[z], new)]
-            acc_ref[g, pl.ds(r, CHUNK)] = acc
-        return [[jnp.sum(a, 0, keepdims=True) for a in sums[z]] for z in members(g)]
 
     def send_off(phase, g):
         det.start(phase, g)
@@ -205,39 +193,20 @@
         across = det.finish(phase, g)
         return beam.finish(phase, g), across
 
-    def turned(rows):
-        return jnp.concatenate([rows, jnp.zeros((N - rows.shape[0], N), F32)], 0).T
-
-    def totals(g, add):
-        if add is not None:
-            rows_ref[g, 0:ROWS] = add
-
-        def body(z, rows, acc):
-            if add is None and rows.start == 0:
-                conc_load(z).wait()
-            sums = []
-            cols = cols_ref[g, rows]
-            for e in range(ELEMENTS):
-                k = ELEMENTS * (z % PER) + e
-                if add is None:
-                    c = c_ref[e, z, rows]
-                else:
-                    c = d_ref[e, z, rows] + rows_ref[g, k : k + 1] + cols[:, k : k + 1]
-                    c_ref[e, z, rows] = c
-                sums.append(c)
-                acc = jnp.where(lane == k, jnp.sum(c, 1, keepdims=True), acc)
-            return sums, acc
-
-        for z, sums in enumerate(sweep(g, body)):
-            for e, row in enumerate(sums):
-                beam.put(0, g, ELEMENTS * z + e, row)
-        dsend[0, g] = acc_ref[g].T[0:ROWS]
-
-    totals(0, None)
-    pl.semaphore_wait(barrier, greeted)
-    send_off(0, 0)
-    totals(1, None)
-    send_off(0, 1)
+    def turn_over(g, rows):
+        high = rows.astype(BF16).astype(F32)
+        rest = rows - high
+        middle = rest.astype(BF16).astype(F32)
+        parts = [high, middle, rest - middle, jnp.zeros((N - 3 * ROWS, N), F32)]
+        cols_ref[g] = jnp.concatenate(parts, 0).T.astype(BF16)
+
+    def spread(g, k, count):
+        out = dot(cols_ref[g], spread_ref[:, k * N : (k + count) * N])
+        return [out[:, n * N : (n + 1) * N] for n in range(count)]
+
+    def row_sum(value):
+        return jnp.sum(jnp.sum(value.reshape(N // 8, 8, N), 0), 0, keepdims=True)
+
     for load in loads:
         load.wait()
 
@@ -286,9 +255,6 @@
         unmix_ref[0:wide] = high
         unmix_ref[wide : 2 * wide] = low
 
-        r, m = iota((16 * PER, 64), 0) & 15, iota((16 * PER, 64), 1)
-        rates_x = exact(one_hot((r < PATHS) & (m == r + PATHS)), tab)
-        rates_y = exact(one_hot((r < PATHS) & (m == r)), tab)
         r, m = iota((16 * PER, 32), 0) & 15, iota((16 * PER, 32), 1)
         sums_x = exact(one_hot(m == jnp.where(r < LINES, r + LINES, 2 * LINES)), back)
         sums_y = exact(one_hot(m == jnp.where(r < LINES, r + LINES, 2 * LINES + 1)), back)
@@ -296,38 +262,33 @@
         sums_x = jnp.where(r <= LINES, -step_x * sums_x, 0.0)
         sums_y = jnp.where(r <= LINES, -step_y * sums_y, 0.0)
 
-        def slice_of(shape, dim):
-            row = iota(shape, dim)
-            return sum((row >= ELEMENTS * z).astype(jnp.int32) for z in range(1, PER))
-
-        shape = (N, N)
-        place = one_hot((iota(shape, 0) - ELEMENTS * slice_of(shape, 0) == iota(shape, 1)) & (iota(shape, 1) < ELEMENTS))
-        shape = (16 * PER, N)
-        same = (iota(shape, 0) >> 4) == slice_of(shape, 1)
-        wax_ref[...] = triple(jnp.where(same, exact_nt(rates_x, place), 0.0))
-        way_ref[...] = triple(jnp.where(same, exact_nt(rates_y, place), 0.0))
-        same = slice_of(shape, 0) == (iota(shape, 1) >> 4)
-        fill = jnp.zeros((N - 16 * PER, N), F32)
+        shape = (ROWS, N)
+        place = one_hot(((iota(shape, 0) & 15) == iota(shape, 1)) & (iota(shape, 1) < ELEMENTS))
+        same = (iota(shape, 0) >> 4) == (iota(shape, 1) >> 4)
+        fill = jnp.zeros((N - ROWS, N), F32)
         for ref, sums in ((wcx_ref, sums_x), (wcy_ref, sums_y)):
-            ref[...] = triple(jnp.where(same, exact_nt(place[0 : 16 * PER], jnp.concatenate([sums, fill], 0)), 0.0))
+            ref[...] = triple(jnp.where(same, exact_nt(place, jnp.concatenate([sums, fill], 0)), 0.0))
+        shape = spread_ref.shape
+        k = iota(shape, 0)
+        spread_ref[...] = one_hot((k < 3 * ROWS) & ((k & (ROWS - 1)) == (iota(shape, 1) >> 7))).astype(BF16)
 
         r, c = iota((2 * N, N), 0) & (N - 1), iota((2 * N, N), 1)
-        up_ref[...] = one_hot(r < c).astype(BF16)
-        down_ref[...] = (step_y * one_hot(r > c)).astype(BF16)
+        ones = jnp.ones((2 * N, N), F32)
+        up_ref[...] = jnp.concatenate([one_hot(r < c), ones], 1).astype(BF16)
+        down_ref[...] = jnp.concatenate([step_y * one_hot(r > c), ones], 1).astype(BF16)
         r, c = iota((N, 2 * N), 0), iota((N, 2 * N), 1) & (N - 1)
         right_ref[...] = (step_x * one_hot(c > r)).astype(BF16)
         for z in range(ZS):
             live1 = live1_ref[z : z + 1, :].astype(F32)
             live2 = live2_ref[z : z + 1, :].astype(F32)
             for l in range(LINES):
-                g, k = z // PER, LINES * (z % PER) + l
+                g, k = z // PER, 16 * (z % PER) + l
                 lx_ref[g, k : k + 1, :] = live1
                 ly_ref[g, k : k + 1, :] = live2
                 mx_ref[g, k : k + 1, :] = m1_ref[l, z : z + 1, :]
                 my_ref[g, k : k + 1, :] = m2_ref[l, z : z + 1, :]
 
     tables()
-    pass_on(0, 0, "earlier")
 
     def mix(z):
         run = [jnp.zeros((8, N), F32)] * PATHS
@@ -352,6 +313,8 @@
                     run[l] = run[l] + whole[b]
             for l in range(LINES):
                 q_ref[z, l, rows, :] = jnp.concatenate(field(3 * PATHS + l), 0)
+        for l in range(PATHS):
+            beam.put(0, z // PER, 16 * (z % PER) + l, run[l][0:1])
 
     def unmix(z):
         wide = 8 * ELEMENTS
@@ -379,11 +342,17 @@
         low = jnp.concatenate([v[:, N : 2 * N] for v in value], 1)
         return jnp.concatenate([high, low], 0)
 
-    def prefixes(z):
-        e1_ref[z] = dot(m_ref[z].reshape(PATHS * N, 2 * N), up_ref[...]).reshape(PATHS, N, N)
+    def prefixes(g):
+        acc = jnp.zeros((N, N), F32)
+        for z in members(g):
+            out = dot(m_ref[z].reshape(PATHS * N, 2 * N), up_ref[...])
+            for l in range(PATHS):
+                part = out[l * N : (l + 1) * N]
+                e1_ref[z, l] = part[:, 0:N]
+                acc = jnp.where(lane == 16 * (z % PER) + l, part[:, N : 2 * N], acc)
+        dsend[0, g] = acc.T[0:ROWS]
 
     def suffixes(z):
-        vy_ref[z] = dot(p1_ref[z].reshape(PATHS * N, 2 * N), down_ref[...]).reshape(PATHS, N, N)
         for l in range(0, LINES, 2):
             over_x = dot(right_ref[...], stacked(p2_ref, z, (l, l + 1)))
             vx_ref[z, l] = over_x[:, 0:N]
@@ -391,109 +360,117 @@
         vx_ref[z, LINES] = dot(right_ref[...], stacked(p2_ref, z, (LINES,)))
 
     def counts(g, enter_x, enter_y):
-        rows_ref[g] = dot(wax_ref[...], rows_of(enter_x))
-        cols_ref[g] = turned(dot(way_ref[...], rows_of(enter_y)))
-
-        def body(z, rows, acc):
-            cols = cols_ref[g, rows]
-            k = 16 * (z % PER) + LINES
-            tin1 = jnp.exp2(e2_ref[z, LINES, rows] + rows_ref[g, k : k + 1])
-            tin2 = jnp.exp2(e1_ref[z, LINES, rows] + cols[:, k : k + 1])
-            sums = []
+        rows_ref[g] = enter_x
+        turn_over(g, enter_y)
+        acc = jnp.zeros((N, N), F32)
+        for z in members(g):
+            first = 16 * (z % PER)
+            k = first + LINES
+            tin1 = jnp.exp2(e2_ref[z, LINES] + rows_ref[g, k : k + 1])
+            tin2 = jnp.exp2(e1_ref[z, LINES] + spread(g, k, 1)[0])
             for l in range(LINES):
-                k = 16 * (z % PER) + l
-                a1 = tin1 * jnp.exp2(e1_ref[z, l, rows] + cols[:, k : k + 1])
-                a2 = tin2 * jnp.exp2(e2_ref[z, l, rows] + rows_ref[g, k : k + 1])
-                a1_ref[z, l, rows] = a1
-                a2_ref[z, l, rows] = a2
-                q = q_ref[z, l, rows]
-                sums.append(q * a1)
-                acc = jnp.where(lane == LINES * (z % PER) + l, jnp.sum(q * a2, 1, keepdims=True), acc)
-            return sums, acc
-
-        for z, sums in enumerate(sweep(g, body)):
-            for l, row in enumerate(sums):
-                beam.put(1, g, LINES * z + l, step_x * row)
-        dsend[1, g] = step_y * acc_ref[g].T[0:ROWS]
+                k = first + l
+                if l % 2 == 0:
+                    cols = spread(g, k, 2)
+                a1 = tin1 * jnp.exp2(e1_ref[z, l] + cols[l % 2])
+                a2 = tin2 * jnp.exp2(e2_ref[z, l] + rows_ref[g, k : k + 1])
+                a1_ref[z, l] = a1
+                a2_ref[z, l] = a2
+                q = q_ref[z, l]
+                beam.put(1, g, k, step_x * row_sum(q * a1))
+                acc = jnp.where(lane == k, jnp.sum(q * a2, 1, keepdims=True), acc)
+        dsend[1, g] = step_y * acc.T[0:ROWS]
 
     def residuals(g, pred1, pred2):
         res1 = lx_ref[g] * (pred1 - mx_ref[g])
         res2 = ly_ref[g] * (pred2 - my_ref[g])
         sum1 = res1 * bsend[1, g] / step_x
         sum2 = res2 * dsend[1, g] / step_y
-        rows_ref[g, 0:ROWS] = res1
-        cols_ref[g] = turned(res2)
-
-        def body(z, rows, acc):
-            cols = cols_ref[g, rows]
-            sums = []
-            all1 = jnp.zeros((CHUNK, N), F32)
-            all2 = jnp.zeros((CHUNK, N), F32)
-
-            def keep(ref, f, value):
-                high, low = split(value)
-                ref[z, f, rows, 0:N] = high
-                ref[z, f, rows, N : 2 * N] = low
-
+        rows_ref[g] = res1
+        turn_over(g, res2)
+
+        def keep(ref, z, f, value):
+            high, low = split(value)
+            ref[z, f, :, 0:N] = high
+            ref[z, f, :, N : 2 * N] = low
+
+        acc = jnp.zeros((N, N), F32)
+        for z in members(g):
+            all1 = jnp.zeros((N, N), F32)
+            all2 = jnp.zeros((N, N), F32)
             for l in range(LINES):
-                k = LINES * (z % PER) + l
-                w1 = a1_ref[z, l, rows] * rows_ref[g, k : k + 1]
-                w2 = a2_ref[z, l, rows] * cols[:, k : k + 1]
-                w_ref[z, l, rows] = w1 + w2
-                q = q_ref[z, l, rows]
+                k = 16 * (z % PER) + l
+                if l % 2 == 0:
+                    cols = spread(g, k, 2)
+                w1 = a1_ref[z, l] * rows_ref[g, k : k + 1]
+                w2 = a2_ref[z, l] * cols[l % 2]
+                w_ref[z, l] = w1 + w2
+                q = q_ref[z, l]
                 p1, p2 = q * w1, q * w2
                 all1, all2 = all1 + p1, all2 + p2
-                sums.append(p2)
-                acc = jnp.where(lane == 16 * (z % PER) + l, jnp.sum(p1, 1, keepdims=True), acc)
-                keep(p1_ref, l, p1)
-                keep(p2_ref, l, p2)
-            keep(p1_ref, LINES, all2)
-            keep(p2_ref, LINES, all1)
-            return sums, acc
-
-        for z, sums in enumerate(sweep(g, body)):
-            for l, row in enumerate(sums):
-                tx_ref[g, 16 * z + l : 16 * z + l + 1] = row
-        ty_ref[g] = acc_ref[g].T[0 : 16 * PER]
+                tx_ref[g, k : k + 1] = row_sum(p2)
+                keep(p1_ref, z, l, p1)
+                keep(p2_ref, z, l, p2)
+            keep(p1_ref, z, LINES, all2)
+            keep(p2_ref, z, LINES, all1)
+            out = dot(p1_ref[z].reshape(PATHS * N, 2 * N), down_ref[...])
+            for l in range(PATHS):
+                part = out[l * N : (l + 1) * N]
+                vy_ref[z, l] = part[:, 0:N]
+                if l < LINES:
+                    acc = jnp.where(lane == 16 * (z % PER) + l, part[:, N : 2 * N], acc)
+        ty_ref[g] = acc.T[0:ROWS]
         for z in range(PER):
-            k, part = 16 * z + LINES, slice(LINES * z, LINES * (z + 1))
+            k, part = 16 * z + LINES, slice(16 * z, 16 * (z + 1))
             tx_ref[g, k : k + 1] = jnp.sum(sum1[part], 0, keepdims=True)
             ty_ref[g, k : k + 1] = jnp.sum(sum2[part], 0, keepdims=True)
-        bsend[2, g] = dot(wcx_ref[...], rows_of(tx_ref[g]))[0:ROWS]
-        dsend[2, g] = dot(wcy_ref[...], rows_of(ty_ref[g]))[0:ROWS]
+        bsend[2, g] = dot(wcx_ref[...], rows_of(tx_ref[g]))
+        dsend[2, g] = dot(wcy_ref[...], rows_of(ty_ref[g]))
 
     def store(z):
         return pltpu.make_async_copy(d_ref.at[:, z], out_hbm.at[:, z], conc_sems.at[z])
 
     def end(g, after_x, after_y):
         for z in range(PER):
-            part = slice(ELEMENTS * z, ELEMENTS * (z + 1))
-            dx_ref[g * PER + z, 0:ELEMENTS] = after_x[part]
-            dy_ref[g * PER + z, 0:ELEMENTS] = after_y[part]
+            dx_ref[g * PER + z] = after_x[16 * z : 16 * (z + 1)]
+            dy_ref[g * PER + z] = after_y[16 * z : 16 * (z + 1)]
 
     def renew(g, after_x, after_y):
-        cols_ref[g] = turned(after_y)
-        totals(g, after_x)
-        send_off(0, g)
+        rows_ref[g] = after_x
+        turn_over(g, after_y)
+        for z in members(g):
+            for e in range(ELEMENTS):
+                k = 16 * (z % PER) + e
+                if e % 2 == 0:
+                    cols = spread(g, k, 2)
+                c_ref[e, z] = d_ref[e, z] + rows_ref[g, k : k + 1] + cols[e % 2]
+
+    def each(stage, g):
+        for z in members(g):
+            stage(z)
+
+    def opening(g):
+        each(mix, g)
+        prefixes(g)
+
+    for z in range(ZS):
+        conc_load(z).wait()
+    opening(0)
+    pl.semaphore_wait(barrier, greeted)
+    send_off(0, 0)
 
     def turn(step, carry):
         last = step == STEPS - 1
         more = jnp.logical_not(last)
-
-        def each(stage, g):
-            for z in members(g):
-                stage(z)
-
-        each(mix, 0)
-        pass_on(0, 1, "earlier")
-        each(prefixes, 0)
         each(mix, 1)
+        pass_on(0, 0, "earlier")
+        prefixes(1)
+        send_off(0, 1)
         counts(0, *take(0, 0))
         send_off(1, 0)
-        each(prefixes, 1)
-        enter = take(0, 1)
+        pass_on(0, 1, "earlier")
         pass_on(1, 0, "sum")
-        counts(1, *enter)
+        counts(1, *take(0, 1))
         send_off(1, 1)
         residuals(0, *take(1, 0))
         send_off(2, 0)
@@ -514,6 +491,8 @@
         @pl.when(more)
         def again():
             renew(0, *after)
+            opening(0)
+            send_off(0, 0)
 
         @pl.when(last)
         def part():
@@ -521,11 +500,6 @@
 
         pass_on(2, 1, "later")
         each(suffixes, 1)
-
-        @pl.when(more)
-        def early():
-            pass_on(0, 0, "earlier")
-
         each(unmix, 1)
 
         @pl.when(last)
@@ -613,17 +587,18 @@
                 *[pltpu.VMEM((ZS, LINES + 1, N, 2 * N), BF16)] * 2,
                 *[pltpu.VMEM((ZS, PATHS) + field, F32)] * 2,
                 pltpu.VMEM(conc.shape, F32),
-                grouped(16 * PER),
-                *[grouped(N)] * 2,
+                grouped(ROWS),
+                pltpu.VMEM((GROUPS, N, N), BF16),
+                pltpu.VMEM((N, ROWS * N), BF16),
                 *[grouped(ROWS)] * 4,
-                *[grouped(16 * PER)] * 2,
+                *[grouped(ROWS)] * 2,
                 pltpu.VMEM((64, N), F32),
                 pltpu.VMEM((32, N), F32),
                 pltpu.VMEM((8 * FIELDS, 2 * N), BF16),
                 pltpu.VMEM((16 * ELEMENTS, 8 * PARTS), BF16),
-                *[pltpu.VMEM((2 * N, N), BF16)] * 2,
+                *[pltpu.VMEM((2 * N, 2 * N), BF16)] * 2,
                 pltpu.VMEM((N, 2 * N), BF16),
-                *[pltpu.VMEM((16 * PER, 3 * N), BF16)] * 4,
+                *[pltpu.VMEM((ROWS, 3 * N), BF16)] * 2,
                 *exchange(beams),
                 *exchange(dets),
             ],

time: 77.2 us -> 71.2 us (0.922)
  Pallas kernels: 76.3 us -> 70.8 us
    pallas_call x1, Pallas kernels: 73.1 us -> 67.6 us  [shards(): pl.pallas_call(body, out_shape=[jax.ShapeDtypeStruct(conc.shape, F32), ja...]
where the time goes in v11:
time: 71.2 us; the launch traced here: 70.9 us
  Pallas kernels  70.8 us (99%)
    pallas_call x1, Pallas kernels, shards(): pl.pallas_call(body, out_shape=[jax.ShapeDtypeStruct(conc.shape, F32), ja...  67.6 us
    pallas_call x1, Pallas kernels, shards(): pl.pallas_call(close, out_shape=jax.ShapeDtypeStruct(conc.shape, F32), in...  3.2 us

profile of v11, /device:TPU:0, one launch (start us, length us, event | category | flops | bytes accessed | tf_op | source)
XLA Modules:
  0.0 70.9 jit_solution(14143164754085675484)
XLA Ops:
  0.0 67.6 %shard_map.100 = (f32[10,4,128,128]{3,2,1,0:T(8,128)}, f32[4,16,128]{2,1,0:T(8,128)}, f32[4,16,128]{2,1,0:T(8,128)}) custom-call(s32[1,2]{1,0:T(1,128)} %bitcast.2, f32[2,10]{1,0:T(2,128)} %refs_1_.1, f32[12,10]{1,0:T(8,128)} %refs_2_.1, f32[12,10]{1,0:T(8,128)} %refs_3_.1, f32[1,10]{1,0:T(1,128)} %bitcast.3, f32[12,4,128]{2,1,0:T(4,128)} %refs_5_.1, ...), custom_call_target="tpu_custom_call" | custom-call | tf_op jit(solution)/shard_map/pallas_call | solution.py:570
  67.6 3.2 %shard_map.101 = f32[10,4,128,128]{3,2,1,0:T(8,128)} custom-call(f32[10,4,128,128]{3,2,1,0:T(8,128)} %get-tuple-element.8.c_hbm, f32[4,16,128]{2,1,0:T(8,128)} %get-tuple-element.9.dx_hbm, f32[4,16,128]{2,1,0:T(8,128)} %get-tuple-element.10.dy_hbm), custom_call_target="tpu_custom_call" | custom-call | tf_op jit(solution)/shard_map/pallas_call | solution.py:610

commit v12 on v11

--- a/solution.py
+++ b/solution.py
@@ -23,6 +23,7 @@
 GROUPS = 2
 PER = ZS // GROUPS
 ROWS = 16 * PER
+SIZES = (ROWS, LINES * PER, LINES * PER)
 LOG2E = math.log2(math.e)
 
 
@@ -61,6 +62,10 @@
 
 def one_hot(condition):
     return jnp.where(condition, 1.0, 0.0).astype(F32)
+
+
+def spot(z, k):
+    return PER * k + z % PER
 
 
 class Ring:
@@ -79,7 +84,7 @@
         return (y * AHEAD + x) * self.cores + c
 
     def near_peers(self):
-        slots = [lax.rem(self.slot + d, self.slots) for d in range(1, self.slots)]
+        slots = [lax.rem(self.slot + d, self.slots) for d in ((2, 1, 3) if self.slots == 4 else (1,))]
         return [self.index(k // self.cores, self.x, lax.rem(k, self.cores)) for k in slots]
 
     def far_peers(self):
@@ -102,23 +107,26 @@
         )
 
     def start(self, phase, g):
-        self.near[phase, g, pl.ds(self.slot, 1)] = self.send[phase, g][None]
+        rows = pl.ds(0, SIZES[phase])
         for peer in self.near_peers():
-            self.copy(self.send.at[phase, g], self.near.at[phase, g, self.slot], phase, g, 0, peer).start()
+            src, dst = self.send.at[phase, g, rows], self.near.at[phase, g, self.slot, rows]
+            self.copy(src, dst, phase, g, 0, peer).start()
+        self.near[phase, g, pl.ds(self.slot, 1), rows] = self.send[phase, g, rows][None]
 
     def wait(self, ref, phase, g, leg, count):
-        some = ref.at[phase, g, pl.ds(0, count)]
+        some = ref.at[phase, g, pl.ds(0, count), pl.ds(0, SIZES[phase])]
         whole = self.copy(some, some, phase, g, leg, self.near_peers()[0])
         whole.wait_send()
         whole.wait_recv()
 
     def middle(self, phase, g, mode):
         self.wait(self.near, phase, g, 0, self.slots - 1)
-        have = [[self.near[phase, g, y * self.cores + c] for c in range(self.cores)] for y in range(2)]
+        rows = pl.ds(0, SIZES[phase])
+        have = [[self.near[phase, g, y * self.cores + c, rows] for c in range(self.cores)] for y in range(2)]
         sums = [sum(cores[1:], cores[0]) for cores in have]
         if mode == "sum":
             mine = sums[0] + sums[1]
-            self.out[phase, g, 0] = mine
+            self.out[phase, g, 0, rows] = mine
         else:
             earlier = mode == "earlier"
 
@@ -131,17 +139,18 @@
             for y in range(2):
                 for c in range(self.cores):
                     mine = mine + have[y][c] * ((self.y == y).astype(F32) * chosen(c, self.c))
-            self.out[phase, g, 0] = base
-            self.out[phase, g, 1] = base + same
-        self.far[phase, g, pl.ds(self.x, 1)] = mine[None]
+            self.out[phase, g, 0, rows] = base
+            self.out[phase, g, 1, rows] = base + same
         for d, peer in self.far_peers():
             wrap = (self.x + d) // AHEAD
             which = {"sum": 0, "earlier": 1 - wrap, "later": wrap}[mode]
-            self.copy(self.out.at[phase, g, which], self.far.at[phase, g, self.x], phase, g, 1, peer).start()
+            src, dst = self.out.at[phase, g, which, rows], self.far.at[phase, g, self.x, rows]
+            self.copy(src, dst, phase, g, 1, peer).start()
+        self.far[phase, g, pl.ds(self.x, 1), rows] = mine[None]
 
     def finish(self, phase, g):
         self.wait(self.far, phase, g, 1, AHEAD - 1)
-        far = [self.far[phase, g, x] for x in range(AHEAD)]
+        far = [self.far[phase, g, x, pl.ds(0, SIZES[phase])] for x in range(AHEAD)]
         return (far[0] + far[1]) + (far[2] + far[3])
 
     def put(self, phase, g, row, value):
@@ -194,13 +203,15 @@
         return beam.finish(phase, g), across
 
     def turn_over(g, rows):
+        rows = jnp.concatenate([rows, jnp.zeros((ROWS - rows.shape[0], N), F32)], 0) if rows.shape[0] < ROWS else rows
         high = rows.astype(BF16).astype(F32)
         rest = rows - high
         middle = rest.astype(BF16).astype(F32)
         parts = [high, middle, rest - middle, jnp.zeros((N - 3 * ROWS, N), F32)]
         cols_ref[g] = jnp.concatenate(parts, 0).T.astype(BF16)
 
-    def spread(g, k, count):
+    def spread(g, z, k, count):
+        k += 16 * (z % PER)
         out = dot(cols_ref[g], spread_ref[:, k * N : (k + count) * N])
         return [out[:, n * N : (n + 1) * N] for n in range(count)]
 
@@ -263,14 +274,16 @@
         sums_y = jnp.where(r <= LINES, -step_y * sums_y, 0.0)
 
         shape = (ROWS, N)
-        place = one_hot(((iota(shape, 0) & 15) == iota(shape, 1)) & (iota(shape, 1) < ELEMENTS))
-        same = (iota(shape, 0) >> 4) == (iota(shape, 1) >> 4)
+        place = one_hot(((iota(shape, 0) // PER) == iota(shape, 1)) & (iota(shape, 1) < ELEMENTS))
+        same = (iota(shape, 0) & (PER - 1)) == (iota(shape, 1) >> 4)
         fill = jnp.zeros((N - ROWS, N), F32)
         for ref, sums in ((wcx_ref, sums_x), (wcy_ref, sums_y)):
             ref[...] = triple(jnp.where(same, exact_nt(place, jnp.concatenate([sums, fill], 0)), 0.0))
         shape = spread_ref.shape
         k = iota(shape, 0)
-        spread_ref[...] = one_hot((k < 3 * ROWS) & ((k & (ROWS - 1)) == (iota(shape, 1) >> 7))).astype(BF16)
+        wanted = iota(shape, 1) >> 7
+        wanted = PER * (wanted & 15) + (wanted >> 4)
+        spread_ref[...] = one_hot((k < 3 * ROWS) & ((k & (ROWS - 1)) == wanted)).astype(BF16)
 
         r, c = iota((2 * N, N), 0) & (N - 1), iota((2 * N, N), 1)
         ones = jnp.ones((2 * N, N), F32)
@@ -282,7 +295,7 @@
             live1 = live1_ref[z : z + 1, :].astype(F32)
             live2 = live2_ref[z : z + 1, :].astype(F32)
             for l in range(LINES):
-                g, k = z // PER, 16 * (z % PER) + l
+                g, k = z // PER, spot(z, l)
                 lx_ref[g, k : k + 1, :] = live1
                 ly_ref[g, k : k + 1, :] = live2
                 mx_ref[g, k : k + 1, :] = m1_ref[l, z : z + 1, :]
@@ -314,7 +327,7 @@
             for l in range(LINES):
                 q_ref[z, l, rows, :] = jnp.concatenate(field(3 * PATHS + l), 0)
         for l in range(PATHS):
-            beam.put(0, z // PER, 16 * (z % PER) + l, run[l][0:1])
+            beam.put(0, z // PER, spot(z, l), run[l][0:1])
 
     def unmix(z):
         wide = 8 * ELEMENTS
@@ -349,7 +362,7 @@
             for l in range(PATHS):
                 part = out[l * N : (l + 1) * N]
                 e1_ref[z, l] = part[:, 0:N]
-                acc = jnp.where(lane == 16 * (z % PER) + l, part[:, N : 2 * N], acc)
+                acc = jnp.where(lane == spot(z, l), part[:, N : 2 * N], acc)
         dsend[0, g] = acc.T[0:ROWS]
 
     def suffixes(z):
@@ -364,14 +377,13 @@
         turn_over(g, enter_y)
         acc = jnp.zeros((N, N), F32)
         for z in members(g):
-            first = 16 * (z % PER)
-            k = first + LINES
+            k = spot(z, LINES)
             tin1 = jnp.exp2(e2_ref[z, LINES] + rows_ref[g, k : k + 1])
-            tin2 = jnp.exp2(e1_ref[z, LINES] + spread(g, k, 1)[0])
+            tin2 = jnp.exp2(e1_ref[z, LINES] + spread(g, z, LINES, 1)[0])
             for l in range(LINES):
-                k = first + l
+                k = spot(z, l)
                 if l % 2 == 0:
-                    cols = spread(g, k, 2)
+                    cols = spread(g, z, l, 2)
                 a1 = tin1 * jnp.exp2(e1_ref[z, l] + cols[l % 2])
                 a2 = tin2 * jnp.exp2(e2_ref[z, l] + rows_ref[g, k : k + 1])
                 a1_ref[z, l] = a1
@@ -382,11 +394,12 @@
         dsend[1, g] = step_y * acc.T[0:ROWS]
 
     def residuals(g, pred1, pred2):
-        res1 = lx_ref[g] * (pred1 - mx_ref[g])
-        res2 = ly_ref[g] * (pred2 - my_ref[g])
-        sum1 = res1 * bsend[1, g] / step_x
-        sum2 = res2 * dsend[1, g] / step_y
-        rows_ref[g] = res1
+        used = pl.ds(0, LINES * PER)
+        res1 = lx_ref[g, used] * (pred1 - mx_ref[g, used])
+        res2 = ly_ref[g, used] * (pred2 - my_ref[g, used])
+        sum1 = res1 * bsend[1, g, used] / step_x
+        sum2 = res2 * dsend[1, g, used] / step_y
+        rows_ref[g, used] = res1
         turn_over(g, res2)
 
         def keep(ref, z, f, value):
@@ -401,8 +414,8 @@
             for l in range(LINES):
                 k = 16 * (z % PER) + l
                 if l % 2 == 0:
-                    cols = spread(g, k, 2)
-                w1 = a1_ref[z, l] * rows_ref[g, k : k + 1]
+                    cols = spread(g, z, l, 2)
+                w1 = a1_ref[z, l] * rows_ref[g, spot(z, l) : spot(z, l) + 1]
                 w2 = a2_ref[z, l] * cols[l % 2]
                 w_ref[z, l] = w1 + w2
                 q = q_ref[z, l]
@@ -421,9 +434,10 @@
                     acc = jnp.where(lane == 16 * (z % PER) + l, part[:, N : 2 * N], acc)
         ty_ref[g] = acc.T[0:ROWS]
         for z in range(PER):
-            k, part = 16 * z + LINES, slice(16 * z, 16 * (z + 1))
-            tx_ref[g, k : k + 1] = jnp.sum(sum1[part], 0, keepdims=True)
-            ty_ref[g, k : k + 1] = jnp.sum(sum2[part], 0, keepdims=True)
+            k = 16 * z + LINES
+            own = (iota((LINES * PER, N), 0) & (PER - 1)) == z
+            tx_ref[g, k : k + 1] = jnp.sum(jnp.where(own, sum1, 0.0), 0, keepdims=True)
+            ty_ref[g, k : k + 1] = jnp.sum(jnp.where(own, sum2, 0.0), 0, keepdims=True)
         bsend[2, g] = dot(wcx_ref[...], rows_of(tx_ref[g]))
         dsend[2, g] = dot(wcy_ref[...], rows_of(ty_ref[g]))
 
@@ -431,18 +445,16 @@
         return pltpu.make_async_copy(d_ref.at[:, z], out_hbm.at[:, z], conc_sems.at[z])
 
     def end(g, after_x, after_y):
-        for z in range(PER):
-            dx_ref[g * PER + z] = after_x[16 * z : 16 * (z + 1)]
-            dy_ref[g * PER + z] = after_y[16 * z : 16 * (z + 1)]
+        dx_ref[g], dy_ref[g] = after_x, after_y
 
     def renew(g, after_x, after_y):
-        rows_ref[g] = after_x
+        rows_ref[g, 0 : SIZES[2]] = after_x
         turn_over(g, after_y)
         for z in members(g):
             for e in range(ELEMENTS):
-                k = 16 * (z % PER) + e
+                k = spot(z, e)
                 if e % 2 == 0:
-                    cols = spread(g, k, 2)
+                    cols = spread(g, z, e, 2)
                 c_ref[e, z] = d_ref[e, z] + rows_ref[g, k : k + 1] + cols[e % 2]
 
     def each(stage, g):
@@ -463,7 +475,11 @@
         last = step == STEPS - 1
         more = jnp.logical_not(last)
         each(mix, 1)
-        pass_on(0, 0, "earlier")
+
+        @pl.when(step == 0)
+        def late():
+            pass_on(0, 0, "earlier")
+
         prefixes(1)
         send_off(0, 1)
         counts(0, *take(0, 0))
@@ -500,6 +516,11 @@
 
         pass_on(2, 1, "later")
         each(suffixes, 1)
+
+        @pl.when(more)
+        def early():
+            pass_on(0, 0, "earlier")
+
         each(unmix, 1)
 
         @pl.when(last)
@@ -533,10 +554,12 @@
     loads[1].wait()
     stores = []
     for z in range(ZS):
-        cols = jnp.concatenate([dy_ref[z], jnp.zeros((N - 16, N), F32)], 0).T
+        g = z // PER
+        cols = jnp.concatenate([dy_ref[g], jnp.zeros((N - SIZES[2], N), F32)], 0).T
         loads[2 + z].wait()
         for e in range(ELEMENTS):
-            c_ref[e, z] = c_ref[e, z] + dx_ref[z, e : e + 1] + cols[:, e : e + 1]
+            k = spot(z, e)
+            c_ref[e, z] = c_ref[e, z] + dx_ref[g, k : k + 1] + cols[:, k : k + 1]
         stores.append(pltpu.make_async_copy(c_ref.at[:, z], out_hbm.at[:, z], sems.at[2 + z]))
         stores[z].start()
     for store in stores:
@@ -571,8 +594,8 @@
             body,
             out_shape=[
                 jax.ShapeDtypeStruct(conc.shape, F32),
-                jax.ShapeDtypeStruct((ZS, 16, N), F32),
-                jax.ShapeDtypeStruct((ZS, 16, N), F32),
+                jax.ShapeDtypeStruct((GROUPS, SIZES[2], N), F32),
+                jax.ShapeDtypeStruct((GROUPS, SIZES[2], N), F32),
             ],
             in_specs=[anywhere] * (len(small) + 1),
             out_specs=[anywhere, vmem, vmem],
@@ -614,7 +637,7 @@
             out_specs=anywhere,
             scratch_shapes=[
                 pltpu.VMEM(conc.shape, F32),
-                *[pltpu.VMEM((ZS, 16, N), F32)] * 2,
+                *[pltpu.VMEM((GROUPS, SIZES[2], N), F32)] * 2,
                 pltpu.SemaphoreType.DMA((2 + ZS,)),
             ],
             compiler_params=pltpu.CompilerParams(vmem_limit_bytes=64 * 1024 * 1024),

time: 71.2 us -> 70.3 us (0.987)
  Pallas kernels: 70.8 us -> 69.8 us
    pallas_call x1, Pallas kernels: 67.6 us -> 66.6 us  [shards(): pl.pallas_call(body, out_shape=[jax.ShapeDtypeStruct(conc.shape, F32), ja...]
where the time goes in v12:
time: 70.3 us; the launch traced here: 70 us
  Pallas kernels  69.8 us (99%)
    pallas_call x1, Pallas kernels, shards(): pl.pallas_call(body, out_shape=[jax.ShapeDtypeStruct(conc.shape, F32), ja...  66.6 us
    pallas_call x1, Pallas kernels, shards(): pl.pallas_call(close, out_shape=jax.ShapeDtypeStruct(conc.shape, F32), in...  3.18 us

profile of v12, /device:TPU:0, one launch (start us, length us, event | category | flops | bytes accessed | tf_op | source)
XLA Modules:
  0.0 70.0 jit_solution(5056397840700028802)
XLA Ops:
  0.0 66.6 %shard_map.100 = (f32[10,4,128,128]{3,2,1,0:T(8,128)}, f32[2,24,128]{2,1,0:T(8,128)}, f32[2,24,128]{2,1,0:T(8,128)}) custom-call(s32[1,2]{1,0:T(1,128)} %bitcast.2, f32[2,10]{1,0:T(2,128)} %refs_1_.1, f32[12,10]{1,0:T(8,128)} %refs_2_.1, f32[12,10]{1,0:T(8,128)} %refs_3_.1, f32[1,10]{1,0:T(1,128)} %bitcast.3, f32[12,4,128]{2,1,0:T(4,128)} %refs_5_.1, ...), custom_call_target="tpu_custom_call" | custom-call | tf_op jit(solution)/shard_map/pallas_call | solution.py:593
  66.6 3.2 %shard_map.101 = f32[10,4,128,128]{3,2,1,0:T(8,128)} custom-call(f32[10,4,128,128]{3,2,1,0:T(8,128)} %get-tuple-element.8.c_hbm, f32[2,24,128]{2,1,0:T(8,128)} %get-tuple-element.9.dx_hbm, f32[2,24,128]{2,1,0:T(8,128)} %get-tuple-element.10.dy_hbm), custom_call_target="tpu_custom_call" | custom-call | tf_op jit(solution)/shard_map/pallas_call | solution.py:633

commit v13 on v12

--- a/solution.py
+++ b/solution.py
@@ -113,14 +113,17 @@
             self.copy(src, dst, phase, g, 0, peer).start()
         self.near[phase, g, pl.ds(self.slot, 1), rows] = self.send[phase, g, rows][None]
 
-    def wait(self, ref, phase, g, leg, count):
+    def whole(self, phase, g, leg):
+        ref, count = ((self.near, self.slots - 1), (self.far, AHEAD - 1))[leg]
         some = ref.at[phase, g, pl.ds(0, count), pl.ds(0, SIZES[phase])]
-        whole = self.copy(some, some, phase, g, leg, self.near_peers()[0])
-        whole.wait_send()
-        whole.wait_recv()
+        return self.copy(some, some, phase, g, leg, self.near_peers()[0])
+
+    def settle(self, phase, g):
+        self.whole(phase, g, 0).wait_send()
+        self.whole(phase, g, 1).wait_send()
 
     def middle(self, phase, g, mode):
-        self.wait(self.near, phase, g, 0, self.slots - 1)
+        self.whole(phase, g, 0).wait_recv()
         rows = pl.ds(0, SIZES[phase])
         have = [[self.near[phase, g, y * self.cores + c, rows] for c in range(self.cores)] for y in range(2)]
         sums = [sum(cores[1:], cores[0]) for cores in have]
@@ -149,7 +152,7 @@
         self.far[phase, g, pl.ds(self.x, 1), rows] = mine[None]
 
     def finish(self, phase, g):
-        self.wait(self.far, phase, g, 1, AHEAD - 1)
+        self.whole(phase, g, 1).wait_recv()
         far = [self.far[phase, g, x, pl.ds(0, SIZES[phase])] for x in range(AHEAD)]
         return (far[0] + far[1]) + (far[2] + far[3])
 
@@ -197,6 +200,10 @@
     def pass_on(phase, g, mode):
         det.middle(phase, g, mode)
         beam.middle(phase, g, mode)
+
+    def settle(phase, g):
+        det.settle(phase, g)
+        beam.settle(phase, g)
 
     def take(phase, g):
         across = det.finish(phase, g)
@@ -490,11 +497,13 @@
         send_off(1, 1)
         residuals(0, *take(1, 0))
         send_off(2, 0)
+        settle(0, 0)
         pass_on(1, 1, "sum")
         each(suffixes, 0)
         pass_on(2, 0, "later")
         residuals(1, *take(1, 1))
         send_off(2, 1)
+        settle(0, 1)
         each(unmix, 0)
 
         @pl.when(last)
@@ -503,6 +512,7 @@
                 store(z).start()
 
         after = take(2, 0)
+        settle(1, 0)
 
         @pl.when(more)
         def again():
@@ -533,6 +543,10 @@
         @pl.when(more)
         def once_more():
             renew(1, *rest)
+
+        settle(1, 1)
+        settle(2, 0)
+        settle(2, 1)
 
         @pl.when(last)
         def finish():

time: 70.3 us -> 70.3 us (level)
  no operation moved by 1% of the time
where the time goes in v13:
time: 70.3 us; the launch traced here: 70 us
  Pallas kernels  69.8 us (99%)
    pallas_call x1, Pallas kernels, shards(): pl.pallas_call(body, out_shape=[jax.ShapeDtypeStruct(conc.shape, F32), ja...  66.6 us
    pallas_call x1, Pallas kernels, shards(): pl.pallas_call(close, out_shape=jax.ShapeDtypeStruct(conc.shape, F32), in...  3.18 us

profile of v13, /device:TPU:0, one launch (start us, length us, event | category | flops | bytes accessed | tf_op | source)
XLA Modules:
  0.0 70.0 jit_solution(8432730424812343222)
XLA Ops:
  0.0 66.6 %shard_map.100 = (f32[10,4,128,128]{3,2,1,0:T(8,128)}, f32[2,24,128]{2,1,0:T(8,128)}, f32[2,24,128]{2,1,0:T(8,128)}) custom-call(s32[1,2]{1,0:T(1,128)} %bitcast.2, f32[2,10]{1,0:T(2,128)} %refs_1_.1, f32[12,10]{1,0:T(8,128)} %refs_2_.1, f32[12,10]{1,0:T(8,128)} %refs_3_.1, f32[1,10]{1,0:T(1,128)} %bitcast.3, f32[12,4,128]{2,1,0:T(4,128)} %refs_5_.1, ...), custom_call_target="tpu_custom_call" | custom-call | tf_op jit(solution)/shard_map/pallas_call | solution.py:607
  66.6 3.2 %shard_map.101 = f32[10,4,128,128]{3,2,1,0:T(8,128)} custom-call(f32[10,4,128,128]{3,2,1,0:T(8,128)} %get-tuple-element.8.c_hbm, f32[2,24,128]{2,1,0:T(8,128)} %get-tuple-element.9.dx_hbm, f32[2,24,128]{2,1,0:T(8,128)} %get-tuple-element.10.dy_hbm), custom_call_target="tpu_custom_call" | custom-call | tf_op jit(solution)/shard_map/pallas_call | solution.py:647

commit v14 on v13

--- a/solution.py
+++ b/solution.py
@@ -178,7 +178,7 @@
     hbm = (axis_hbm, inc_hbm, sig_hbm, yld_hbm, rate_hbm, m1_hbm, live1_hbm, m2_hbm, live2_hbm)
     vmem = (axis_ref, inc_ref, sig_ref, yld_ref, rate_ref, m1_ref, live1_ref, m2_ref, live2_ref)
     loads = [pltpu.make_async_copy(a, b, load_sems.at[k]) for k, (a, b) in enumerate(zip(hbm, vmem))]
-    for load in [conc_load(z) for z in range(ZS)] + loads:
+    for load in loads + [conc_load(z) for z in range(ZS)]:
         load.start()
     beam = Ring("beam", beams, bsend, bnear, bout, bfar, bsems)
     det = Ring("det", dets, dsend, dnear, dout, dfar, dsems)
@@ -472,7 +472,7 @@
         each(mix, g)
         prefixes(g)
 
-    for z in range(ZS):
+    for z in members(0):
         conc_load(z).wait()
     opening(0)
     pl.semaphore_wait(barrier, greeted)
@@ -481,6 +481,12 @@
     def turn(step, carry):
         last = step == STEPS - 1
         more = jnp.logical_not(last)
+
+        @pl.when(step == 0)
+        def arrive():
+            for z in members(1):
+                conc_load(z).wait()
+
         each(mix, 1)
 
         @pl.when(step == 0)

time: 70.3 us -> 70.1 us (level)
  no operation moved by 1% of the time
where the time goes in v14:
time: 70.1 us; the launch traced here: 69.8 us
  Pallas kernels  69.6 us (99%)
    pallas_call x1, Pallas kernels, shards(): pl.pallas_call(body, out_shape=[jax.ShapeDtypeStruct(conc.shape, F32), ja...  66.4 us
    pallas_call x1, Pallas kernels, shards(): pl.pallas_call(close, out_shape=jax.ShapeDtypeStruct(conc.shape, F32), in...  3.18 us

profile of v14, /device:TPU:0, one launch (start us, length us, event | category | flops | bytes accessed | tf_op | source)
XLA Modules:
  0.0 69.8 jit_solution(17517914086623107385)
XLA Ops:
  0.0 66.4 %shard_map.100 = (f32[10,4,128,128]{3,2,1,0:T(8,128)}, f32[2,24,128]{2,1,0:T(8,128)}, f32[2,24,128]{2,1,0:T(8,128)}) custom-call(s32[1,2]{1,0:T(1,128)} %bitcast.2, f32[2,10]{1,0:T(2,128)} %refs_1_.1, f32[12,10]{1,0:T(8,128)} %refs_2_.1, f32[12,10]{1,0:T(8,128)} %refs_3_.1, f32[1,10]{1,0:T(1,128)} %bitcast.3, f32[12,4,128]{2,1,0:T(4,128)} %refs_5_.1, ...), custom_call_target="tpu_custom_call" | custom-call | tf_op jit(solution)/shard_map/pallas_call | solution.py:613
  66.5 3.2 %shard_map.101 = f32[10,4,128,128]{3,2,1,0:T(8,128)} custom-call(f32[10,4,128,128]{3,2,1,0:T(8,128)} %get-tuple-element.8.c_hbm, f32[2,24,128]{2,1,0:T(8,128)} %get-tuple-element.9.dx_hbm, f32[2,24,128]{2,1,0:T(8,128)} %get-tuple-element.10.dy_hbm), custom_call_target="tpu_custom_call" | custom-call | tf_op jit(solution)/shard_map/pallas_call | solution.py:653
